TPU v7x, 32 devices: a whole 2x2x4 slice. The times are simulated.
32 devices in a mesh: sec: 16 (over z, x, core), mpo: 2 (over y).
Axes of the slice: x: 2, y: 2, z: 4, core: 2. Of those that a mesh axis runs over, the one named last changes fastest.
Arguments:
- wavefunction: bfloat16 [1280, 128, 128], P('sec'), may hold values from -6 to 6
- left_sector: int32 [1280], P('sec'), may hold values from 0 to 159, as said below
- right_sector: int32 [1280], P('sec'), may hold values from 0 to 159, as said below
- term_mask: int32 [4, 160], P('mpo', 'sec'), may hold values 0 or 1
- left_operators: bfloat16 [4, 160, 128, 128], P('mpo', 'sec'), may hold values from -0.5 to 0.5
- right_operators: bfloat16 [4, 160, 128, 128], P('mpo', 'sec'), may hold values from -0.375 to 0.375
Outputs:
- applied: bfloat16 [1280, 128, 128], P('sec', 'mpo')
Inputs may be any that keep to these rules, and one draw needn't show every extreme that they name: `left_sector`: the blocks 80 * d to 80 * d + 79 have left sectors from 10 * d to 10 * d + 9. `right_sector`: among the blocks 80 * d to 80 * d + 79, at most 10 have right sectors in any one range 10 * e to 10 * e + 9; for one e, drawn from the seed, every d has exactly 10 there.
All inputs are finite; a program needn't handle non-finite values. No bound on the sum of `term_mask` on one device may be relied on, other than what follows from the above.
Results may differ from a plain program's by a relative error of at most 0.015.
Values may be sent and summed in bfloat16 or wider, within the bound.
No kernel may reach another device: no remote copies, remote signals or barrier semaphores. Data moves between devices by JAX's collectives and lax.ppermute only.
A program may use at most 128 MiB of HBM per device.

v0:
```python
import jax
import jax.numpy as jnp
from jax import lax
from jax.sharding import PartitionSpec as P


def on_device(wavefunction, left_sector, right_sector, term_mask, left_operators, right_operators):
    owners = lax.axis_size("sec")
    own_index = lax.axis_index("sec")
    sector_count = left_operators.shape[1]
    block_count = wavefunction.shape[0]
    block_width = wavefunction.shape[1]
    term_count = left_operators.shape[0]
    local_left = left_sector - own_index * sector_count
    chosen_left = jnp.take(left_operators, local_left, axis=1)
    weights = jnp.take(term_mask, local_left, axis=1).astype(jnp.float32)
    left_full = jnp.einsum(
        "kbij,bjc->bkic", chosen_left, wavefunction, preferred_element_type=jnp.float32
    )
    left_part = (left_full * jnp.transpose(weights)[:, :, None, None]).astype(jnp.bfloat16)
    target = right_sector // sector_count
    same_target = target[:, None] == target[None, :]
    earlier = jnp.arange(block_count)[None, :] < jnp.arange(block_count)[:, None]
    ordinal = jnp.sum(jnp.logical_and(same_target, earlier), axis=1)
    slot_index = target * sector_count + ordinal
    slot_count = owners * sector_count
    outgoing = (
        jnp.zeros((slot_count, term_count, block_width, block_width), jnp.bfloat16)
        .at[slot_index]
        .set(left_part)
    )
    labels = (
        jnp.zeros((slot_count,), jnp.int32).at[slot_index].set(right_sector - target * sector_count)
    )
    received = lax.all_to_all(
        outgoing.reshape(owners, sector_count, term_count, block_width, block_width),
        "sec",
        split_axis=0,
        concat_axis=0,
        tiled=True,
    )
    sectors = lax.all_to_all(
        labels.reshape(owners, sector_count), "sec", split_axis=0, concat_axis=0, tiled=True
    )
    item_count = received.shape[0] * received.shape[1]
    flattened = received.reshape(item_count, term_count, block_width, block_width)
    sector_ids = sectors.reshape(item_count)
    running = jnp.zeros((item_count, block_width, block_width), jnp.float32)
    for number in range(term_count):
        chosen_right = jnp.take(right_operators[number], sector_ids, axis=0)
        running = running + jnp.einsum(
            "bij,bcj->bic", flattened[:, number], chosen_right, preferred_element_type=jnp.float32
        )
    returned = running.astype(jnp.bfloat16).reshape(
        received.shape[0], received.shape[1], block_width, block_width
    )
    arrived = lax.all_to_all(returned, "sec", split_axis=0, concat_axis=0, tiled=True)
    partial_value = arrived.reshape(slot_count, block_width, block_width)[slot_index]
    summed = lax.psum_scatter(
        partial_value.astype(jnp.float32).astype(jnp.bfloat16),
        "mpo",
        scatter_dimension=1,
        tiled=True,
    )
    return summed


def solution(mesh):
    placed = (
        P("sec", None, None),
        P("sec"),
        P("sec"),
        P("mpo", "sec"),
        P("mpo", "sec", None, None),
        P("mpo", "sec", None, None),
    )
    return jax.shard_map(
        on_device, mesh=mesh, in_specs=placed, out_specs=P("sec", "mpo", None), check_vma=False
    )
```

profile of v0, /device:TPU:0, one launch (start us, length us, event | category | flops | bytes accessed | tf_op | source)
XLA Modules:
  0.0 506.8 jit_solution(947796018629721381)
XLA Ops:
  6.5 0.0 copy-start
  6.5 0.8 multiply_subtract_fusion
  7.4 0.2 convert_reduce_fusion
  7.5 0.8 scatter_custom_fusion.1
  8.4 0.7 all_to_all.13
  9.1 7.4 %all-to-all-start.1 = ((s32[16,1,10]{2,1,0:T(1,128)}), s32[16,1,10]{2,1,0:T(1,128)S(1)}, u32[]{:S(2)}, u32[]{:S(2)}) async-start(s32[16,1,10]{2,1,0:T(1,128)} %bitcast.6), calls=%async_computation.1 | async-start | bytes 16384 | tf_op jit(solution)/shard_map/all_to_all | solution.py:42
  16.4 0.7 compare_and_fusion.1
  17.1 0.8 copy.14
  17.9 0.6 gather_fusion.1
  18.5 6.8 %gather_fusion = bf16[80,2,128,128]{3,2,1,0:T(8,128)(2,1)} fusion(bf16[2,10,128,128]{3,2,1,0:T(8,128)(2,1)} %param.12, s32[1024]{0:T(1024)S(1)} %pad_clamp_fusion.2), kind=kCustom, calls=%fused_computation.2 | custom fusion | bytes 10486080 | tf_op jit(solution)/shard_map/jit(_take)/gather | solution.py:15
  25.2 0.1 select_convert_fusion
  25.3 0.0 copy-done
  25.3 6.4 %multiply_convert_fusion = bf16[80,2,128,128]{3,2,1,0:T(8,128)(2,1)} fusion(f32[80,2]{1,0:T(8,128)S(1)} %select_convert_fusion, bf16[80,2,128,128]{3,2,1,0:T(8,128)(2,1)} %gather_fusion, pred[80]{0:T(512)(128)(4,1)S(1)} %get-tuple-element.8, bf16[80,128,128]{2,1,0:T(8,128)(2,1)S(1)} %copy-done), kind=kOutput, calls=%fused_computation.8 | convolution fusion | flops 678952960 | bytes 13107920 | tf_op jit(solution)/shard_map/kbij,bjc->bkic/dot_general | solution.py:17
  31.7 6.5 %broadcast_in_dim.47 = bf16[160,2,128,128]{3,2,1,0:T(8,128)(2,1)} broadcast(bf16[]{:T(256)} %constant.34.clone.1), dimensions={} | broadcast | bytes 10485762 | tf_op jit(solution)/shard_map/broadcast_in_dim | solution.py:28
  38.2 14.9 %scatter_fusion = bf16[160,2,128,128]{3,2,1,0:T(8,128)(2,1)} fusion(bf16[160,2,128,128]{3,2,1,0:T(8,128)(2,1)} %broadcast_in_dim.47, s32[80]{0:T(128)S(1)} %compare_select_fusion.2, bf16[80,2,128,128]{3,2,1,0:T(8,128)(2,1)} %multiply_convert_fusion), kind=kCustom, calls=%fused_computation.5 | custom fusion | bytes 15728960 | tf_op jit(solution)/shard_map/scatter | solution.py:30
  53.1 12.8 %copy.15 = bf16[16,10,2,128,128]{4,3,1,2,0:T(8,128)(2,1)} copy(bf16[16,10,2,128,128]{4,3,2,1,0:T(8,128)(2,1)} %bitcast.27) | data formatting | bytes 20971520 | tf_op jit(solution)/shard_map/reshape | solution.py:36
  65.9 0.0 copy-start.2
  65.9 0.0 all-to-all-done.1
  65.9 6.1 %all-to-all-start = ((bf16[16,10,2,128,128]{4,3,1,2,0:T(8,128)(2,1)}), bf16[16,10,2,128,128]{4,3,1,2,0:T(8,128)(2,1)}, u32[]{:S(2)}, u32[]{:S(2)}) async-start(bf16[16,10,2,128,128]{4,3,1,2,0:T(8,128)(2,1)} %copy.15), calls=%async_computation | async-start | bytes 20971520 | tf_op jit(solution)/shard_map/all_to_all | solution.py:35
  72.0 0.0 copy-done.2
  72.0 0.1 slice_bitcast_fusion.7
  72.1 0.5 broadcast.59
  72.6 0.7 reduce.3
  73.3 0.1 reshape.35
  73.4 7.7 %gather_fusion.4 = bf16[160,128,128]{2,1,0:T(8,128)(2,1)} fusion(bf16[10,128,128]{2,1,0:T(8,128)(2,1)S(1)} %get-tuple-element.11, s32[1024]{0:T(1024)S(1)} %pad_clamp_fusion.1), kind=kCustom, calls=%fused_computation.1.clone | custom fusion | bytes 10486400 | tf_op jit(solution)/shard_map/jit(_take)/gather | solution.py:50
  81.1 7.7 %gather_fusion.3 = bf16[160,128,128]{2,1,0:T(8,128)(2,1)} fusion(bf16[10,128,128]{2,1,0:T(8,128)(2,1)S(1)} %get-tuple-element.10, s32[1024]{0:T(1024)S(1)} %pad_clamp_fusion.1), kind=kCustom, calls=%fused_computation.clone | custom fusion | bytes 10486400 | tf_op jit(solution)/shard_map/jit(_take)/gather | solution.py:50
  88.8 170.4 %all-to-all-done = bf16[16,10,2,128,128]{4,3,1,2,0:T(8,128)(2,1)} async-done(((bf16[16,10,2,128,128]{4,3,1,2,0:T(8,128)(2,1)}), bf16[16,10,2,128,128]{4,3,1,2,0:T(8,128)(2,1)}, u32[]{:S(2)}, u32[]{:S(2)}) %all-to-all-start) | async-done | bytes 10485792 | tf_op jit(solution)/shard_map/all_to_all | solution.py:35
  259.2 12.8 %copy.16 = bf16[16,10,2,128,128]{4,3,1,0,2:T(8,128)(2,1)} copy(bf16[16,10,2,128,128]{4,3,1,2,0:T(8,128)(2,1)} %all-to-all-done) | data formatting | bytes 20971520 | tf_op jit(solution)/shard_map/all_to_all | solution.py:35
  272.0 11.7 %fusion = f32[160,128,128]{2,1,0:T(8,128)} fusion(bf16[160,2,128,128]{3,2,0,1:T(8,128)(2,1)} %bitcast.28, bf16[160,128,128]{2,1,0:T(8,128)(2,1)} %gather_fusion.4, pred[160]{0:T(512)(128)(4,1)S(1)} %compare_and_fusion), kind=kOutput, calls=%fused_computation.10 | convolution fusion | flops 673710080 | bytes 20971680 | tf_op jit(solution)/shard_map/bij,bcj->bic/dot_general | solution.py:51
  283.7 13.3 %add_convert_fusion = bf16[160,128,128]{2,1,0:T(8,128)(2,1)} fusion(f32[160,128,128]{2,1,0:T(8,128)} %fusion, bf16[160,128,128]{2,1,0:T(8,128)(2,1)} %gather_fusion.3, pred[160]{0:T(512)(128)(4,1)S(1)} %compare_and_fusion, bf16[160,2,128,128]{3,2,0,1:T(8,128)(2,1)} %bitcast.29), kind=kOutput, calls=%fused_computation.7 | convolution fusion | flops 678952960 | bytes 26214560 | tf_op jit(solution)/shard_map/bij,bcj->bic/dot_general | solution.py:51
  297.0 45.0 %all-to-all-start.2 = ((bf16[16,10,128,128]{3,2,1,0:T(8,128)(2,1)}), bf16[16,10,128,128]{3,2,1,0:T(8,128)(2,1)}, u32[]{:S(2)}, u32[]{:S(2)}) async-start(bf16[16,10,128,128]{3,2,1,0:T(8,128)(2,1)} %bitcast.30), calls=%async_computation.2 | async-start | bytes 10485760 | tf_op jit(solution)/shard_map/all_to_all | solution.py:57
  342.0 0.0 copy-start.1
  342.0 0.0 reduce-scatter.2.cloned.1.call-start
  342.1 95.9 %all-to-all-done.2 = bf16[16,10,128,128]{3,2,1,0:T(8,128)(2,1)} async-done(((bf16[16,10,128,128]{3,2,1,0:T(8,128)(2,1)}), bf16[16,10,128,128]{3,2,1,0:T(8,128)(2,1)}, u32[]{:S(2)}, u32[]{:S(2)}) %all-to-all-start.2) | async-done | bytes 5242912 | tf_op jit(solution)/shard_map/all_to_all | solution.py:57
  437.9 5.0 gather_fusion.2
  442.9 0.0 reduce-scatter.2.cloned.1.call-update
  443.0 56.9 %reduce-scatter.2.cloned.1.call-done = bf16[80,64,128]{2,1,0:T(8,128)(2,1)} async-done(((bf16[80,128,128]{2,1,0:T(8,128)(2,1)}), bf16[80,64,128]{2,1,0:T(8,128)(2,1)}) %reduce-scatter.2.cloned.1.call-update) | async-done | bytes 1310736 | tf_op jit(solution)/shard_map/reduce_scatter | solution.py:59
  499.9 0.0 copy-done.1
  (6 shorter events, 0.0 us)
Async XLA Ops:
  6.5 18.8 %copy-start = (bf16[80,128,128]{2,1,0:T(8,128)(2,1)S(1)}, bf16[80,128,128]{2,1,0:T(8,128)(2,1)}, u32[]{:S(2)}) copy-start(bf16[80,128,128]{2,1,0:T(8,128)(2,1)} %param.8) | copy-start | bytes 7864324
  9.1 56.8 %all-to-all-start.1 = ((s32[16,1,10]{2,1,0:T(1,128)}), s32[16,1,10]{2,1,0:T(1,128)S(1)}, u32[]{:S(2)}, u32[]{:S(2)}) async-start(s32[16,1,10]{2,1,0:T(1,128)} %bitcast.6), calls=%async_computation.1 | async-start | bytes 16384 | tf_op jit(solution)/shard_map/all_to_all | solution.py:42
  65.9 6.1 %copy-start.2 = (bf16[2,10,128,128]{3,2,1,0:T(8,128)(2,1)S(1)}, bf16[2,10,128,128]{3,2,1,0:T(8,128)(2,1)}, u32[]{:S(2)}) copy-start(bf16[2,10,128,128]{3,2,1,0:T(8,128)(2,1)} %param.13) | copy-start | bytes 1966084
  65.9 193.3 %all-to-all-start = ((bf16[16,10,2,128,128]{4,3,1,2,0:T(8,128)(2,1)}), bf16[16,10,2,128,128]{4,3,1,2,0:T(8,128)(2,1)}, u32[]{:S(2)}, u32[]{:S(2)}) async-start(bf16[16,10,2,128,128]{4,3,1,2,0:T(8,128)(2,1)} %copy.15), calls=%async_computation | async-start | bytes 20971520 | tf_op jit(solution)/shard_map/all_to_all | solution.py:35
  297.0 140.9 %all-to-all-start.2 = ((bf16[16,10,128,128]{3,2,1,0:T(8,128)(2,1)}), bf16[16,10,128,128]{3,2,1,0:T(8,128)(2,1)}, u32[]{:S(2)}, u32[]{:S(2)}) async-start(bf16[16,10,128,128]{3,2,1,0:T(8,128)(2,1)} %bitcast.30), calls=%async_computation.2 | async-start | bytes 10485760 | tf_op jit(solution)/shard_map/all_to_all | solution.py:57
  342.0 157.9 %copy-start.1 = (bf16[80,128,128]{2,1,0:T(8,128)(2,1)S(1)}, bf16[80,128,128]{2,1,0:T(8,128)(2,1)}, u32[]{:S(2)}) copy-start(bf16[80,128,128]{2,1,0:T(8,128)(2,1)} %param.8) | copy-start | bytes 7864324
  342.0 157.9 %reduce-scatter.2.cloned.1.call-start = ((), (), s32[]{:S(2)}) async-start(), calls=%async_computation.4 | async-start | bytes 3932160 | tf_op jit(solution)/shard_map/reduce_scatter | solution.py:59
Sparse Core Ops, SparseCore 0:
  443.1 56.7 reduce-scatter.1
where the time goes:
time: 507 us
  waiting for transfers between devices  323 us (64%)
  local copies, waits for them, and re-layouts  77.7 us (15%)
  starting transfers between devices  58.5 us (12%)
  matrix products  31.3 us (6%)
  between operations  13.5 us (3%)
    all_to_all x1, waiting for transfers between devices, on_device(): lax.all_to_all(outgoing.reshape(owners, sector_count, term_count, block_w...  170 us
    all_to_all x1, waiting for transfers between devices, on_device(): lax.all_to_all(returned, 'sec', split_axis=0, concat_axis=0, tiled=True)  95.9 us
    reduce_scatter x1, waiting for transfers between devices, on_device(): lax.psum_scatter(partial_value.astype(jnp.float32).astype(jnp.bfloat16),...  56.9 us
    all_to_all x1, starting transfers between devices, on_device(): lax.all_to_all(returned, 'sec', split_axis=0, concat_axis=0, tiled=True)  45 us
    dot_general x2, matrix products, on_device(): jnp.einsum('bij,bcj->bic', flattened[:, number], chosen_right, preferred_...  25 us
    gather x2, local copies, waits for them, and re-layouts, on_device(): chosen_right = jnp.take(right_operators[number], sector_ids, axis=0)  15.4 us
    scatter x1, local copies, waits for them, and re-layouts, on_device(): outgoing = jnp.zeros((slot_count, term_count, block_width, block_width),...  14.9 us
    all_to_all x1, local copies, waits for them, and re-layouts, on_device(): lax.all_to_all(outgoing.reshape(owners, sector_count, term_count, block_w...  12.8 us
  transfers between devices with their start and end apart: 4, of which 3 were waited for; matrix products, arithmetic and copies ran while one was open for 13% of the time, Pallas kernels for 0%

commit v1 on v0

v1 whole, which is shorter than its diff:
```python
import functools

import jax
import jax.numpy as jnp
import numpy as np
from jax import lax
from jax.experimental import pallas as pl
from jax.experimental.pallas import tpu as pltpu
from jax.sharding import PartitionSpec as P

WIDTHS = (64, 64)
RING_LIMIT = 16
VMEM_LIMIT = 48 * 1024 * 1024


def chip_ring(chips):
    across = 2 if chips % 2 == 0 else 1
    up = [z * across for z in range(chips // across)]
    down = [z * across + 1 for z in reversed(range(chips // across))] if across == 2 else []
    return up + down


def ring_gather(part, forward_steps, chips):
    order = chip_ring(chips)
    after = {order[i]: order[(i + 1) % chips] for i in range(chips)}
    before = {order[i]: order[i - 1] for i in range(chips)}
    devices = range(2 * chips)
    forward = [(d, 2 * after[d // 2] + d % 2) for d in devices]
    backward = [(d, 2 * before[d // 2] + d % 2) for d in devices]
    swap = [(d, d ^ 1) for d in devices]
    ahead, behind, pieces, shifts = part, part, [part], [0]
    for step in range(1, chips):
        if step <= forward_steps:
            ahead = lax.ppermute(ahead, "sec", forward)
            pieces.append(ahead)
            shifts.append(-step)
        if step < chips - forward_steps:
            behind = lax.ppermute(behind, "sec", backward)
            pieces.append(behind)
            shifts.append(step)
    pieces = pieces + [lax.ppermute(piece, "sec", swap) for piece in pieces]
    place = {chip: i for i, chip in enumerate(order)}
    owners = np.zeros((2 * chips, len(pieces)), np.int32)
    for d in devices:
        for number, shift in enumerate(shifts):
            chip = order[(place[d // 2] + shift) % chips]
            owners[d, number] = 2 * chip + d % 2
            owners[d, number + len(shifts)] = 2 * chip + 1 - d % 2
    return pieces, owners


def left_kernel(here_ref, sector_ref, mask_ref, operator_ref, wave_ref, out_ref, *, parties):
    terms, sectors, width, _ = operator_ref.shape
    blocks = wave_ref.shape[0]
    rows = width // parties
    own, first = here_ref[0], here_ref[1] * sectors

    def one_block(b, carry):
        local = sector_ref[b] - first
        bands = [
            operator_ref[k, local, pl.ds(pl.multiple_of(lax.rem(own + j, parties) * rows, rows), rows), :]
            for k in range(terms)
            for j in range(parties)
        ]
        product = jnp.dot(
            jnp.concatenate(bands, axis=0), wave_ref[b], preferred_element_type=jnp.float32
        )
        for k in range(terms):
            weight = mask_ref[k, local].astype(jnp.float32)
            out_ref[b, :, k * width : (k + 1) * width] = (
                product[k * width : (k + 1) * width] * weight
            ).astype(out_ref.dtype)
        return carry

    lax.fori_loop(0, blocks, one_block, 0, unroll=8)


def right_kernel(owner_ref, sector_ref, left_ref, *refs, pieces, parties):
    piece_refs, out_refs = refs[:pieces], refs[pieces : pieces + parties]
    held, arrived = refs[pieces + parties :]
    terms, _, columns, width = held.shape
    sectors = piece_refs[0].shape[1]
    blocks, rows = left_ref.shape[0], left_ref.shape[1] // parties
    pack = width // columns
    copies = [
        pltpu.make_async_copy(
            piece, held.at[:, pl.ds(owner_ref[number] * sectors, sectors)], arrived.at[number]
        )
        for number, piece in enumerate(piece_refs)
    ]
    for copy in copies:
        copy.start()
    for copy in copies:
        copy.wait()
    lane = lax.broadcasted_iota(jnp.int32, (left_ref.shape[1], width), 1) // columns

    def one_group(g, carry):
        factors = []
        for q in range(pack):
            sector = sector_ref[g * pack + q]
            factors.append(jnp.concatenate([held[k, sector] for k in range(terms)], axis=1))
        factor = jnp.concatenate(factors, axis=0)
        lefts = jnp.concatenate([left_ref[g * pack + q] for q in range(pack)], axis=0)
        product = lax.dot_general(
            lefts, factor, (((1,), (1,)), ((), ())), preferred_element_type=jnp.float32
        ).reshape(pack, left_ref.shape[1], width)
        chosen = product[0]
        for q in range(1, pack):
            chosen = jnp.where(lane == q, product[q], chosen)
        for j in range(parties):
            out_refs[j][g] = chosen[j * rows : (j + 1) * rows].astype(out_refs[j].dtype)
        return carry

    lax.fori_loop(0, blocks // pack, one_group, 0, unroll=4)


def join_kernel(*refs, widths, parties):
    out_ref = refs[-1]
    blocks, rows, width = out_ref.shape
    parts = [refs[c * parties : (c + 1) * parties] for c in range(len(widths))]
    most = max(width // columns for columns in widths)
    lane = lax.broadcasted_iota(jnp.int32, (rows, width), 1)

    def one_group(g, carry):
        sums = []
        for columns, given in zip(widths, parts):
            pack = width // columns
            inside = []
            for t in range(most // pack):
                total = given[0][g * (most // pack) + t].astype(jnp.float32)
                for other in given[1:]:
                    total = total + other[g * (most // pack) + t].astype(jnp.float32)
                inside.append(total)
            sums.append(inside)
        for b in range(most):
            start, value = 0, None
            for columns, inside in zip(widths, sums):
                pack = width // columns
                source, q = inside[b // pack], b % pack
                turn = (start - q * columns) % width
                moved = pltpu.roll(source, turn, 1) if turn else source
                value = moved if value is None else jnp.where(lane >= start, moved, value)
                start += columns
            out_ref[g * most + b] = value.astype(out_ref.dtype)
        return carry

    lax.fori_loop(0, blocks // most, one_group, 0, unroll=4)


def on_device(wavefunction, left_sector, right_sector, term_mask, left_operators, right_operators):
    owners, parties = lax.axis_size("sec"), lax.axis_size("mpo")
    me, own = lax.axis_index("sec"), lax.axis_index("mpo")
    terms, sectors, width, _ = left_operators.shape
    blocks = wavefunction.shape[0]
    rows = width // parties
    smem = pl.BlockSpec(memory_space=pltpu.SMEM)
    vmem = pl.BlockSpec(memory_space=pltpu.VMEM)
    anywhere = pl.BlockSpec(memory_space=pl.ANY)
    params = pltpu.CompilerParams(vmem_limit_bytes=VMEM_LIMIT)

    left_part = pl.pallas_call(
        functools.partial(left_kernel, parties=parties),
        out_shape=jax.ShapeDtypeStruct((blocks, width, terms * width), jnp.bfloat16),
        in_specs=[smem, smem, smem, vmem, vmem],
        out_specs=vmem,
        compiler_params=params,
        cost_estimate=pl.CostEstimate(
            flops=2 * blocks * terms * width**3, bytes_accessed=9 * 2**20, transcendentals=0
        ),
        name="left_products",
    )(
        jnp.stack([own, me]).astype(jnp.int32),
        left_sector,
        term_mask,
        left_operators,
        wavefunction,
    )

    kept = []
    start = 0
    for number, columns in enumerate(WIDTHS):
        part = right_operators[:, :, start : start + columns, :]
        start += columns
        if owners <= RING_LIMIT and owners % 2 == 0:
            chips = owners // 2
            forward_steps = chips // 2 - number % 2
            pieces, table = ring_gather(part, forward_steps, chips)
        else:
            whole = lax.all_gather(part, "sec", axis=1, tiled=True)
            pieces, table = [whole], np.zeros((owners, 1), np.int32)
        pack = width // columns
        groups = blocks // pack
        partial = pl.pallas_call(
            functools.partial(right_kernel, pieces=len(pieces), parties=parties),
            out_shape=[jax.ShapeDtypeStruct((groups, rows, width), jnp.bfloat16)] * parties,
            in_specs=[smem, smem, vmem] + [anywhere] * len(pieces),
            out_specs=[vmem] * parties,
            scratch_shapes=[
                pltpu.VMEM((terms, owners * sectors, columns, width), jnp.bfloat16),
                pltpu.SemaphoreType.DMA((len(pieces),)),
            ],
            compiler_params=params,
            cost_estimate=pl.CostEstimate(
                flops=2 * blocks * terms * width**2 * columns,
                bytes_accessed=12 * 2**20,
                transcendentals=0,
            ),
            name="right_products",
        )(jnp.asarray(table)[me], right_sector, left_part, *pieces)
        kept.append(partial[0])
        for j in range(1, parties):
            turn = [(d, (d + j) % parties) for d in range(parties)]
            kept.append(lax.ppermute(partial[j], "mpo", turn))

    return pl.pallas_call(
        functools.partial(join_kernel, widths=WIDTHS, parties=parties),
        out_shape=jax.ShapeDtypeStruct((blocks, rows, width), jnp.bfloat16),
        in_specs=[vmem] * len(kept),
        out_specs=vmem,
        compiler_params=params,
        cost_estimate=pl.CostEstimate(flops=0, bytes_accessed=4 * 2**20, transcendentals=0),
        name="join_columns",
    )(*kept)


def solution(mesh):
    placed = (
        P("sec", None, None),
        P("sec"),
        P("sec"),
        P("mpo", "sec"),
        P("mpo", "sec", None, None),
        P("mpo", "sec", None, None),
    )
    return jax.shard_map(
        on_device, mesh=mesh, in_specs=placed, out_specs=P("sec", "mpo", None), check_vma=False
    )
```

time: 507 us -> 114 us (0.22)
  waiting for transfers between devices: 323 us -> 49.9 us
  local copies, waits for them, and re-layouts: 77.7 us -> 16.3 us
  starting transfers between devices: 58.5 us -> 23.1 us
  matrix products: 31.3 us -> 0 us
  Pallas kernels: 0 us -> 24.2 us
  between operations: 13.5 us -> 0.29 us
    all_to_all x3 -> x0, waiting for transfers between devices: 266 us -> none  [the longest x1 170 us: on_device(): lax.all_to_all(outgoing.reshape(owners, sector_count, term_count, block_w...]
    all_to_all x3 -> x0, starting transfers between devices: 58.5 us -> none  [the longest x1 45 us: on_device(): lax.all_to_all(returned, 'sec', split_axis=0, concat_axis=0, tiled=True)]
    reduce_scatter x1 -> x0, waiting for transfers between devices: 56.9 us -> none  [on_device(): lax.psum_scatter(partial_value.astype(jnp.float32).astype(jnp.bfloat16),...]
    ppermute x0 -> x32, waiting for transfers between devices: none -> 49.9 us  [the longest x2 20.7 us: on_device(): kept.append(lax.ppermute(partial[j], 'mpo', turn))]
    dot_general x3 -> x0, matrix products: 31.3 us -> none  [the longest x2 25 us: on_device(): jnp.einsum('bij,bcj->bic', flattened[:, number], chosen_right, preferred_...]
    gather x5 -> x0, local copies, waits for them, and re-layouts: 27.8 us -> none  [the longest x2 15.4 us: on_device(): chosen_right = jnp.take(right_operators[number], sector_ids, axis=0)]
    pallas_call x0 -> x4, Pallas kernels: none -> 24.2 us  [the longest x2 16.3 us: on_device(): pl.pallas_call(functools.partial(right_kernel, pieces=len(pieces), partie...]
    ppermute x0 -> x32, starting transfers between devices: none -> 23.1 us  [the longest x7 10.9 us: ring_gather(): behind = lax.ppermute(behind, 'sec', backward)]
  transfers between devices with their start and end apart: 4 -> 32, of which waited for: 3 -> 13; matrix products, arithmetic and copies ran while one was open for 13% -> 1% of each run, Pallas kernels for 0% -> 19%
where the time goes in v1:
time: 114 us
  waiting for transfers between devices  49.9 us (44%)
  Pallas kernels  24.2 us (21%)
  starting transfers between devices  23.1 us (20%)
  local copies, waits for them, and re-layouts  16.3 us (14%)
    ppermute x2, waiting for transfers between devices, on_device(): kept.append(lax.ppermute(partial[j], 'mpo', turn))  20.7 us
    ppermute x7, waiting for transfers between devices, ring_gather(): behind = lax.ppermute(behind, 'sec', backward)  17.6 us
    pallas_call x2, Pallas kernels, on_device(): pl.pallas_call(functools.partial(right_kernel, pieces=len(pieces), partie...  16.3 us
    unnamed x66, local copies, waits for them, and re-layouts  14.5 us
    ppermute x7, waiting for transfers between devices, ring_gather(): ahead = lax.ppermute(ahead, 'sec', forward)  11.6 us
    ppermute x7, starting transfers between devices, ring_gather(): behind = lax.ppermute(behind, 'sec', backward)  10.9 us
    ppermute x7, starting transfers between devices, ring_gather(): ahead = lax.ppermute(ahead, 'sec', forward)  6.95 us
    pallas_call x1, Pallas kernels, on_device(): pl.pallas_call(functools.partial(left_kernel, parties=parties), out_shape...  5.76 us
  transfers between devices with their start and end apart: 32, of which 13 were waited for; matrix products, arithmetic and copies ran while one was open for 1% of the time, Pallas kernels for 19%

profile of v1, /device:TPU:0, one launch (start us, length us, event | category | flops | bytes accessed | tf_op | source)
XLA Modules:
  0.0 113.8 jit_solution(4701240067520687035)
XLA Ops:
  0.0 1.1 fusion
  1.1 3.0 %collective-permute-start.17 = (bf16[2,10,64,128]{3,2,1,0:T(8,128)(2,1)S(1)}, bf16[2,10,64,128]{3,2,1,0:T(8,128)(2,1)S(1)}, u32[]{:S(2)}, u32[]{:S(2)}) collective-permute-start(bf16[2,10,64,128]{3,2,1,0:T(8,128)(2,1)S(1)} %get-tuple-element.13.refs_0_), channel_id=1, source_target_pairs={{0,4},{2,6},{4,12},{6,14},{8,0},{10,2},{12,20},{14,22},{16,8},{18,... | collective-permute-start | bytes 983048 | tf_op jit(solution)/shard_map/ppermute | solution.py:38
  4.3 2.0 %collective-permute-start = (bf16[2,10,64,128]{3,2,1,0:T(8,128)(2,1)S(1)}, bf16[2,10,64,128]{3,2,1,0:T(8,128)(2,1)S(1)}, u32[]{:S(2)}, u32[]{:S(2)}) collective-permute-start(bf16[2,10,64,128]{3,2,1,0:T(8,128)(2,1)S(1)} %get-tuple-element.14.refs_0_), channel_id=1, source_target_pairs={{0,8},{2,10},{4,0},{6,2},{8,16},{10,18},{12,4},{14,6},{16,24},{18,... | collective-permute-start | bytes 983048 | tf_op jit(solution)/shard_map/ppermute | solution.py:34
  6.3 6.4 %collective-permute-done.17.refs_2_ = bf16[2,10,64,128]{3,2,1,0:T(8,128)(2,1)S(1)} collective-permute-done((bf16[2,10,64,128]{3,2,1,0:T(8,128)(2,1)S(1)}, bf16[2,10,64,128]{3,2,1,0:T(8,128)(2,1)S(1)}, u32[]{:S(2)}, u32[]{:S(2)}) %collective-permute-start.17) | collective-permute-done | bytes 327712 | tf_op jit(solution)/shard_map/ppermute | solution.py:38
  12.7 2.0 %collective-permute-done.16.refs_1_ = bf16[2,10,64,128]{3,2,1,0:T(8,128)(2,1)S(1)} collective-permute-done((bf16[2,10,64,128]{3,2,1,0:T(8,128)(2,1)S(1)}, bf16[2,10,64,128]{3,2,1,0:T(8,128)(2,1)S(1)}, u32[]{:S(2)}, u32[]{:S(2)}) %collective-permute-start.16) | collective-permute-done | bytes 327712 | tf_op jit(solution)/shard_map/ppermute | solution.py:34
  14.8 1.6 %collective-permute-start.19 = (bf16[2,10,64,128]{3,2,1,0:T(8,128)(2,1)S(1)}, bf16[2,10,64,128]{3,2,1,0:T(8,128)(2,1)S(1)}, u32[]{:S(2)}, u32[]{:S(2)}) collective-permute-start(bf16[2,10,64,128]{3,2,1,0:T(8,128)(2,1)S(1)} %collective-permute-done.17.refs_2_), channel_id=1, source_target_pairs={{0,4},{2,6},{4,12},{6,14},{8,0},{10,2},{12,20},{14,22},{16,8},{18,... | collective-permute-start | bytes 983048 | tf_op jit(solution)/shard_map/ppermute | solution.py:38
  16.8 5.0 %collective-permute-done.refs_1_ = bf16[2,10,64,128]{3,2,1,0:T(8,128)(2,1)S(1)} collective-permute-done((bf16[2,10,64,128]{3,2,1,0:T(8,128)(2,1)S(1)}, bf16[2,10,64,128]{3,2,1,0:T(8,128)(2,1)S(1)}, u32[]{:S(2)}, u32[]{:S(2)}) %collective-permute-start) | collective-permute-done | bytes 327712 | tf_op jit(solution)/shard_map/ppermute | solution.py:34
  21.8 0.5 collective-permute-start.25
  22.4 3.6 %collective-permute-done.19.refs_4_ = bf16[2,10,64,128]{3,2,1,0:T(8,128)(2,1)S(1)} collective-permute-done((bf16[2,10,64,128]{3,2,1,0:T(8,128)(2,1)S(1)}, bf16[2,10,64,128]{3,2,1,0:T(8,128)(2,1)S(1)}, u32[]{:S(2)}, u32[]{:S(2)}) %collective-permute-start.19) | collective-permute-done | bytes 327712 | tf_op jit(solution)/shard_map/ppermute | solution.py:38
  26.0 1.7 %collective-permute-start.3 = (bf16[2,10,64,128]{3,2,1,0:T(8,128)(2,1)S(1)}, bf16[2,10,64,128]{3,2,1,0:T(8,128)(2,1)S(1)}, u32[]{:S(2)}, u32[]{:S(2)}) collective-permute-start(bf16[2,10,64,128]{3,2,1,0:T(8,128)(2,1)S(1)} %collective-permute-done.1.refs_2_), channel_id=1, source_target_pairs={{0,4},{2,6},{4,12},{6,14},{8,0},{10,2},{12,20},{14,22},{16,8},{18,... | collective-permute-start | bytes 983048 | tf_op jit(solution)/shard_map/ppermute | solution.py:38
  27.6 1.2 %collective-permute-done.18.refs_3_ = bf16[2,10,64,128]{3,2,1,0:T(8,128)(2,1)S(1)} collective-permute-done((bf16[2,10,64,128]{3,2,1,0:T(8,128)(2,1)S(1)}, bf16[2,10,64,128]{3,2,1,0:T(8,128)(2,1)S(1)}, u32[]{:S(2)}, u32[]{:S(2)}) %collective-permute-start.18) | collective-permute-done | bytes 327712 | tf_op jit(solution)/shard_map/ppermute | solution.py:34
  28.8 0.7 copy-done.10
  30.1 0.7 copy-done.12
  30.8 1.6 %collective-permute-start.21 = (bf16[2,10,64,128]{3,2,1,0:T(8,128)(2,1)S(1)}, bf16[2,10,64,128]{3,2,1,0:T(8,128)(2,1)S(1)}, u32[]{:S(2)}, u32[]{:S(2)}) collective-permute-start(bf16[2,10,64,128]{3,2,1,0:T(8,128)(2,1)S(1)} %collective-permute-done.19.refs_4_), channel_id=1, source_target_pairs={{0,4},{2,6},{4,12},{6,14},{8,0},{10,2},{12,20},{14,22},{16,8},{18,... | collective-permute-start | bytes 983048 | tf_op jit(solution)/shard_map/ppermute | solution.py:38
  32.4 2.0 %collective-permute-done.2.refs_3_ = bf16[2,10,64,128]{3,2,1,0:T(8,128)(2,1)S(1)} collective-permute-done((bf16[2,10,64,128]{3,2,1,0:T(8,128)(2,1)S(1)}, bf16[2,10,64,128]{3,2,1,0:T(8,128)(2,1)S(1)}, u32[]{:S(2)}, u32[]{:S(2)}) %collective-permute-start.2) | collective-permute-done | bytes 327712 | tf_op jit(solution)/shard_map/ppermute | solution.py:34
  34.8 1.5 %collective-permute-done.3.refs_4_ = bf16[2,10,64,128]{3,2,1,0:T(8,128)(2,1)S(1)} collective-permute-done((bf16[2,10,64,128]{3,2,1,0:T(8,128)(2,1)S(1)}, bf16[2,10,64,128]{3,2,1,0:T(8,128)(2,1)S(1)}, u32[]{:S(2)}, u32[]{:S(2)}) %collective-permute-start.3) | collective-permute-done | bytes 327712 | tf_op jit(solution)/shard_map/ppermute | solution.py:38
  36.3 0.7 copy-done.6
  37.0 0.7 copy-done.4
  38.2 0.7 copy-done.2
  39.0 0.7 copy-done.8
  39.7 2.1 %collective-permute-start.4 = (bf16[2,10,64,128]{3,2,1,0:T(8,128)(2,1)S(1)}, bf16[2,10,64,128]{3,2,1,0:T(8,128)(2,1)}, u32[]{:S(2)}, u32[]{:S(2)}) collective-permute-start(bf16[2,10,64,128]{3,2,1,0:T(8,128)(2,1)S(1)} %collective-permute-done.2.refs_3_), channel_id=1, source_target_pairs={{0,8},{2,10},{4,0},{6,2},{8,16},{10,18},{12,4},{14,6},{16,24},{18,... | collective-permute-start | bytes 983048 | tf_op jit(solution)/shard_map/ppermute | solution.py:34
  41.9 1.3 %collective-permute-start.22 = (bf16[2,10,64,128]{3,2,1,0:T(8,128)(2,1)S(1)}, bf16[2,10,64,128]{3,2,1,0:T(8,128)(2,1)S(1)}, u32[]{:S(2)}, u32[]{:S(2)}) collective-permute-start(bf16[2,10,64,128]{3,2,1,0:T(8,128)(2,1)S(1)} %collective-permute-done.21.refs_6_), channel_id=1, source_target_pairs={{0,4},{2,6},{4,12},{6,14},{8,0},{10,2},{12,20},{14,22},{16,8},{18,... | collective-permute-start | bytes 983048 | tf_op jit(solution)/shard_map/ppermute | solution.py:38
  43.2 1.7 %collective-permute-start.5 = (bf16[2,10,64,128]{3,2,1,0:T(8,128)(2,1)S(1)}, bf16[2,10,64,128]{3,2,1,0:T(8,128)(2,1)}, u32[]{:S(2)}, u32[]{:S(2)}) collective-permute-start(bf16[2,10,64,128]{3,2,1,0:T(8,128)(2,1)S(1)} %collective-permute-done.3.refs_4_), channel_id=1, source_target_pairs={{0,4},{2,6},{4,12},{6,14},{8,0},{10,2},{12,20},{14,22},{16,8},{18,... | collective-permute-start | bytes 983048 | tf_op jit(solution)/shard_map/ppermute | solution.py:38
  44.9 0.7 copy-done.18
  45.7 0.7 copy-done.14
  46.4 0.7 copy-done.20
  47.6 0.7 copy-done.16
  48.4 1.4 %collective-permute-done.4.refs_5_ = bf16[2,10,64,128]{3,2,1,0:T(8,128)(2,1)} collective-permute-done((bf16[2,10,64,128]{3,2,1,0:T(8,128)(2,1)S(1)}, bf16[2,10,64,128]{3,2,1,0:T(8,128)(2,1)}, u32[]{:S(2)}, u32[]{:S(2)}) %collective-permute-start.4) | collective-permute-done | bytes 327712 | tf_op jit(solution)/shard_map/ppermute | solution.py:34
  49.7 1.8 %collective-permute-start.6 = (bf16[2,10,64,128]{3,2,1,0:T(8,128)(2,1)}, bf16[2,10,64,128]{3,2,1,0:T(8,128)(2,1)}, u32[]{:S(2)}, u32[]{:S(2)}) collective-permute-start(bf16[2,10,64,128]{3,2,1,0:T(8,128)(2,1)} %collective-permute-done.4.refs_5_), channel_id=1, source_target_pairs={{0,8},{2,10},{4,0},{6,2},{8,16},{10,18},{12,4},{14,6},{16,24},{18,... | collective-permute-start | bytes 983048 | tf_op jit(solution)/shard_map/ppermute | solution.py:34
  51.5 1.0 collective-permute-done.22.refs_7_
  52.5 0.7 copy-done.22
  53.2 5.0 %collective-permute-done.5.refs_6_ = bf16[2,10,64,128]{3,2,1,0:T(8,128)(2,1)} collective-permute-done((bf16[2,10,64,128]{3,2,1,0:T(8,128)(2,1)S(1)}, bf16[2,10,64,128]{3,2,1,0:T(8,128)(2,1)}, u32[]{:S(2)}, u32[]{:S(2)}) %collective-permute-start.5) | collective-permute-done | bytes 327712 | tf_op jit(solution)/shard_map/ppermute | solution.py:38
  58.3 0.7 copy-done.24
  59.5 0.7 copy-done.26
  60.8 0.8 copy-done.28
  61.6 1.7 %copy-done = bf16[80,128,128]{2,1,0:T(8,128)(2,1)S(1)} copy-done((bf16[80,128,128]{2,1,0:T(8,128)(2,1)S(1)}, bf16[80,128,128]{2,1,0:T(8,128)(2,1)}, u32[]{:S(2)}) %copy-start) | copy-done | bytes 2621464
  63.4 1.1 copy-done.1
  64.4 0.7 copy-done.31
  65.1 0.7 copy-done.32
  65.9 5.8 %left_products.1.left_ref = bf16[80,128,256]{2,1,0:T(8,128)(2,1)} custom-call(s32[2]{0:T(128)S(1)} %pad_add_fusion.here_ref, s32[80]{0:T(128)S(1)} %copy-done.32, s32[2,10]{1,0:T(2,128)S(1)} %copy-done.31, bf16[2,10,128,128]{3,2,1,0:T(8,128)(2,1)S(1)} %copy-done.1, bf16[80,128,128]{2,1,0:T(8,128)(2,1)S(1)} %copy-done), custom_call_target="tpu_custom_call" | custom-call | flops 671088640 | bytes 9437184 | tf_op jit(solution)/shard_map/left_products/pallas_call | solution.py:161
  71.6 0.7 dynamic-slice_bitcast_fusion.owner_ref
  72.5 7.7 %right_products.3 = (bf16[40,64,128]{2,1,0:T(8,128)(2,1)S(1)}, bf16[40,64,128]{2,1,0:T(8,128)(2,1)}) custom-call(s32[16]{0:T(128)S(1)} %dynamic-slice_bitcast_fusion.owner_ref, s32[80]{0:T(128)S(1)} %copy-done.30, bf16[80,128,256]{2,1,0:T(8,128)(2,1)} %left_products.1.left_ref, bf16[2,10,64,128]{3,2,1,0:T(8,128)(2,1)S(1)} %get-tuple-element.13.refs_0_, ...), custom_call_target="tpu_custom_call" | custom-call | flops 335544320 | bytes 12582912 | tf_op jit(solution)/shard_map/right_products/pallas_call | solution.py:193
  80.2 1.6 %collective-permute-start.31 = (bf16[40,64,128]{2,1,0:T(8,128)(2,1)}, bf16[40,64,128]{2,1,0:T(8,128)(2,1)S(1)}, u32[]{:S(2)}, u32[]{:S(2)}) collective-permute-start(bf16[40,64,128]{2,1,0:T(8,128)(2,1)} %get-tuple-element.12), channel_id=1, source_target_pairs={{0,1},{1,0},{2,3},{3,2},{4,5},{5,4},{6,7},{7,6},{8,9},{9,8},{10,11... | collective-permute-start | bytes 1966088 | tf_op jit(solution)/shard_map/ppermute | solution.py:213
  81.8 8.6 %right_products.2 = (bf16[40,64,128]{2,1,0:T(8,128)(2,1)S(1)}, bf16[40,64,128]{2,1,0:T(8,128)(2,1)}) custom-call(s32[16]{0:T(128)S(1)} %dynamic-slice_bitcast_fusion.owner_ref, s32[80]{0:T(128)S(1)} %copy-done.30, bf16[80,128,256]{2,1,0:T(8,128)(2,1)} %left_products.1.left_ref, bf16[2,10,64,128]{3,2,1,0:T(8,128)(2,1)S(1)} %get-tuple-element.14.refs_0_, ...), custom_call_target="tpu_custom_call" | custom-call | flops 335544320 | bytes 12582912 | tf_op jit(solution)/shard_map/right_products/pallas_call | solution.py:193
  90.4 0.6 collective-permute-start.15
  91.0 7.0 %collective-permute-done.31.refs_3_ = bf16[40,64,128]{2,1,0:T(8,128)(2,1)S(1)} collective-permute-done((bf16[40,64,128]{2,1,0:T(8,128)(2,1)}, bf16[40,64,128]{2,1,0:T(8,128)(2,1)S(1)}, u32[]{:S(2)}, u32[]{:S(2)}) %collective-permute-start.31) | collective-permute-done | bytes 655392 | tf_op jit(solution)/shard_map/ppermute | solution.py:213
  98.0 13.7 %collective-permute-done.15.refs_1_ = bf16[40,64,128]{2,1,0:T(8,128)(2,1)S(1)} collective-permute-done((bf16[40,64,128]{2,1,0:T(8,128)(2,1)}, bf16[40,64,128]{2,1,0:T(8,128)(2,1)S(1)}, u32[]{:S(2)}, u32[]{:S(2)}) %collective-permute-start.15) | collective-permute-done | bytes 655392 | tf_op jit(solution)/shard_map/ppermute | solution.py:213
  111.7 2.1 %join_columns.1 = bf16[80,64,128]{2,1,0:T(8,128)(2,1)} custom-call(bf16[40,64,128]{2,1,0:T(8,128)(2,1)S(1)} %get-tuple-element.9.refs_0_, bf16[40,64,128]{2,1,0:T(8,128)(2,1)S(1)} %collective-permute-done.15.refs_1_, bf16[40,64,128]{2,1,0:T(8,128)(2,1)S(1)} %get-tuple-element.11.refs_2_, bf16[40,64,128]{2,1,0:T(8,128)(2,1)S(1)} %collective-permute-done.31.refs_3_), custom_call_target="tpu_custom_call" | custom-call | bytes 4194304 | tf_op jit(solution)/shard_map/join_columns/pallas_call | solution.py:215
  (89 shorter events, 4.1 us)
Async XLA Ops:
  1.1 11.6 %collective-permute-start.17 = (bf16[2,10,64,128]{3,2,1,0:T(8,128)(2,1)S(1)}, bf16[2,10,64,128]{3,2,1,0:T(8,128)(2,1)S(1)}, u32[]{:S(2)}, u32[]{:S(2)}) collective-permute-start(bf16[2,10,64,128]{3,2,1,0:T(8,128)(2,1)S(1)} %get-tuple-element.13.refs_0_), channel_id=1, source_target_pairs={{0,4},{2,6},{4,12},{6,14},{8,0},{10,2},{12,20},{14,22},{16,8},{18,... | collective-permute-start | bytes 983048 | tf_op jit(solution)/shard_map/ppermute | solution.py:38
  4.1 10.6 %collective-permute-start.16 = (bf16[2,10,64,128]{3,2,1,0:T(8,128)(2,1)S(1)}, bf16[2,10,64,128]{3,2,1,0:T(8,128)(2,1)S(1)}, u32[]{:S(2)}, u32[]{:S(2)}) collective-permute-start(bf16[2,10,64,128]{3,2,1,0:T(8,128)(2,1)S(1)} %get-tuple-element.13.refs_0_), channel_id=1, source_target_pairs={{0,8},{2,10},{4,0},{6,2},{8,16},{10,18},{12,4},{14,6},{16,24},{18,... | collective-permute-start | bytes 983048 | tf_op jit(solution)/shard_map/ppermute | solution.py:34
  4.3 12.1 %collective-permute-start.23 = (bf16[2,10,64,128]{3,2,1,0:T(8,128)(2,1)S(1)}, bf16[2,10,64,128]{3,2,1,0:T(8,128)(2,1)S(1)}, u32[]{:S(2)}, u32[]{:S(2)}) collective-permute-start(bf16[2,10,64,128]{3,2,1,0:T(8,128)(2,1)S(1)} %get-tuple-element.13.refs_0_), channel_id=1, source_target_pairs={{0,2},{2,0},{4,6},{6,4},{8,10},{10,8},{12,14},{14,12},{16,18},{18,... | collective-permute-start | bytes 983048 | tf_op jit(solution)/shard_map/ppermute | solution.py:41
  4.3 17.5 %collective-permute-start = (bf16[2,10,64,128]{3,2,1,0:T(8,128)(2,1)S(1)}, bf16[2,10,64,128]{3,2,1,0:T(8,128)(2,1)S(1)}, u32[]{:S(2)}, u32[]{:S(2)}) collective-permute-start(bf16[2,10,64,128]{3,2,1,0:T(8,128)(2,1)S(1)} %get-tuple-element.14.refs_0_), channel_id=1, source_target_pairs={{0,8},{2,10},{4,0},{6,2},{8,16},{10,18},{12,4},{14,6},{16,24},{18,... | collective-permute-start | bytes 983048 | tf_op jit(solution)/shard_map/ppermute | solution.py:34
  6.2 15.5 %collective-permute-start.1 = (bf16[2,10,64,128]{3,2,1,0:T(8,128)(2,1)S(1)}, bf16[2,10,64,128]{3,2,1,0:T(8,128)(2,1)S(1)}, u32[]{:S(2)}, u32[]{:S(2)}) collective-permute-start(bf16[2,10,64,128]{3,2,1,0:T(8,128)(2,1)S(1)} %get-tuple-element.14.refs_0_), channel_id=1, source_target_pairs={{0,4},{2,6},{4,12},{6,14},{8,0},{10,2},{12,20},{14,22},{16,8},{18,... | collective-permute-start | bytes 983048 | tf_op jit(solution)/shard_map/ppermute | solution.py:38
  12.7 9.6 %collective-permute-start.7 = (bf16[2,10,64,128]{3,2,1,0:T(8,128)(2,1)S(1)}, bf16[2,10,64,128]{3,2,1,0:T(8,128)(2,1)S(1)}, u32[]{:S(2)}, u32[]{:S(2)}) collective-permute-start(bf16[2,10,64,128]{3,2,1,0:T(8,128)(2,1)S(1)} %get-tuple-element.14.refs_0_), channel_id=1, source_target_pairs={{0,2},{2,0},{4,6},{6,4},{8,10},{10,8},{12,14},{14,12},{16,18},{18,... | collective-permute-start | bytes 983048 | tf_op jit(solution)/shard_map/ppermute | solution.py:41
  14.8 11.2 %collective-permute-start.19 = (bf16[2,10,64,128]{3,2,1,0:T(8,128)(2,1)S(1)}, bf16[2,10,64,128]{3,2,1,0:T(8,128)(2,1)S(1)}, u32[]{:S(2)}, u32[]{:S(2)}) collective-permute-start(bf16[2,10,64,128]{3,2,1,0:T(8,128)(2,1)S(1)} %collective-permute-done.17.refs_2_), channel_id=1, source_target_pairs={{0,4},{2,6},{4,12},{6,14},{8,0},{10,2},{12,20},{14,22},{16,8},{18,... | collective-permute-start | bytes 983048 | tf_op jit(solution)/shard_map/ppermute | solution.py:38
  16.3 12.5 %collective-permute-start.18 = (bf16[2,10,64,128]{3,2,1,0:T(8,128)(2,1)S(1)}, bf16[2,10,64,128]{3,2,1,0:T(8,128)(2,1)S(1)}, u32[]{:S(2)}, u32[]{:S(2)}) collective-permute-start(bf16[2,10,64,128]{3,2,1,0:T(8,128)(2,1)S(1)} %collective-permute-done.16.refs_1_), channel_id=1, source_target_pairs={{0,8},{2,10},{4,0},{6,2},{8,16},{10,18},{12,4},{14,6},{16,24},{18,... | collective-permute-start | bytes 983048 | tf_op jit(solution)/shard_map/ppermute | solution.py:34
  21.8 7.0 %collective-permute-start.24 = (bf16[2,10,64,128]{3,2,1,0:T(8,128)(2,1)S(1)}, bf16[2,10,64,128]{3,2,1,0:T(8,128)(2,1)S(1)}, u32[]{:S(2)}, u32[]{:S(2)}) collective-permute-start(bf16[2,10,64,128]{3,2,1,0:T(8,128)(2,1)S(1)} %collective-permute-done.16.refs_1_), channel_id=1, source_target_pairs={{0,2},{2,0},{4,6},{6,4},{8,10},{10,8},{12,14},{14,12},{16,18},{18,... | collective-permute-start | bytes 983048 | tf_op jit(solution)/shard_map/ppermute | solution.py:41
  21.8 8.3 %collective-permute-start.25 = (bf16[2,10,64,128]{3,2,1,0:T(8,128)(2,1)S(1)}, bf16[2,10,64,128]{3,2,1,0:T(8,128)(2,1)S(1)}, u32[]{:S(2)}, u32[]{:S(2)}) collective-permute-start(bf16[2,10,64,128]{3,2,1,0:T(8,128)(2,1)S(1)} %collective-permute-done.17.refs_2_), channel_id=1, source_target_pairs={{0,2},{2,0},{4,6},{6,4},{8,10},{10,8},{12,14},{14,12},{16,18},{18,... | collective-permute-start | bytes 983048 | tf_op jit(solution)/shard_map/ppermute | solution.py:41
  22.3 12.1 %collective-permute-start.2 = (bf16[2,10,64,128]{3,2,1,0:T(8,128)(2,1)S(1)}, bf16[2,10,64,128]{3,2,1,0:T(8,128)(2,1)S(1)}, u32[]{:S(2)}, u32[]{:S(2)}) collective-permute-start(bf16[2,10,64,128]{3,2,1,0:T(8,128)(2,1)S(1)} %collective-permute-done.refs_1_), channel_id=1, source_target_pairs={{0,8},{2,10},{4,0},{6,2},{8,16},{10,18},{12,4},{14,6},{16,24},{18,... | collective-permute-start | bytes 983048 | tf_op jit(solution)/shard_map/ppermute | solution.py:34
  26.0 10.3 %collective-permute-start.3 = (bf16[2,10,64,128]{3,2,1,0:T(8,128)(2,1)S(1)}, bf16[2,10,64,128]{3,2,1,0:T(8,128)(2,1)S(1)}, u32[]{:S(2)}, u32[]{:S(2)}) collective-permute-start(bf16[2,10,64,128]{3,2,1,0:T(8,128)(2,1)S(1)} %collective-permute-done.1.refs_2_), channel_id=1, source_target_pairs={{0,4},{2,6},{4,12},{6,14},{8,0},{10,2},{12,20},{14,22},{16,8},{18,... | collective-permute-start | bytes 983048 | tf_op jit(solution)/shard_map/ppermute | solution.py:38
  28.8 8.2 %collective-permute-start.8 = (bf16[2,10,64,128]{3,2,1,0:T(8,128)(2,1)S(1)}, bf16[2,10,64,128]{3,2,1,0:T(8,128)(2,1)S(1)}, u32[]{:S(2)}, u32[]{:S(2)}) collective-permute-start(bf16[2,10,64,128]{3,2,1,0:T(8,128)(2,1)S(1)} %collective-permute-done.refs_1_), channel_id=1, source_target_pairs={{0,2},{2,0},{4,6},{6,4},{8,10},{10,8},{12,14},{14,12},{16,18},{18,... | collective-permute-start | bytes 983048 | tf_op jit(solution)/shard_map/ppermute | solution.py:41
  29.6 9.4 %collective-permute-start.9 = (bf16[2,10,64,128]{3,2,1,0:T(8,128)(2,1)S(1)}, bf16[2,10,64,128]{3,2,1,0:T(8,128)(2,1)S(1)}, u32[]{:S(2)}, u32[]{:S(2)}) collective-permute-start(bf16[2,10,64,128]{3,2,1,0:T(8,128)(2,1)S(1)} %collective-permute-done.1.refs_2_), channel_id=1, source_target_pairs={{0,2},{2,0},{4,6},{6,4},{8,10},{10,8},{12,14},{14,12},{16,18},{18,... | collective-permute-start | bytes 983048 | tf_op jit(solution)/shard_map/ppermute | solution.py:41
  30.8 11.1 %collective-permute-start.21 = (bf16[2,10,64,128]{3,2,1,0:T(8,128)(2,1)S(1)}, bf16[2,10,64,128]{3,2,1,0:T(8,128)(2,1)S(1)}, u32[]{:S(2)}, u32[]{:S(2)}) collective-permute-start(bf16[2,10,64,128]{3,2,1,0:T(8,128)(2,1)S(1)} %collective-permute-done.19.refs_4_), channel_id=1, source_target_pairs={{0,4},{2,6},{4,12},{6,14},{8,0},{10,2},{12,20},{14,22},{16,8},{18,... | collective-permute-start | bytes 983048 | tf_op jit(solution)/shard_map/ppermute | solution.py:38
  34.4 8.9 %collective-permute-start.20 = (bf16[2,10,64,128]{3,2,1,0:T(8,128)(2,1)S(1)}, bf16[2,10,64,128]{3,2,1,0:T(8,128)(2,1)S(1)}, u32[]{:S(2)}, u32[]{:S(2)}) collective-permute-start(bf16[2,10,64,128]{3,2,1,0:T(8,128)(2,1)S(1)} %collective-permute-done.18.refs_3_), channel_id=1, source_target_pairs={{0,8},{2,10},{4,0},{6,2},{8,16},{10,18},{12,4},{14,6},{16,24},{18,... | collective-permute-start | bytes 983048 | tf_op jit(solution)/shard_map/ppermute | solution.py:34
  36.3 8.7 %collective-permute-start.26 = (bf16[2,10,64,128]{3,2,1,0:T(8,128)(2,1)S(1)}, bf16[2,10,64,128]{3,2,1,0:T(8,128)(2,1)S(1)}, u32[]{:S(2)}, u32[]{:S(2)}) collective-permute-start(bf16[2,10,64,128]{3,2,1,0:T(8,128)(2,1)S(1)} %collective-permute-done.18.refs_3_), channel_id=1, source_target_pairs={{0,2},{2,0},{4,6},{6,4},{8,10},{10,8},{12,14},{14,12},{16,18},{18,... | collective-permute-start | bytes 983048 | tf_op jit(solution)/shard_map/ppermute | solution.py:41
  37.7 8.7 %collective-permute-start.27 = (bf16[2,10,64,128]{3,2,1,0:T(8,128)(2,1)S(1)}, bf16[2,10,64,128]{3,2,1,0:T(8,128)(2,1)S(1)}, u32[]{:S(2)}, u32[]{:S(2)}) collective-permute-start(bf16[2,10,64,128]{3,2,1,0:T(8,128)(2,1)S(1)} %collective-permute-done.19.refs_4_), channel_id=1, source_target_pairs={{0,2},{2,0},{4,6},{6,4},{8,10},{10,8},{12,14},{14,12},{16,18},{18,... | collective-permute-start | bytes 983048 | tf_op jit(solution)/shard_map/ppermute | solution.py:41
  39.7 10.1 %collective-permute-start.4 = (bf16[2,10,64,128]{3,2,1,0:T(8,128)(2,1)S(1)}, bf16[2,10,64,128]{3,2,1,0:T(8,128)(2,1)}, u32[]{:S(2)}, u32[]{:S(2)}) collective-permute-start(bf16[2,10,64,128]{3,2,1,0:T(8,128)(2,1)S(1)} %collective-permute-done.2.refs_3_), channel_id=1, source_target_pairs={{0,8},{2,10},{4,0},{6,2},{8,16},{10,18},{12,4},{14,6},{16,24},{18,... | collective-permute-start | bytes 983048 | tf_op jit(solution)/shard_map/ppermute | solution.py:34
  41.9 10.6 %collective-permute-start.22 = (bf16[2,10,64,128]{3,2,1,0:T(8,128)(2,1)S(1)}, bf16[2,10,64,128]{3,2,1,0:T(8,128)(2,1)S(1)}, u32[]{:S(2)}, u32[]{:S(2)}) collective-permute-start(bf16[2,10,64,128]{3,2,1,0:T(8,128)(2,1)S(1)} %collective-permute-done.21.refs_6_), channel_id=1, source_target_pairs={{0,4},{2,6},{4,12},{6,14},{8,0},{10,2},{12,20},{14,22},{16,8},{18,... | collective-permute-start | bytes 983048 | tf_op jit(solution)/shard_map/ppermute | solution.py:38
  43.2 15.0 %collective-permute-start.5 = (bf16[2,10,64,128]{3,2,1,0:T(8,128)(2,1)S(1)}, bf16[2,10,64,128]{3,2,1,0:T(8,128)(2,1)}, u32[]{:S(2)}, u32[]{:S(2)}) collective-permute-start(bf16[2,10,64,128]{3,2,1,0:T(8,128)(2,1)S(1)} %collective-permute-done.3.refs_4_), channel_id=1, source_target_pairs={{0,4},{2,6},{4,12},{6,14},{8,0},{10,2},{12,20},{14,22},{16,8},{18,... | collective-permute-start | bytes 983048 | tf_op jit(solution)/shard_map/ppermute | solution.py:38
  45.7 12.6 %collective-permute-start.29 = (bf16[2,10,64,128]{3,2,1,0:T(8,128)(2,1)S(1)}, bf16[2,10,64,128]{3,2,1,0:T(8,128)(2,1)S(1)}, u32[]{:S(2)}, u32[]{:S(2)}) collective-permute-start(bf16[2,10,64,128]{3,2,1,0:T(8,128)(2,1)S(1)} %collective-permute-done.21.refs_6_), channel_id=1, source_target_pairs={{0,2},{2,0},{4,6},{6,4},{8,10},{10,8},{12,14},{14,12},{16,18},{18,... | collective-permute-start | bytes 983048 | tf_op jit(solution)/shard_map/ppermute | solution.py:41
  47.1 12.4 %collective-permute-start.28 = (bf16[2,10,64,128]{3,2,1,0:T(8,128)(2,1)S(1)}, bf16[2,10,64,128]{3,2,1,0:T(8,128)(2,1)S(1)}, u32[]{:S(2)}, u32[]{:S(2)}) collective-permute-start(bf16[2,10,64,128]{3,2,1,0:T(8,128)(2,1)S(1)} %collective-permute-done.20.refs_5_), channel_id=1, source_target_pairs={{0,2},{2,0},{4,6},{6,4},{8,10},{10,8},{12,14},{14,12},{16,18},{18,... | collective-permute-start | bytes 983048 | tf_op jit(solution)/shard_map/ppermute | solution.py:41
  49.7 10.5 %collective-permute-start.6 = (bf16[2,10,64,128]{3,2,1,0:T(8,128)(2,1)}, bf16[2,10,64,128]{3,2,1,0:T(8,128)(2,1)}, u32[]{:S(2)}, u32[]{:S(2)}) collective-permute-start(bf16[2,10,64,128]{3,2,1,0:T(8,128)(2,1)} %collective-permute-done.4.refs_5_), channel_id=1, source_target_pairs={{0,8},{2,10},{4,0},{6,2},{8,16},{10,18},{12,4},{14,6},{16,24},{18,... | collective-permute-start | bytes 983048 | tf_op jit(solution)/shard_map/ppermute | solution.py:34
  52.5 8.3 %collective-permute-start.30 = (bf16[2,10,64,128]{3,2,1,0:T(8,128)(2,1)S(1)}, bf16[2,10,64,128]{3,2,1,0:T(8,128)(2,1)S(1)}, u32[]{:S(2)}, u32[]{:S(2)}) collective-permute-start(bf16[2,10,64,128]{3,2,1,0:T(8,128)(2,1)S(1)} %collective-permute-done.22.refs_7_), channel_id=1, source_target_pairs={{0,2},{2,0},{4,6},{6,4},{8,10},{10,8},{12,14},{14,12},{16,18},{18,... | collective-permute-start | bytes 983048 | tf_op jit(solution)/shard_map/ppermute | solution.py:41
  58.2 21.9 %collective-permute-start.10 = (bf16[2,10,64,128]{3,2,1,0:T(8,128)(2,1)S(1)}, bf16[2,10,64,128]{3,2,1,0:T(8,128)(2,1)}, u32[]{:S(2)}, u32[]{:S(2)}) collective-permute-start(bf16[2,10,64,128]{3,2,1,0:T(8,128)(2,1)S(1)} %collective-permute-done.2.refs_3_), channel_id=1, source_target_pairs={{0,2},{2,0},{4,6},{6,4},{8,10},{10,8},{12,14},{14,12},{16,18},{18,... | collective-permute-start | bytes 983048 | tf_op jit(solution)/shard_map/ppermute | solution.py:41
  59.0 22.8 %collective-permute-start.11 = (bf16[2,10,64,128]{3,2,1,0:T(8,128)(2,1)S(1)}, bf16[2,10,64,128]{3,2,1,0:T(8,128)(2,1)}, u32[]{:S(2)}, u32[]{:S(2)}) collective-permute-start(bf16[2,10,64,128]{3,2,1,0:T(8,128)(2,1)S(1)} %collective-permute-done.3.refs_4_), channel_id=1, source_target_pairs={{0,2},{2,0},{4,6},{6,4},{8,10},{10,8},{12,14},{14,12},{16,18},{18,... | collective-permute-start | bytes 983048 | tf_op jit(solution)/shard_map/ppermute | solution.py:41
  60.2 21.5 %collective-permute-start.12 = (bf16[2,10,64,128]{3,2,1,0:T(8,128)(2,1)}, bf16[2,10,64,128]{3,2,1,0:T(8,128)(2,1)}, u32[]{:S(2)}, u32[]{:S(2)}) collective-permute-start(bf16[2,10,64,128]{3,2,1,0:T(8,128)(2,1)} %collective-permute-done.4.refs_5_), channel_id=1, source_target_pairs={{0,2},{2,0},{4,6},{6,4},{8,10},{10,8},{12,14},{14,12},{16,18},{18,... | collective-permute-start | bytes 983048 | tf_op jit(solution)/shard_map/ppermute | solution.py:41
  60.3 21.5 %collective-permute-start.13 = (bf16[2,10,64,128]{3,2,1,0:T(8,128)(2,1)}, bf16[2,10,64,128]{3,2,1,0:T(8,128)(2,1)}, u32[]{:S(2)}, u32[]{:S(2)}) collective-permute-start(bf16[2,10,64,128]{3,2,1,0:T(8,128)(2,1)} %collective-permute-done.5.refs_6_), channel_id=1, source_target_pairs={{0,2},{2,0},{4,6},{6,4},{8,10},{10,8},{12,14},{14,12},{16,18},{18,... | collective-permute-start | bytes 983048 | tf_op jit(solution)/shard_map/ppermute | solution.py:41
  61.5 20.3 %collective-permute-start.14 = (bf16[2,10,64,128]{3,2,1,0:T(8,128)(2,1)}, bf16[2,10,64,128]{3,2,1,0:T(8,128)(2,1)}, u32[]{:S(2)}, u32[]{:S(2)}) collective-permute-start(bf16[2,10,64,128]{3,2,1,0:T(8,128)(2,1)} %collective-permute-done.6.refs_7_), channel_id=1, source_target_pairs={{0,2},{2,0},{4,6},{6,4},{8,10},{10,8},{12,14},{14,12},{16,18},{18,... | collective-permute-start | bytes 983048 | tf_op jit(solution)/shard_map/ppermute | solution.py:41
  61.6 1.7 %copy-start = (bf16[80,128,128]{2,1,0:T(8,128)(2,1)S(1)}, bf16[80,128,128]{2,1,0:T(8,128)(2,1)}, u32[]{:S(2)}) copy-start(bf16[80,128,128]{2,1,0:T(8,128)(2,1)} %wave_ref.1) | copy-start | bytes 7864324
  65.8 6.6 %copy-start.3 = (bf16[2,10,64,128]{3,2,1,0:T(8,128)(2,1)S(1)}, bf16[2,10,64,128]{3,2,1,0:T(8,128)(2,1)}, u32[]{:S(2)}) copy-start(bf16[2,10,64,128]{3,2,1,0:T(8,128)(2,1)} %copy-done.2) | copy-start | bytes 983044
  65.8 6.6 %copy-start.7 = (bf16[2,10,64,128]{3,2,1,0:T(8,128)(2,1)S(1)}, bf16[2,10,64,128]{3,2,1,0:T(8,128)(2,1)}, u32[]{:S(2)}) copy-start(bf16[2,10,64,128]{3,2,1,0:T(8,128)(2,1)} %copy-done.6) | copy-start | bytes 983044
  65.8 6.6 %copy-start.11 = (bf16[2,10,64,128]{3,2,1,0:T(8,128)(2,1)S(1)}, bf16[2,10,64,128]{3,2,1,0:T(8,128)(2,1)}, u32[]{:S(2)}) copy-start(bf16[2,10,64,128]{3,2,1,0:T(8,128)(2,1)} %copy-done.10) | copy-start | bytes 983044
  65.8 6.6 %copy-start.13 = (bf16[2,10,64,128]{3,2,1,0:T(8,128)(2,1)S(1)}, bf16[2,10,64,128]{3,2,1,0:T(8,128)(2,1)}, u32[]{:S(2)}) copy-start(bf16[2,10,64,128]{3,2,1,0:T(8,128)(2,1)} %copy-done.12) | copy-start | bytes 983044
  65.8 6.6 %copy-start.15 = (bf16[2,10,64,128]{3,2,1,0:T(8,128)(2,1)S(1)}, bf16[2,10,64,128]{3,2,1,0:T(8,128)(2,1)}, u32[]{:S(2)}) copy-start(bf16[2,10,64,128]{3,2,1,0:T(8,128)(2,1)} %copy-done.14) | copy-start | bytes 983044
  65.8 6.6 %copy-start.17 = (bf16[2,10,64,128]{3,2,1,0:T(8,128)(2,1)S(1)}, bf16[2,10,64,128]{3,2,1,0:T(8,128)(2,1)}, u32[]{:S(2)}) copy-start(bf16[2,10,64,128]{3,2,1,0:T(8,128)(2,1)} %copy-done.16) | copy-start | bytes 983044
  65.8 6.6 %copy-start.19 = (bf16[2,10,64,128]{3,2,1,0:T(8,128)(2,1)S(1)}, bf16[2,10,64,128]{3,2,1,0:T(8,128)(2,1)}, u32[]{:S(2)}) copy-start(bf16[2,10,64,128]{3,2,1,0:T(8,128)(2,1)} %copy-done.18) | copy-start | bytes 983044
  65.8 6.6 %copy-start.21 = (bf16[2,10,64,128]{3,2,1,0:T(8,128)(2,1)S(1)}, bf16[2,10,64,128]{3,2,1,0:T(8,128)(2,1)}, u32[]{:S(2)}) copy-start(bf16[2,10,64,128]{3,2,1,0:T(8,128)(2,1)} %copy-done.20) | copy-start | bytes 983044
  65.8 6.6 %copy-start.23 = (bf16[2,10,64,128]{3,2,1,0:T(8,128)(2,1)S(1)}, bf16[2,10,64,128]{3,2,1,0:T(8,128)(2,1)}, u32[]{:S(2)}) copy-start(bf16[2,10,64,128]{3,2,1,0:T(8,128)(2,1)} %copy-done.22) | copy-start | bytes 983044
  65.8 6.6 %copy-start.25 = (bf16[2,10,64,128]{3,2,1,0:T(8,128)(2,1)S(1)}, bf16[2,10,64,128]{3,2,1,0:T(8,128)(2,1)}, u32[]{:S(2)}) copy-start(bf16[2,10,64,128]{3,2,1,0:T(8,128)(2,1)} %copy-done.24) | copy-start | bytes 983044
  65.8 6.6 %copy-start.27 = (bf16[2,10,64,128]{3,2,1,0:T(8,128)(2,1)S(1)}, bf16[2,10,64,128]{3,2,1,0:T(8,128)(2,1)}, u32[]{:S(2)}) copy-start(bf16[2,10,64,128]{3,2,1,0:T(8,128)(2,1)} %copy-done.26) | copy-start | bytes 983044
  65.9 6.6 %copy-start.29 = (bf16[2,10,64,128]{3,2,1,0:T(8,128)(2,1)S(1)}, bf16[2,10,64,128]{3,2,1,0:T(8,128)(2,1)}, u32[]{:S(2)}) copy-start(bf16[2,10,64,128]{3,2,1,0:T(8,128)(2,1)} %copy-done.28) | copy-start | bytes 983044
  65.9 6.6 %copy-start.30 = (s32[80]{0:T(128)S(1)}, s32[80]{0:T(128)}, u32[]{:S(2)}) copy-start(s32[80]{0:T(128)} %sector_ref.5) | copy-start | bytes 964
  72.4 9.4 %copy-start.5 = (bf16[2,10,64,128]{3,2,1,0:T(8,128)(2,1)S(1)}, bf16[2,10,64,128]{3,2,1,0:T(8,128)(2,1)}, u32[]{:S(2)}) copy-start(bf16[2,10,64,128]{3,2,1,0:T(8,128)(2,1)} %copy-done.4) | copy-start | bytes 983044
  72.5 9.4 %copy-start.9 = (bf16[2,10,64,128]{3,2,1,0:T(8,128)(2,1)S(1)}, bf16[2,10,64,128]{3,2,1,0:T(8,128)(2,1)}, u32[]{:S(2)}) copy-start(bf16[2,10,64,128]{3,2,1,0:T(8,128)(2,1)} %copy-done.8) | copy-start | bytes 983044
  80.2 17.8 %collective-permute-start.31 = (bf16[40,64,128]{2,1,0:T(8,128)(2,1)}, bf16[40,64,128]{2,1,0:T(8,128)(2,1)S(1)}, u32[]{:S(2)}, u32[]{:S(2)}) collective-permute-start(bf16[40,64,128]{2,1,0:T(8,128)(2,1)} %get-tuple-element.12), channel_id=1, source_target_pairs={{0,1},{1,0},{2,3},{3,2},{4,5},{5,4},{6,7},{7,6},{8,9},{9,8},{10,11... | collective-permute-start | bytes 1966088 | tf_op jit(solution)/shard_map/ppermute | solution.py:213
  90.4 21.3 %collective-permute-start.15 = (bf16[40,64,128]{2,1,0:T(8,128)(2,1)}, bf16[40,64,128]{2,1,0:T(8,128)(2,1)S(1)}, u32[]{:S(2)}, u32[]{:S(2)}) collective-permute-start(bf16[40,64,128]{2,1,0:T(8,128)(2,1)} %get-tuple-element.10), channel_id=1, source_target_pairs={{0,1},{1,0},{2,3},{3,2},{4,5},{5,4},{6,7},{7,6},{8,9},{9,8},{10,11... | collective-permute-start | bytes 1966088 | tf_op jit(solution)/shard_map/ppermute | solution.py:213
  (17 other events, 12.7 us)

commit v2 on v1

v2 whole, which is shorter than its diff:
```python
import functools

import jax
import jax.numpy as jnp
import numpy as np
from jax import lax
from jax.experimental import pallas as pl
from jax.experimental.pallas import tpu as pltpu
from jax.sharding import PartitionSpec as P

PLAN = "0P 0Q 0P 0Q La:0P 0Q Lb:0P 0Q:1P 0P:1Q 1P m0 m0:1Q 1P 1Q 1P y0:m1"
RING_LIMIT = 16
VMEM_LIMIT = 16 * 1024 * 1024
UNROLL = 10


def chip_ring(chips):
    across = 2 if chips % 2 == 0 else 1
    up = [z * across for z in range(chips // across)]
    down = [z * across + 1 for z in reversed(range(chips // across))] if across == 2 else []
    return up + down


def swap_cores(value, owners):
    return lax.ppermute(value, "sec", [(d, d ^ 1) for d in range(owners)])


def step_round(value, owners):
    order = chip_ring(owners // 2)
    after = {chip: order[(i + 1) % len(order)] for i, chip in enumerate(order)}
    before = {chip: order[i - 1] for i, chip in enumerate(order)}
    pairs = [(d, 2 * (after if d % 2 == 0 else before)[d // 2] + d % 2) for d in range(owners)]
    return lax.ppermute(value, "sec", pairs)


class RingGather:
    def __init__(self, part, owners):
        self.owners, self.chips = owners, owners // 2
        self.heads = [part, swap_cores(part, owners)]
        self.steps = [0, 0]
        self.pieces = list(self.heads)
        self.places = [(0, 0), (0, 1)]

    def rounds(self, lane):
        return self.chips // 2 if lane == 0 else (self.chips - 1) // 2

    def advance(self, lane, wait_for=()):
        head = self.heads[lane]
        if wait_for:
            head = lax.optimization_barrier((head, *wait_for))[0]
        head = step_round(head, self.owners)
        self.heads[lane] = head
        self.steps[lane] += 1
        self.pieces += [head, swap_cores(head, self.owners)]
        self.places += [(self.steps[lane], lane), (-self.steps[lane], 1 - lane)]

    def table(self):
        order = chip_ring(self.chips)
        place = {chip: i for i, chip in enumerate(order)}
        owners = np.zeros((self.owners, len(self.pieces)), np.int32)
        for d in range(self.owners):
            way = 1 if d % 2 else -1
            for number, (shift, other) in enumerate(self.places):
                chip = order[(place[d // 2] + way * shift) % self.chips]
                owners[d, number] = 2 * chip + (d % 2) ^ other
        return owners


def left_kernel(index_ref, operator_ref, wave_ref, out_ref, *, parties):
    terms, _, width, _ = operator_ref.shape
    blocks = wave_ref.shape[0]
    rows = width // parties
    own, before = index_ref[0], 1

    def one_block(b, carry):
        local = index_ref[before + b]
        bands = [
            operator_ref[k, local, pl.ds(pl.multiple_of(lax.rem(own + j, parties) * rows, rows), rows), :]
            for k in range(terms)
            for j in range(parties)
        ]
        product = jnp.dot(
            jnp.concatenate(bands, axis=0), wave_ref[b], preferred_element_type=jnp.float32
        )
        for k in range(terms):
            out_ref[b, :, k * width : (k + 1) * width] = product[
                k * width : (k + 1) * width
            ].astype(out_ref.dtype)
        return carry

    lax.fori_loop(0, blocks, one_block, 0, unroll=UNROLL)


def right_kernel(index_ref, *refs, lefts, pieces, parties):
    left_refs, refs = refs[:lefts], refs[lefts:]
    piece_refs, out_refs = refs[:pieces], refs[pieces : pieces + parties]
    held, arrived = refs[pieces + parties :]
    terms, total, columns, width = held.shape
    sectors = piece_refs[0].shape[1]
    blocks, height, _ = left_refs[0].shape
    rows = height // parties
    pack = width // columns
    before = pieces

    copies = [
        pltpu.make_async_copy(
            piece, held.at[:, pl.ds(index_ref[number] * sectors, sectors)], arrived.at[number]
        )
        for number, piece in enumerate(piece_refs)
    ]
    for copy in copies:
        copy.start()
    for copy in copies:
        copy.wait()
    lane = lax.broadcasted_iota(jnp.int32, (height, width), 1) // columns

    def one_group(g, carry):
        factors = []
        for q in range(pack):
            sector = index_ref[before + g * pack + q]
            factors.append(jnp.concatenate([held[k, sector] for k in range(terms)], axis=1))
        factor = jnp.concatenate(factors, axis=0)
        left = jnp.concatenate(
            [jnp.concatenate([ref[g * pack + q] for q in range(pack)], axis=0) for ref in left_refs],
            axis=1,
        )
        product = lax.dot_general(
            left, factor, (((1,), (1,)), ((), ())), preferred_element_type=jnp.float32
        ).reshape(pack, height, width)
        chosen = product[0]
        for q in range(1, pack):
            chosen = jnp.where(lane == q, product[q], chosen)
        for j in range(parties):
            out_refs[j][g] = chosen[j * rows : (j + 1) * rows].astype(out_refs[j].dtype)
        return carry

    lax.fori_loop(0, blocks // pack, one_group, 0, unroll=min(UNROLL, blocks // pack))


def join_kernel(own_ref, *refs, layout, parties):
    out_ref = refs[-1]
    blocks, rows, width = out_ref.shape
    most = max(width // columns for columns, _ in layout)
    lane = lax.broadcasted_iota(jnp.int32, (rows, width), 1)
    own = own_ref[0]

    def one_group(g, carry):
        bands = []
        for c, (columns, by_columns) in enumerate(layout):
            pack = width // columns
            given = refs[c * parties : (c + 1) * parties]
            inside = [[] for _ in range(parties if by_columns else 1)]
            for t in range(most // pack):
                values = [ref[g * (most // pack) + t].astype(jnp.float32) for ref in given]
                if by_columns:
                    inside[0].append(jnp.where(own == 0, values[0], values[1]))
                    inside[1].append(jnp.where(own == 0, values[1], values[0]))
                else:
                    total = values[0]
                    for other in values[1:]:
                        total = total + other
                    inside[0].append(total)
            bands += [(columns, packed) for packed in inside]
        for b in range(most):
            start, value = 0, None
            for columns, packed in bands:
                pack = width // columns
                turn = (start - (b % pack) * columns) % width
                moved = packed[b // pack]
                moved = pltpu.roll(moved, turn, 1) if turn else moved
                value = moved if value is None else jnp.where(lane >= start, moved, value)
                start += columns
            out_ref[g * most + b] = value.astype(out_ref.dtype)
        return carry

    lax.fori_loop(0, blocks // most, one_group, 0, unroll=4)


def follow_plan(rings, lefts, finish):
    done, results = dict(lefts), []
    for word in PLAN.split():
        wants, _, act = word.rpartition(":")
        others = [value for want in wants.split(",") if want for value in done[want]]
        if act[0] == "m":
            number = int(act[1])
            ring = rings[number]
            out, partial = finish(number, ring.pieces, ring.table(), others)
            results += out
            done[act], done["y" + act[1]] = partial, out[1:]
        else:
            ring, lane = rings[int(act[0])], "PQ".index(act[1])
            if ring.steps[lane] < ring.rounds(lane):
                ring.advance(lane, others)
            done[act] = [ring.heads[lane]]
    return results


def on_device(wavefunction, left_sector, right_sector, term_mask, left_operators, right_operators):
    owners, parties = lax.axis_size("sec"), lax.axis_size("mpo")
    me, own = lax.axis_index("sec"), lax.axis_index("mpo")
    terms, sectors, width, _ = left_operators.shape
    blocks = wavefunction.shape[0]
    rows, half = width // parties, width // 2
    smem = pl.BlockSpec(memory_space=pltpu.SMEM)
    vmem = pl.BlockSpec(memory_space=pltpu.VMEM)
    anywhere = pl.BlockSpec(memory_space=pl.ANY)
    params = pltpu.CompilerParams(vmem_limit_bytes=VMEM_LIMIT)

    def to_party(value, j):
        return lax.ppermute(value, "mpo", [(d, (d + j) % parties) for d in range(parties)])

    def left_products(operators):
        return pl.pallas_call(
            functools.partial(left_kernel, parties=parties),
            out_shape=jax.ShapeDtypeStruct((blocks, width, terms * width), jnp.bfloat16),
            in_specs=[smem, vmem, vmem],
            out_specs=vmem,
            compiler_params=params,
            cost_estimate=pl.CostEstimate(
                flops=2 * blocks * terms * width**3, bytes_accessed=9 * 2**20, transcendentals=0
            ),
            name="left_products",
        )(left_index, operators, wavefunction)

    def right_products(columns, lefts, pieces, table):
        pack = width // columns
        piece_terms = pieces[0].shape[0]
        index = jnp.concatenate([jnp.asarray(table)[me], right_sector])
        partial = pl.pallas_call(
            functools.partial(
                right_kernel, lefts=len(lefts), pieces=len(pieces), parties=parties
            ),
            out_shape=[jax.ShapeDtypeStruct((blocks // pack, rows, width), jnp.bfloat16)] * parties,
            in_specs=[smem] + [vmem] * len(lefts) + [anywhere] * len(pieces),
            out_specs=[vmem] * parties,
            scratch_shapes=[
                pltpu.VMEM((piece_terms, owners * sectors, columns, width), jnp.bfloat16),
                pltpu.SemaphoreType.DMA((len(pieces),)),
            ],
            compiler_params=params,
            cost_estimate=pl.CostEstimate(
                flops=2 * blocks * piece_terms * width**2 * columns,
                bytes_accessed=12 * 2**20,
                transcendentals=0,
            ),
            name="right_products",
        )(index, *lefts, *pieces)
        return [partial[0]] + [to_party(partial[j], j) for j in range(1, parties)], partial

    mask = term_mask.astype(left_operators.dtype)[:, :, None, None]
    masked = left_operators * mask
    left_index = jnp.concatenate([own[None], left_sector - me * sectors]).astype(jnp.int32)
    first = right_operators[:, :, :half, :]
    if parties == 2 and owners <= RING_LIMIT and owners % 2 == 0:
        quarter = half // 2
        others_masked = to_party(masked, 1)
        for_other = lax.dynamic_slice_in_dim(right_operators, half + quarter * (1 - own), quarter, 2)
        for_own = lax.dynamic_slice_in_dim(right_operators, half + quarter * own, quarter, 2)
        second = jnp.concatenate([for_own, to_party(for_other, 1)], axis=0)
        rings = [RingGather(first, owners), RingGather(second, owners)]
        lefts = [left_products(masked), left_products(others_masked)]
        layout = ((half, False), (quarter, True))

        def finish(number, pieces, table, others):
            if others:
                pieces = lax.optimization_barrier((*pieces, *others))[: len(pieces)]
            return right_products(layout[number][0], lefts[: number + 1], pieces, table)

        kept = follow_plan(rings, {"La": lefts[:1], "Lb": lefts[1:]}, finish)
    else:
        lefts = [left_products(masked)]
        layout = ((half, False), (width - half, False))
        kept = []
        for part in (first, right_operators[:, :, half:, :]):
            whole = lax.all_gather(part, "sec", axis=1, tiled=True)
            kept += right_products(part.shape[2], lefts, [whole], np.zeros((owners, 1), np.int32))[0]

    return pl.pallas_call(
        functools.partial(join_kernel, layout=layout, parties=parties),
        out_shape=jax.ShapeDtypeStruct((blocks, rows, width), jnp.bfloat16),
        in_specs=[smem] + [vmem] * len(kept),
        out_specs=vmem,
        compiler_params=params,
        cost_estimate=pl.CostEstimate(flops=0, bytes_accessed=4 * 2**20, transcendentals=0),
        name="join_columns",
    )(own[None].astype(jnp.int32), *kept)


def solution(mesh):
    placed = (
        P("sec", None, None),
        P("sec"),
        P("sec"),
        P("mpo", "sec"),
        P("mpo", "sec", None, None),
        P("mpo", "sec", None, None),
    )
    return jax.shard_map(
        on_device, mesh=mesh, in_specs=placed, out_specs=P("sec", "mpo", None), check_vma=False
    )
```

time: 114 us -> 96.1 us (0.84)
  waiting for transfers between devices: 49.9 us -> 27.2 us
  Pallas kernels: 24.2 us -> 18.4 us
  starting transfers between devices: 23.1 us -> 28.6 us
  other arithmetic: 0.07 us -> 3.63 us
  local copies, waits for them, and re-layouts: 16.3 us -> 17.6 us
    ppermute x32 -> x34, waiting for transfers between devices: 49.9 us -> 27.2 us  [the longest x14 14.2 us: step_round(): return lax.ppermute(value, 'sec', pairs)]
    pallas_call x4 -> x5, Pallas kernels: 24.2 us -> 18.4 us  [the longest x2 9.51 us: right_products(): pl.pallas_call(functools.partial(right_kernel, lefts=len(lefts), pieces=l...]
    ppermute x32 -> x34, starting transfers between devices: 23.1 us -> 28.6 us  [the longest x14 19.3 us: step_round(): return lax.ppermute(value, 'sec', pairs)]
    dynamic_slice x0 -> x1, local copies, waits for them, and re-layouts: none -> 1.68 us  [on_device(): lax.dynamic_slice_in_dim(right_operators, half + quarter * own, quarter, 2)]
    mul x0 -> x1, other arithmetic: none -> 1.2 us  [on_device(): masked = left_operators * mask]
    unnamed x66 -> x30, local copies, waits for them, and re-layouts: 14.5 us -> 13.3 us
  transfers between devices with their start and end apart: 32 -> 34, of which waited for: 13 -> 10; matrix products, arithmetic and copies ran while one was open for 1% -> 6% of each run, Pallas kernels for 19% -> 12%
where the time goes in v2:
time: 96.1 us; the launch traced here: 95.5 us
  starting transfers between devices  28.6 us (30%)
  waiting for transfers between devices  27.2 us (28%)
  Pallas kernels  18.4 us (19%)
  local copies, waits for them, and re-layouts  17.6 us (18%)
  other arithmetic  3.63 us (4%)
    ppermute x14, starting transfers between devices, step_round(): return lax.ppermute(value, 'sec', pairs)  19.3 us
    ppermute x14, waiting for transfers between devices, step_round(): return lax.ppermute(value, 'sec', pairs)  14.2 us
    unnamed x30, local copies, waits for them, and re-layouts  13.3 us
    ppermute x4, waiting for transfers between devices, to_party(): lax.ppermute(value, 'mpo', [(d, (d + j) % parties) for d in range(parties)])  12.7 us
    pallas_call x2, Pallas kernels, right_products(): pl.pallas_call(functools.partial(right_kernel, lefts=len(lefts), pieces=l...  9.51 us
    pallas_call x2, Pallas kernels, left_products(): pl.pallas_call(functools.partial(left_kernel, parties=parties), out_shape...  6.76 us
    ppermute x4, starting transfers between devices, to_party(): lax.ppermute(value, 'mpo', [(d, (d + j) % parties) for d in range(parties)])  5.19 us
    ppermute x16, starting transfers between devices, swap_cores(): return lax.ppermute(value, 'sec', [(d, d ^ 1) for d in range(owners)])  4.07 us
  transfers between devices with their start and end apart: 34, of which 10 were waited for; matrix products, arithmetic and copies ran while one was open for 6% of the time, Pallas kernels for 12%

profile of v2, /device:TPU:0, one launch (start us, length us, event | category | flops | bytes accessed | tf_op | source)
XLA Modules:
  0.0 95.5 jit_solution(16172690633960696122)
XLA Ops:
  0.0 1.9 %slice.3.refs_1_ = bf16[2,10,64,128]{3,2,1,0:T(8,128)(2,1)} slice(bf16[2,10,128,128]{3,2,1,0:T(8,128)(2,1)} %param.13), slice={[0:2], [0:10], [0:64], [0:128]} | slice | bytes 655360 | tf_op jit(solution)/shard_map/slice | solution.py:253
  2.3 2.6 %collective-permute-start.1 = (bf16[2,10,64,128]{3,2,1,0:T(8,128)(2,1)}, bf16[2,10,64,128]{3,2,1,0:T(8,128)(2,1)}, u32[]{:S(2)}, u32[]{:S(2)}) collective-permute-start(bf16[2,10,64,128]{3,2,1,0:T(8,128)(2,1)} %slice.3.refs_1_), channel_id=1, source_target_pairs={{0,8},{2,6},{4,0},{6,14},{8,16},{10,2},{12,4},{14,22},{16,24},{18,... | collective-permute-start | bytes 983048 | tf_op jit(solution)/shard_map/ppermute | solution.py:33
  4.9 0.7 convert_element_type.3
  5.6 1.6 %collective-permute-start.3 = (bf16[2,10,64,128]{3,2,1,0:T(8,128)(2,1)}, bf16[2,10,64,128]{3,2,1,0:T(8,128)(2,1)}, u32[]{:S(2)}, u32[]{:S(2)}) collective-permute-start(bf16[2,10,64,128]{3,2,1,0:T(8,128)(2,1)} %collective-permute-done.refs_2_), channel_id=1, source_target_pairs={{0,8},{2,6},{4,0},{6,14},{8,16},{10,2},{12,4},{14,22},{16,24},{18,... | collective-permute-start | bytes 983048 | tf_op jit(solution)/shard_map/ppermute | solution.py:33
  7.2 1.2 %broadcast_multiply_fusion.operator_ref = bf16[2,10,128,128]{3,2,1,0:T(8,128)(2,1)S(1)} fusion(bf16[2,10,128,128]{3,2,1,0:T(8,128)(2,1)} %param.12, bf16[2,10]{1,0:T(2,128)(2,1)S(1)} %convert_element_type.3), kind=kLoop, calls=%fused_computation.1 | loop fusion | flops 327680 | bytes 1310760 | tf_op jit(solution)/shard_map/mul | solution.py:251
  8.4 1.6 %collective-permute-start.13 = (bf16[2,10,128,128]{3,2,1,0:T(8,128)(2,1)S(1)}, bf16[2,10,128,128]{3,2,1,0:T(8,128)(2,1)}, u32[]{:S(2)}, u32[]{:S(2)}) collective-permute-start(bf16[2,10,128,128]{3,2,1,0:T(8,128)(2,1)S(1)} %broadcast_multiply_fusion.operator_ref), channel_id=1, source_target_pairs={{0,1},{1,0},{2,3},{3,2},{4,5},{5,4},{6,7},{7,6},{8,9},{9,8},{10,11... | collective-permute-start | bytes 1966088 | tf_op jit(solution)/shard_map/ppermute | solution.py:210
  10.0 1.7 %constant_dynamic-slice_fusion = (bf16[2,10,32,128]{3,2,1,0:T(8,128)(2,1)S(1)}, bf16[2,10,32,128]{3,2,1,0:T(8,128)(2,1)}) fusion(bf16[2,10,128,128]{3,2,1,0:T(8,128)(2,1)} %param.13, s32[]{:T(128)S(6)} %select_n.11, s32[]{:T(128)S(6)} %select_n.12), kind=kLoop, calls=%fused_computation.2 | loop fusion | bytes 655368 | tf_op jit(solution)/shard_map/dynamic_slice | solution.py:258
  12.1 1.6 %collective-permute-start.5 = (bf16[2,10,64,128]{3,2,1,0:T(8,128)(2,1)}, bf16[2,10,64,128]{3,2,1,0:T(8,128)(2,1)S(1)}, u32[]{:S(2)}, u32[]{:S(2)}) collective-permute-start(bf16[2,10,64,128]{3,2,1,0:T(8,128)(2,1)} %collective-permute-done.1.refs_3_), channel_id=1, source_target_pairs={{0,8},{2,6},{4,0},{6,14},{8,16},{10,2},{12,4},{14,22},{16,24},{18,... | collective-permute-start | bytes 983048 | tf_op jit(solution)/shard_map/ppermute | solution.py:33
  13.7 2.1 %collective-permute-start.7 = (bf16[2,10,64,128]{3,2,1,0:T(8,128)(2,1)}, bf16[2,10,64,128]{3,2,1,0:T(8,128)(2,1)}, u32[]{:S(2)}, u32[]{:S(2)}) collective-permute-start(bf16[2,10,64,128]{3,2,1,0:T(8,128)(2,1)} %collective-permute-done.3.refs_5_), channel_id=1, source_target_pairs={{0,8},{2,6},{4,0},{6,14},{8,16},{10,2},{12,4},{14,22},{16,24},{18,... | collective-permute-start | bytes 983048 | tf_op jit(solution)/shard_map/ppermute | solution.py:33
  15.8 0.7 broadcast_subtract_fusion
  16.5 1.7 %copy-done.4 = bf16[80,128,128]{2,1,0:T(8,128)(2,1)S(1)} copy-done((bf16[80,128,128]{2,1,0:T(8,128)(2,1)S(1)}, bf16[80,128,128]{2,1,0:T(8,128)(2,1)}, u32[]{:S(2)}) %copy-start.4) | copy-done | bytes 2621464
  18.3 3.1 %left_products.2.refs_0_ = bf16[80,128,256]{2,1,0:T(8,128)(2,1)S(1)} custom-call(s32[81]{0:T(128)S(1)} %pad_add_fusion.1.index_ref, bf16[2,10,128,128]{3,2,1,0:T(8,128)(2,1)S(1)} %broadcast_multiply_fusion.operator_ref, bf16[80,128,128]{2,1,0:T(8,128)(2,1)S(1)} %copy-done.4), custom_call_target="tpu_custom_call" | custom-call | flops 671088640 | bytes 9437184 | tf_op jit(solution)/shard_map/left_products/pallas_call | solution.py:213
  21.4 2.4 %copy-done = bf16[80,128,256]{2,1,0:T(8,128)(2,1)} copy-done((bf16[80,128,256]{2,1,0:T(8,128)(2,1)}, bf16[80,128,256]{2,1,0:T(8,128)(2,1)S(1)}, u32[]{:S(2)}) %copy-start) | copy-done | bytes 5242904
  23.8 1.6 %collective-permute-start.9 = (bf16[2,10,64,128]{3,2,1,0:T(8,128)(2,1)S(1)}, bf16[2,10,64,128]{3,2,1,0:T(8,128)(2,1)S(1)}, u32[]{:S(2)}, u32[]{:S(2)}) collective-permute-start(bf16[2,10,64,128]{3,2,1,0:T(8,128)(2,1)S(1)} %collective-permute-done.5.refs_7_), channel_id=1, source_target_pairs={{0,8},{2,6},{4,0},{6,14},{8,16},{10,2},{12,4},{14,22},{16,24},{18,... | collective-permute-start | bytes 983048 | tf_op jit(solution)/shard_map/ppermute | solution.py:33
  25.4 3.2 %collective-permute-done.17 = bf16[2,10,32,128]{3,2,1,0:T(8,128)(2,1)} collective-permute-done((bf16[2,10,32,128]{3,2,1,0:T(8,128)(2,1)}, bf16[2,10,32,128]{3,2,1,0:T(8,128)(2,1)}, u32[]{:S(2)}, u32[]{:S(2)}) %collective-permute-start.17) | collective-permute-done | bytes 163872 | tf_op jit(solution)/shard_map/ppermute | solution.py:210
  28.5 0.9 pad_maximum_fusion.refs_2_
  30.1 1.2 %collective-permute-start.2 = (bf16[2,10,64,128]{3,2,1,0:T(8,128)(2,1)}, bf16[2,10,64,128]{3,2,1,0:T(8,128)(2,1)S(1)}, u32[]{:S(2)}, u32[]{:S(2)}) collective-permute-start(bf16[2,10,64,128]{3,2,1,0:T(8,128)(2,1)} %collective-permute-done.1.refs_3_), channel_id=1, source_target_pairs={{0,2},{2,0},{4,6},{6,4},{8,10},{10,8},{12,14},{14,12},{16,18},{18,... | collective-permute-start | bytes 983048 | tf_op jit(solution)/shard_map/ppermute | solution.py:25
  31.4 3.6 %left_products.3.refs_1_ = bf16[80,128,256]{2,1,0:T(8,128)(2,1)S(1)} custom-call(s32[81]{0:T(128)S(1)} %pad_add_fusion.1.index_ref, bf16[2,10,128,128]{3,2,1,0:T(8,128)(2,1)} %collective-permute-done.13.operator_ref, bf16[80,128,128]{2,1,0:T(8,128)(2,1)S(1)} %copy-done.5), custom_call_target="tpu_custom_call" | custom-call | flops 671088640 | bytes 9437184 | tf_op jit(solution)/shard_map/left_products/pallas_call | solution.py:213
  35.0 2.3 %copy-done.2 = bf16[80,128,256]{2,1,0:T(8,128)(2,1)} copy-done((bf16[80,128,256]{2,1,0:T(8,128)(2,1)}, bf16[80,128,256]{2,1,0:T(8,128)(2,1)S(1)}, u32[]{:S(2)}) %copy-start.2) | copy-done | bytes 5242904
  37.9 0.6 collective-permute-start.4
  38.6 0.7 copy-done.10
  39.3 0.7 copy-done.12
  40.0 1.4 %collective-permute-start.19 = (bf16[4,10,32,128]{3,2,1,0:T(8,128)(2,1)S(1)}, bf16[4,10,32,128]{3,2,1,0:T(8,128)(2,1)S(1)}, u32[]{:S(2)}, u32[]{:S(2)}) collective-permute-start(bf16[4,10,32,128]{3,2,1,0:T(8,128)(2,1)S(1)} %pad_maximum_fusion.refs_2_), channel_id=1, source_target_pairs={{0,8},{2,6},{4,0},{6,14},{8,16},{10,2},{12,4},{14,22},{16,24},{18,... | collective-permute-start | bytes 983048 | tf_op jit(solution)/shard_map/ppermute | solution.py:33
  41.5 0.6 collective-permute-start.8
  42.1 2.4 %collective-permute-done.14.refs_15_ = bf16[2,10,64,128]{3,2,1,0:T(8,128)(2,1)S(1)} collective-permute-done((bf16[2,10,64,128]{3,2,1,0:T(8,128)(2,1)S(1)}, bf16[2,10,64,128]{3,2,1,0:T(8,128)(2,1)S(1)}, u32[]{:S(2)}, u32[]{:S(2)}) %collective-permute-start.14) | collective-permute-done | bytes 327712 | tf_op jit(solution)/shard_map/ppermute | solution.py:33
  45.0 0.5 collective-permute-start.21
  45.5 2.5 %collective-permute-done.19.refs_4_ = bf16[4,10,32,128]{3,2,1,0:T(8,128)(2,1)S(1)} collective-permute-done((bf16[4,10,32,128]{3,2,1,0:T(8,128)(2,1)S(1)}, bf16[4,10,32,128]{3,2,1,0:T(8,128)(2,1)S(1)}, u32[]{:S(2)}, u32[]{:S(2)}) %collective-permute-start.19) | collective-permute-done | bytes 327712 | tf_op jit(solution)/shard_map/ppermute | solution.py:33
  48.0 0.6 collective-permute-start.23
  48.5 0.7 fusion
  49.3 2.5 %copy-done.1 = bf16[80,128,256]{2,1,0:T(8,128)(2,1)S(1)} copy-done((bf16[80,128,256]{2,1,0:T(8,128)(2,1)S(1)}, bf16[80,128,256]{2,1,0:T(8,128)(2,1)}, u32[]{:S(2)}) %copy-start.1) | copy-done | bytes 5242904
  51.8 1.0 %copy-done.9 = bf16[2,10,64,128]{3,2,1,0:T(8,128)(2,1)S(1)} copy-done((bf16[2,10,64,128]{3,2,1,0:T(8,128)(2,1)S(1)}, bf16[2,10,64,128]{3,2,1,0:T(8,128)(2,1)}, u32[]{:S(2)}) %copy-start.9) | copy-done | bytes 327704
  52.8 1.0 %copy-done.11 = bf16[2,10,64,128]{3,2,1,0:T(8,128)(2,1)S(1)} copy-done((bf16[2,10,64,128]{3,2,1,0:T(8,128)(2,1)S(1)}, bf16[2,10,64,128]{3,2,1,0:T(8,128)(2,1)}, u32[]{:S(2)}) %copy-start.11) | copy-done | bytes 327704
  53.8 1.0 %copy-done.13 = bf16[2,10,64,128]{3,2,1,0:T(8,128)(2,1)S(1)} copy-done((bf16[2,10,64,128]{3,2,1,0:T(8,128)(2,1)S(1)}, bf16[2,10,64,128]{3,2,1,0:T(8,128)(2,1)}, u32[]{:S(2)}) %copy-start.13) | copy-done | bytes 327704
  54.7 4.7 %right_products.2 = (bf16[40,64,128]{2,1,0:T(8,128)(2,1)S(1)}, bf16[40,64,128]{2,1,0:T(8,128)(2,1)S(1)}) custom-call(s32[96]{0:T(128)S(1)} %pad_add_fusion.index_ref, bf16[80,128,256]{2,1,0:T(8,128)(2,1)S(1)} %copy-done.1, bf16[2,10,64,128]{3,2,1,0:T(8,128)(2,1)} %slice.3.refs_1_, bf16[2,10,64,128]{3,2,1,0:T(8,128)(2,1)} %collective-permute-done.refs_2_, ...), custom_call_target="tpu_custom_call" | custom-call | flops 335544320 | bytes 12582912 | tf_op jit(solution)/shard_map/right_products/pallas_call | solution.py:229
  59.4 1.6 %collective-permute-start.25 = (bf16[4,10,32,128]{3,2,1,0:T(8,128)(2,1)S(1)}, bf16[4,10,32,128]{3,2,1,0:T(8,128)(2,1)S(1)}, u32[]{:S(2)}, u32[]{:S(2)}) collective-permute-start(bf16[4,10,32,128]{3,2,1,0:T(8,128)(2,1)S(1)} %collective-permute-done.21.refs_6_), channel_id=1, source_target_pairs={{0,8},{2,6},{4,0},{6,14},{8,16},{10,2},{12,4},{14,22},{16,24},{18,... | collective-permute-start | bytes 983048 | tf_op jit(solution)/shard_map/ppermute | solution.py:33
  61.1 1.5 %collective-permute-start.27 = (bf16[4,10,32,128]{3,2,1,0:T(8,128)(2,1)S(1)}, bf16[4,10,32,128]{3,2,1,0:T(8,128)(2,1)S(1)}, u32[]{:S(2)}, u32[]{:S(2)}) collective-permute-start(bf16[4,10,32,128]{3,2,1,0:T(8,128)(2,1)S(1)} %collective-permute-done.23.refs_8_), channel_id=1, source_target_pairs={{0,8},{2,6},{4,0},{6,14},{8,16},{10,2},{12,4},{14,22},{16,24},{18,... | collective-permute-start | bytes 983048 | tf_op jit(solution)/shard_map/ppermute | solution.py:33
  62.6 1.5 %collective-permute-start.16 = (bf16[40,64,128]{2,1,0:T(8,128)(2,1)S(1)}, bf16[40,64,128]{2,1,0:T(8,128)(2,1)S(1)}, u32[]{:S(2)}, u32[]{:S(2)}) collective-permute-start(bf16[40,64,128]{2,1,0:T(8,128)(2,1)S(1)} %get-tuple-element.33), channel_id=1, source_target_pairs={{0,1},{1,0},{2,3},{3,2},{4,5},{5,4},{6,7},{7,6},{8,9},{9,8},{10,11... | collective-permute-start | bytes 1966088 | tf_op jit(solution)/shard_map/ppermute | solution.py:210
  64.1 2.4 %collective-permute-done.25.refs_10_ = bf16[4,10,32,128]{3,2,1,0:T(8,128)(2,1)S(1)} collective-permute-done((bf16[4,10,32,128]{3,2,1,0:T(8,128)(2,1)S(1)}, bf16[4,10,32,128]{3,2,1,0:T(8,128)(2,1)S(1)}, u32[]{:S(2)}, u32[]{:S(2)}) %collective-permute-start.25) | collective-permute-done | bytes 327712 | tf_op jit(solution)/shard_map/ppermute | solution.py:33
  66.6 1.6 %collective-permute-start.29 = (bf16[4,10,32,128]{3,2,1,0:T(8,128)(2,1)S(1)}, bf16[4,10,32,128]{3,2,1,0:T(8,128)(2,1)S(1)}, u32[]{:S(2)}, u32[]{:S(2)}) collective-permute-start(bf16[4,10,32,128]{3,2,1,0:T(8,128)(2,1)S(1)} %collective-permute-done.25.refs_10_), channel_id=1, source_target_pairs={{0,8},{2,6},{4,0},{6,14},{8,16},{10,2},{12,4},{14,22},{16,24},{18,... | collective-permute-start | bytes 983048 | tf_op jit(solution)/shard_map/ppermute | solution.py:33
  68.1 1.9 %collective-permute-done.27.refs_12_ = bf16[4,10,32,128]{3,2,1,0:T(8,128)(2,1)S(1)} collective-permute-done((bf16[4,10,32,128]{3,2,1,0:T(8,128)(2,1)S(1)}, bf16[4,10,32,128]{3,2,1,0:T(8,128)(2,1)S(1)}, u32[]{:S(2)}, u32[]{:S(2)}) %collective-permute-start.27) | collective-permute-done | bytes 327712 | tf_op jit(solution)/shard_map/ppermute | solution.py:33
  70.1 1.6 %collective-permute-start.31 = (bf16[4,10,32,128]{3,2,1,0:T(8,128)(2,1)S(1)}, bf16[4,10,32,128]{3,2,1,0:T(8,128)(2,1)S(1)}, u32[]{:S(2)}, u32[]{:S(2)}) collective-permute-start(bf16[4,10,32,128]{3,2,1,0:T(8,128)(2,1)S(1)} %collective-permute-done.27.refs_12_), channel_id=1, source_target_pairs={{0,8},{2,6},{4,0},{6,14},{8,16},{10,2},{12,4},{14,22},{16,24},{18,... | collective-permute-start | bytes 983048 | tf_op jit(solution)/shard_map/ppermute | solution.py:33
  71.7 2.0 %collective-permute-done.29.refs_14_ = bf16[4,10,32,128]{3,2,1,0:T(8,128)(2,1)S(1)} collective-permute-done((bf16[4,10,32,128]{3,2,1,0:T(8,128)(2,1)S(1)}, bf16[4,10,32,128]{3,2,1,0:T(8,128)(2,1)S(1)}, u32[]{:S(2)}, u32[]{:S(2)}) %collective-permute-start.29) | collective-permute-done | bytes 327712 | tf_op jit(solution)/shard_map/ppermute | solution.py:33
  74.2 3.0 %collective-permute-done.31.refs_16_ = bf16[4,10,32,128]{3,2,1,0:T(8,128)(2,1)S(1)} collective-permute-done((bf16[4,10,32,128]{3,2,1,0:T(8,128)(2,1)S(1)}, bf16[4,10,32,128]{3,2,1,0:T(8,128)(2,1)S(1)}, u32[]{:S(2)}, u32[]{:S(2)}) %collective-permute-start.31) | collective-permute-done | bytes 327712 | tf_op jit(solution)/shard_map/ppermute | solution.py:33
  77.2 1.2 %collective-permute-done.16.refs_1_ = bf16[40,64,128]{2,1,0:T(8,128)(2,1)S(1)} collective-permute-done((bf16[40,64,128]{2,1,0:T(8,128)(2,1)S(1)}, bf16[40,64,128]{2,1,0:T(8,128)(2,1)S(1)}, u32[]{:S(2)}, u32[]{:S(2)}) %collective-permute-start.16) | collective-permute-done | bytes 655392 | tf_op jit(solution)/shard_map/ppermute | solution.py:210
  78.8 4.8 %right_products.3 = (bf16[20,64,128]{2,1,0:T(8,128)(2,1)S(1)}, bf16[20,64,128]{2,1,0:T(8,128)(2,1)S(1)}) custom-call(s32[96]{0:T(128)S(1)} %pad_add_fusion.index_ref, bf16[80,128,256]{2,1,0:T(8,128)(2,1)S(1)} %copy-done.1, bf16[80,128,256]{2,1,0:T(8,128)(2,1)S(1)} %copy-done.3, bf16[4,10,32,128]{3,2,1,0:T(8,128)(2,1)S(1)} %copy-done.7, ...), custom_call_target="tpu_custom_call" | custom-call | flops 335544320 | bytes 12582912 | tf_op jit(solution)/shard_map/right_products/pallas_call | solution.py:229
  83.6 1.6 %collective-permute-start.33 = (bf16[20,64,128]{2,1,0:T(8,128)(2,1)S(1)}, bf16[20,64,128]{2,1,0:T(8,128)(2,1)S(1)}, u32[]{:S(2)}, u32[]{:S(2)}) collective-permute-start(bf16[20,64,128]{2,1,0:T(8,128)(2,1)S(1)} %get-tuple-element.54), channel_id=1, source_target_pairs={{0,1},{1,0},{2,3},{3,2},{4,5},{5,4},{6,7},{7,6},{8,9},{9,8},{10,11... | collective-permute-start | bytes 983048 | tf_op jit(solution)/shard_map/ppermute | solution.py:210
  85.2 8.2 %collective-permute-done.33.refs_3_ = bf16[20,64,128]{2,1,0:T(8,128)(2,1)S(1)} collective-permute-done((bf16[20,64,128]{2,1,0:T(8,128)(2,1)S(1)}, bf16[20,64,128]{2,1,0:T(8,128)(2,1)S(1)}, u32[]{:S(2)}, u32[]{:S(2)}) %collective-permute-start.33) | collective-permute-done | bytes 327712 | tf_op jit(solution)/shard_map/ppermute | solution.py:210
  93.4 2.1 %join_columns.1 = bf16[80,64,128]{2,1,0:T(8,128)(2,1)} custom-call(s32[1]{0:T(128)} %bitcast.own_ref, bf16[40,64,128]{2,1,0:T(8,128)(2,1)S(1)} %get-tuple-element.32.refs_0_, bf16[40,64,128]{2,1,0:T(8,128)(2,1)S(1)} %collective-permute-done.16.refs_1_, bf16[20,64,128]{2,1,0:T(8,128)(2,1)S(1)} %get-tuple-element.53.refs_2_, ...), custom_call_target="tpu_custom_call" | custom-call | bytes 4194304 | tf_op jit(solution)/shard_map/join_columns/pallas_call | solution.py:278
  (64 shorter events, 3.8 us)
Async XLA Ops:
  0.0 31.4 %copy-start.5 = (bf16[80,128,128]{2,1,0:T(8,128)(2,1)S(1)}, bf16[80,128,128]{2,1,0:T(8,128)(2,1)}, u32[]{:S(2)}) copy-start(bf16[80,128,128]{2,1,0:T(8,128)(2,1)} %wave_ref.3) | copy-start | bytes 7864324
  1.9 3.7 %collective-permute-start = (bf16[2,10,64,128]{3,2,1,0:T(8,128)(2,1)}, bf16[2,10,64,128]{3,2,1,0:T(8,128)(2,1)}, u32[]{:S(2)}, u32[]{:S(2)}) collective-permute-start(bf16[2,10,64,128]{3,2,1,0:T(8,128)(2,1)} %slice.3.refs_1_), channel_id=1, source_target_pairs={{0,2},{2,0},{4,6},{6,4},{8,10},{10,8},{12,14},{14,12},{16,18},{18,... | collective-permute-start | bytes 983048 | tf_op jit(solution)/shard_map/ppermute | solution.py:25
  2.3 9.8 %collective-permute-start.1 = (bf16[2,10,64,128]{3,2,1,0:T(8,128)(2,1)}, bf16[2,10,64,128]{3,2,1,0:T(8,128)(2,1)}, u32[]{:S(2)}, u32[]{:S(2)}) collective-permute-start(bf16[2,10,64,128]{3,2,1,0:T(8,128)(2,1)} %slice.3.refs_1_), channel_id=1, source_target_pairs={{0,8},{2,6},{4,0},{6,14},{8,16},{10,2},{12,4},{14,22},{16,24},{18,... | collective-permute-start | bytes 983048 | tf_op jit(solution)/shard_map/ppermute | solution.py:33
  5.6 8.1 %collective-permute-start.3 = (bf16[2,10,64,128]{3,2,1,0:T(8,128)(2,1)}, bf16[2,10,64,128]{3,2,1,0:T(8,128)(2,1)}, u32[]{:S(2)}, u32[]{:S(2)}) collective-permute-start(bf16[2,10,64,128]{3,2,1,0:T(8,128)(2,1)} %collective-permute-done.refs_2_), channel_id=1, source_target_pairs={{0,8},{2,6},{4,0},{6,14},{8,16},{10,2},{12,4},{14,22},{16,24},{18,... | collective-permute-start | bytes 983048 | tf_op jit(solution)/shard_map/ppermute | solution.py:33
  8.4 23.0 %collective-permute-start.13 = (bf16[2,10,128,128]{3,2,1,0:T(8,128)(2,1)S(1)}, bf16[2,10,128,128]{3,2,1,0:T(8,128)(2,1)}, u32[]{:S(2)}, u32[]{:S(2)}) collective-permute-start(bf16[2,10,128,128]{3,2,1,0:T(8,128)(2,1)S(1)} %broadcast_multiply_fusion.operator_ref), channel_id=1, source_target_pairs={{0,1},{1,0},{2,3},{3,2},{4,5},{5,4},{6,7},{7,6},{8,9},{9,8},{10,11... | collective-permute-start | bytes 1966088 | tf_op jit(solution)/shard_map/ppermute | solution.py:210
  11.6 16.9 %collective-permute-start.17 = (bf16[2,10,32,128]{3,2,1,0:T(8,128)(2,1)}, bf16[2,10,32,128]{3,2,1,0:T(8,128)(2,1)}, u32[]{:S(2)}, u32[]{:S(2)}) collective-permute-start(bf16[2,10,32,128]{3,2,1,0:T(8,128)(2,1)} %get-tuple-element.56), channel_id=1, source_target_pairs={{0,1},{1,0},{2,3},{3,2},{4,5},{5,4},{6,7},{7,6},{8,9},{9,8},{10,11... | collective-permute-start | bytes 491528 | tf_op jit(solution)/shard_map/ppermute | solution.py:210
  12.1 11.7 %collective-permute-start.5 = (bf16[2,10,64,128]{3,2,1,0:T(8,128)(2,1)}, bf16[2,10,64,128]{3,2,1,0:T(8,128)(2,1)S(1)}, u32[]{:S(2)}, u32[]{:S(2)}) collective-permute-start(bf16[2,10,64,128]{3,2,1,0:T(8,128)(2,1)} %collective-permute-done.1.refs_3_), channel_id=1, source_target_pairs={{0,8},{2,6},{4,0},{6,14},{8,16},{10,2},{12,4},{14,22},{16,24},{18,... | collective-permute-start | bytes 983048 | tf_op jit(solution)/shard_map/ppermute | solution.py:33
  13.7 15.9 %collective-permute-start.7 = (bf16[2,10,64,128]{3,2,1,0:T(8,128)(2,1)}, bf16[2,10,64,128]{3,2,1,0:T(8,128)(2,1)}, u32[]{:S(2)}, u32[]{:S(2)}) collective-permute-start(bf16[2,10,64,128]{3,2,1,0:T(8,128)(2,1)} %collective-permute-done.3.refs_5_), channel_id=1, source_target_pairs={{0,8},{2,6},{4,0},{6,14},{8,16},{10,2},{12,4},{14,22},{16,24},{18,... | collective-permute-start | bytes 983048 | tf_op jit(solution)/shard_map/ppermute | solution.py:33
  16.5 1.7 %copy-start.4 = (bf16[80,128,128]{2,1,0:T(8,128)(2,1)S(1)}, bf16[80,128,128]{2,1,0:T(8,128)(2,1)}, u32[]{:S(2)}) copy-start(bf16[80,128,128]{2,1,0:T(8,128)(2,1)} %wave_ref.3) | copy-start | bytes 7864324
  21.4 2.4 %copy-start = (bf16[80,128,256]{2,1,0:T(8,128)(2,1)}, bf16[80,128,256]{2,1,0:T(8,128)(2,1)S(1)}, u32[]{:S(2)}) copy-start(bf16[80,128,256]{2,1,0:T(8,128)(2,1)S(1)} %left_products.2.refs_0_) | copy-start | bytes 15728644
  23.8 25.4 %copy-start.14 = (s32[80]{0:T(128)S(1)}, s32[80]{0:T(128)}, u32[]{:S(2)}) copy-start(s32[80]{0:T(128)} %param.10) | copy-start | bytes 964
  23.8 24.2 %copy-start.8 = (bf16[2,10,64,128]{3,2,1,0:T(8,128)(2,1)}, bf16[2,10,64,128]{3,2,1,0:T(8,128)(2,1)S(1)}, u32[]{:S(2)}) copy-start(bf16[2,10,64,128]{3,2,1,0:T(8,128)(2,1)S(1)} %collective-permute-done.5.refs_7_) | copy-start | bytes 983044
  23.8 13.6 %collective-permute-start.9 = (bf16[2,10,64,128]{3,2,1,0:T(8,128)(2,1)S(1)}, bf16[2,10,64,128]{3,2,1,0:T(8,128)(2,1)S(1)}, u32[]{:S(2)}, u32[]{:S(2)}) collective-permute-start(bf16[2,10,64,128]{3,2,1,0:T(8,128)(2,1)S(1)} %collective-permute-done.5.refs_7_), channel_id=1, source_target_pairs={{0,8},{2,6},{4,0},{6,14},{8,16},{10,2},{12,4},{14,22},{16,24},{18,... | collective-permute-start | bytes 983048 | tf_op jit(solution)/shard_map/ppermute | solution.py:33
  29.5 9.8 %copy-start.6 = (bf16[4,10,32,128]{3,2,1,0:T(8,128)(2,1)}, bf16[4,10,32,128]{3,2,1,0:T(8,128)(2,1)S(1)}, u32[]{:S(2)}) copy-start(bf16[4,10,32,128]{3,2,1,0:T(8,128)(2,1)S(1)} %pad_maximum_fusion.refs_2_) | copy-start | bytes 983044
  29.5 8.4 %collective-permute-start.18 = (bf16[4,10,32,128]{3,2,1,0:T(8,128)(2,1)S(1)}, bf16[4,10,32,128]{3,2,1,0:T(8,128)(2,1)}, u32[]{:S(2)}, u32[]{:S(2)}) collective-permute-start(bf16[4,10,32,128]{3,2,1,0:T(8,128)(2,1)S(1)} %pad_maximum_fusion.refs_2_), channel_id=1, source_target_pairs={{0,2},{2,0},{4,6},{6,4},{8,10},{10,8},{12,14},{14,12},{16,18},{18,... | collective-permute-start | bytes 983048 | tf_op jit(solution)/shard_map/ppermute | solution.py:25
  29.6 8.9 %collective-permute-start.11 = (bf16[2,10,64,128]{3,2,1,0:T(8,128)(2,1)}, bf16[2,10,64,128]{3,2,1,0:T(8,128)(2,1)}, u32[]{:S(2)}, u32[]{:S(2)}) collective-permute-start(bf16[2,10,64,128]{3,2,1,0:T(8,128)(2,1)} %collective-permute-done.7.refs_9_), channel_id=1, source_target_pairs={{0,8},{2,6},{4,0},{6,14},{8,16},{10,2},{12,4},{14,22},{16,24},{18,... | collective-permute-start | bytes 983048 | tf_op jit(solution)/shard_map/ppermute | solution.py:33
  30.1 9.2 %collective-permute-start.2 = (bf16[2,10,64,128]{3,2,1,0:T(8,128)(2,1)}, bf16[2,10,64,128]{3,2,1,0:T(8,128)(2,1)S(1)}, u32[]{:S(2)}, u32[]{:S(2)}) collective-permute-start(bf16[2,10,64,128]{3,2,1,0:T(8,128)(2,1)} %collective-permute-done.1.refs_3_), channel_id=1, source_target_pairs={{0,2},{2,0},{4,6},{6,4},{8,10},{10,8},{12,14},{14,12},{16,18},{18,... | collective-permute-start | bytes 983048 | tf_op jit(solution)/shard_map/ppermute | solution.py:25
  31.3 10.1 %collective-permute-start.6 = (bf16[2,10,64,128]{3,2,1,0:T(8,128)(2,1)S(1)}, bf16[2,10,64,128]{3,2,1,0:T(8,128)(2,1)S(1)}, u32[]{:S(2)}, u32[]{:S(2)}) collective-permute-start(bf16[2,10,64,128]{3,2,1,0:T(8,128)(2,1)S(1)} %collective-permute-done.5.refs_7_), channel_id=1, source_target_pairs={{0,2},{2,0},{4,6},{6,4},{8,10},{10,8},{12,14},{14,12},{16,18},{18,... | collective-permute-start | bytes 983048 | tf_op jit(solution)/shard_map/ppermute | solution.py:25
  35.0 2.4 %copy-start.2 = (bf16[80,128,256]{2,1,0:T(8,128)(2,1)}, bf16[80,128,256]{2,1,0:T(8,128)(2,1)S(1)}, u32[]{:S(2)}) copy-start(bf16[80,128,256]{2,1,0:T(8,128)(2,1)S(1)} %left_products.3.refs_1_) | copy-start | bytes 15728644
  37.4 7.1 %collective-permute-start.14 = (bf16[2,10,64,128]{3,2,1,0:T(8,128)(2,1)S(1)}, bf16[2,10,64,128]{3,2,1,0:T(8,128)(2,1)S(1)}, u32[]{:S(2)}, u32[]{:S(2)}) collective-permute-start(bf16[2,10,64,128]{3,2,1,0:T(8,128)(2,1)S(1)} %collective-permute-done.9.refs_11_), channel_id=1, source_target_pairs={{0,8},{2,6},{4,0},{6,14},{8,16},{10,2},{12,4},{14,22},{16,24},{18,... | collective-permute-start | bytes 983048 | tf_op jit(solution)/shard_map/ppermute | solution.py:33
  37.9 6.5 %collective-permute-start.4 = (bf16[2,10,64,128]{3,2,1,0:T(8,128)(2,1)}, bf16[2,10,64,128]{3,2,1,0:T(8,128)(2,1)S(1)}, u32[]{:S(2)}, u32[]{:S(2)}) collective-permute-start(bf16[2,10,64,128]{3,2,1,0:T(8,128)(2,1)} %collective-permute-done.3.refs_5_), channel_id=1, source_target_pairs={{0,2},{2,0},{4,6},{6,4},{8,10},{10,8},{12,14},{14,12},{16,18},{18,... | collective-permute-start | bytes 983048 | tf_op jit(solution)/shard_map/ppermute | solution.py:25
  38.5 6.5 %collective-permute-start.10 = (bf16[2,10,64,128]{3,2,1,0:T(8,128)(2,1)S(1)}, bf16[2,10,64,128]{3,2,1,0:T(8,128)(2,1)S(1)}, u32[]{:S(2)}, u32[]{:S(2)}) collective-permute-start(bf16[2,10,64,128]{3,2,1,0:T(8,128)(2,1)S(1)} %collective-permute-done.9.refs_11_), channel_id=1, source_target_pairs={{0,2},{2,0},{4,6},{6,4},{8,10},{10,8},{12,14},{14,12},{16,18},{18,... | collective-permute-start | bytes 983048 | tf_op jit(solution)/shard_map/ppermute | solution.py:25
  39.3 0.7 copy-start.12
  40.0 7.9 %collective-permute-start.19 = (bf16[4,10,32,128]{3,2,1,0:T(8,128)(2,1)S(1)}, bf16[4,10,32,128]{3,2,1,0:T(8,128)(2,1)S(1)}, u32[]{:S(2)}, u32[]{:S(2)}) collective-permute-start(bf16[4,10,32,128]{3,2,1,0:T(8,128)(2,1)S(1)} %pad_maximum_fusion.refs_2_), channel_id=1, source_target_pairs={{0,8},{2,6},{4,0},{6,14},{8,16},{10,2},{12,4},{14,22},{16,24},{18,... | collective-permute-start | bytes 983048 | tf_op jit(solution)/shard_map/ppermute | solution.py:33
  41.5 7.8 %collective-permute-start.8 = (bf16[2,10,64,128]{3,2,1,0:T(8,128)(2,1)}, bf16[2,10,64,128]{3,2,1,0:T(8,128)(2,1)S(1)}, u32[]{:S(2)}, u32[]{:S(2)}) collective-permute-start(bf16[2,10,64,128]{3,2,1,0:T(8,128)(2,1)} %collective-permute-done.7.refs_9_), channel_id=1, source_target_pairs={{0,2},{2,0},{4,6},{6,4},{8,10},{10,8},{12,14},{14,12},{16,18},{18,... | collective-permute-start | bytes 983048 | tf_op jit(solution)/shard_map/ppermute | solution.py:25
  44.4 4.9 %collective-permute-start.15 = (bf16[2,10,64,128]{3,2,1,0:T(8,128)(2,1)S(1)}, bf16[2,10,64,128]{3,2,1,0:T(8,128)(2,1)S(1)}, u32[]{:S(2)}, u32[]{:S(2)}) collective-permute-start(bf16[2,10,64,128]{3,2,1,0:T(8,128)(2,1)S(1)} %collective-permute-done.14.refs_15_), channel_id=1, source_target_pairs={{0,2},{2,0},{4,6},{6,4},{8,10},{10,8},{12,14},{14,12},{16,18},{18,... | collective-permute-start | bytes 983048 | tf_op jit(solution)/shard_map/ppermute | solution.py:25
  44.4 4.9 %collective-permute-start.12 = (bf16[2,10,64,128]{3,2,1,0:T(8,128)(2,1)}, bf16[2,10,64,128]{3,2,1,0:T(8,128)(2,1)S(1)}, u32[]{:S(2)}, u32[]{:S(2)}) collective-permute-start(bf16[2,10,64,128]{3,2,1,0:T(8,128)(2,1)} %collective-permute-done.11.refs_13_), channel_id=1, source_target_pairs={{0,2},{2,0},{4,6},{6,4},{8,10},{10,8},{12,14},{14,12},{16,18},{18,... | collective-permute-start | bytes 983048 | tf_op jit(solution)/shard_map/ppermute | solution.py:25
  45.0 14.5 %collective-permute-start.21 = (bf16[4,10,32,128]{3,2,1,0:T(8,128)(2,1)}, bf16[4,10,32,128]{3,2,1,0:T(8,128)(2,1)S(1)}, u32[]{:S(2)}, u32[]{:S(2)}) collective-permute-start(bf16[4,10,32,128]{3,2,1,0:T(8,128)(2,1)} %collective-permute-done.18.refs_3_), channel_id=1, source_target_pairs={{0,8},{2,6},{4,0},{6,14},{8,16},{10,2},{12,4},{14,22},{16,24},{18,... | collective-permute-start | bytes 983048 | tf_op jit(solution)/shard_map/ppermute | solution.py:33
  48.0 13.1 %collective-permute-start.23 = (bf16[4,10,32,128]{3,2,1,0:T(8,128)(2,1)S(1)}, bf16[4,10,32,128]{3,2,1,0:T(8,128)(2,1)S(1)}, u32[]{:S(2)}, u32[]{:S(2)}) collective-permute-start(bf16[4,10,32,128]{3,2,1,0:T(8,128)(2,1)S(1)} %collective-permute-done.19.refs_4_), channel_id=1, source_target_pairs={{0,8},{2,6},{4,0},{6,14},{8,16},{10,2},{12,4},{14,22},{16,24},{18,... | collective-permute-start | bytes 983048 | tf_op jit(solution)/shard_map/ppermute | solution.py:33
  49.3 2.5 %copy-start.1 = (bf16[80,128,256]{2,1,0:T(8,128)(2,1)S(1)}, bf16[80,128,256]{2,1,0:T(8,128)(2,1)}, u32[]{:S(2)}) copy-start(bf16[80,128,256]{2,1,0:T(8,128)(2,1)} %copy-done) | copy-start | bytes 15728644
  51.8 1.0 %copy-start.9 = (bf16[2,10,64,128]{3,2,1,0:T(8,128)(2,1)S(1)}, bf16[2,10,64,128]{3,2,1,0:T(8,128)(2,1)}, u32[]{:S(2)}) copy-start(bf16[2,10,64,128]{3,2,1,0:T(8,128)(2,1)} %copy-done.8) | copy-start | bytes 983044
  52.8 1.0 %copy-start.11 = (bf16[2,10,64,128]{3,2,1,0:T(8,128)(2,1)S(1)}, bf16[2,10,64,128]{3,2,1,0:T(8,128)(2,1)}, u32[]{:S(2)}) copy-start(bf16[2,10,64,128]{3,2,1,0:T(8,128)(2,1)} %copy-done.10) | copy-start | bytes 983044
  53.8 1.0 %copy-start.13 = (bf16[2,10,64,128]{3,2,1,0:T(8,128)(2,1)S(1)}, bf16[2,10,64,128]{3,2,1,0:T(8,128)(2,1)}, u32[]{:S(2)}) copy-start(bf16[2,10,64,128]{3,2,1,0:T(8,128)(2,1)} %copy-done.12) | copy-start | bytes 983044
  54.7 24.1 %copy-start.3 = (bf16[80,128,256]{2,1,0:T(8,128)(2,1)S(1)}, bf16[80,128,256]{2,1,0:T(8,128)(2,1)}, u32[]{:S(2)}) copy-start(bf16[80,128,256]{2,1,0:T(8,128)(2,1)} %copy-done.2) | copy-start | bytes 15728644
  54.7 24.1 %copy-start.7 = (bf16[4,10,32,128]{3,2,1,0:T(8,128)(2,1)S(1)}, bf16[4,10,32,128]{3,2,1,0:T(8,128)(2,1)}, u32[]{:S(2)}) copy-start(bf16[4,10,32,128]{3,2,1,0:T(8,128)(2,1)} %copy-done.6) | copy-start | bytes 983044
  59.4 7.1 %collective-permute-start.25 = (bf16[4,10,32,128]{3,2,1,0:T(8,128)(2,1)S(1)}, bf16[4,10,32,128]{3,2,1,0:T(8,128)(2,1)S(1)}, u32[]{:S(2)}, u32[]{:S(2)}) collective-permute-start(bf16[4,10,32,128]{3,2,1,0:T(8,128)(2,1)S(1)} %collective-permute-done.21.refs_6_), channel_id=1, source_target_pairs={{0,8},{2,6},{4,0},{6,14},{8,16},{10,2},{12,4},{14,22},{16,24},{18,... | collective-permute-start | bytes 983048 | tf_op jit(solution)/shard_map/ppermute | solution.py:33
  61.1 7.1 %collective-permute-start.22 = (bf16[4,10,32,128]{3,2,1,0:T(8,128)(2,1)S(1)}, bf16[4,10,32,128]{3,2,1,0:T(8,128)(2,1)S(1)}, u32[]{:S(2)}, u32[]{:S(2)}) collective-permute-start(bf16[4,10,32,128]{3,2,1,0:T(8,128)(2,1)S(1)} %collective-permute-done.21.refs_6_), channel_id=1, source_target_pairs={{0,2},{2,0},{4,6},{6,4},{8,10},{10,8},{12,14},{14,12},{16,18},{18,... | collective-permute-start | bytes 983048 | tf_op jit(solution)/shard_map/ppermute | solution.py:25
  61.1 9.0 %collective-permute-start.27 = (bf16[4,10,32,128]{3,2,1,0:T(8,128)(2,1)S(1)}, bf16[4,10,32,128]{3,2,1,0:T(8,128)(2,1)S(1)}, u32[]{:S(2)}, u32[]{:S(2)}) collective-permute-start(bf16[4,10,32,128]{3,2,1,0:T(8,128)(2,1)S(1)} %collective-permute-done.23.refs_8_), channel_id=1, source_target_pairs={{0,8},{2,6},{4,0},{6,14},{8,16},{10,2},{12,4},{14,22},{16,24},{18,... | collective-permute-start | bytes 983048 | tf_op jit(solution)/shard_map/ppermute | solution.py:33
  62.6 15.8 %collective-permute-start.16 = (bf16[40,64,128]{2,1,0:T(8,128)(2,1)S(1)}, bf16[40,64,128]{2,1,0:T(8,128)(2,1)S(1)}, u32[]{:S(2)}, u32[]{:S(2)}) collective-permute-start(bf16[40,64,128]{2,1,0:T(8,128)(2,1)S(1)} %get-tuple-element.33), channel_id=1, source_target_pairs={{0,1},{1,0},{2,3},{3,2},{4,5},{5,4},{6,7},{7,6},{8,9},{9,8},{10,11... | collective-permute-start | bytes 1966088 | tf_op jit(solution)/shard_map/ppermute | solution.py:210
  64.1 7.5 %collective-permute-start.20 = (bf16[4,10,32,128]{3,2,1,0:T(8,128)(2,1)S(1)}, bf16[4,10,32,128]{3,2,1,0:T(8,128)(2,1)S(1)}, u32[]{:S(2)}, u32[]{:S(2)}) collective-permute-start(bf16[4,10,32,128]{3,2,1,0:T(8,128)(2,1)S(1)} %collective-permute-done.19.refs_4_), channel_id=1, source_target_pairs={{0,2},{2,0},{4,6},{6,4},{8,10},{10,8},{12,14},{14,12},{16,18},{18,... | collective-permute-start | bytes 983048 | tf_op jit(solution)/shard_map/ppermute | solution.py:25
  66.6 7.1 %collective-permute-start.29 = (bf16[4,10,32,128]{3,2,1,0:T(8,128)(2,1)S(1)}, bf16[4,10,32,128]{3,2,1,0:T(8,128)(2,1)S(1)}, u32[]{:S(2)}, u32[]{:S(2)}) collective-permute-start(bf16[4,10,32,128]{3,2,1,0:T(8,128)(2,1)S(1)} %collective-permute-done.25.refs_10_), channel_id=1, source_target_pairs={{0,8},{2,6},{4,0},{6,14},{8,16},{10,2},{12,4},{14,22},{16,24},{18,... | collective-permute-start | bytes 983048 | tf_op jit(solution)/shard_map/ppermute | solution.py:33
  68.1 5.5 %collective-permute-start.26 = (bf16[4,10,32,128]{3,2,1,0:T(8,128)(2,1)S(1)}, bf16[4,10,32,128]{3,2,1,0:T(8,128)(2,1)S(1)}, u32[]{:S(2)}, u32[]{:S(2)}) collective-permute-start(bf16[4,10,32,128]{3,2,1,0:T(8,128)(2,1)S(1)} %collective-permute-done.25.refs_10_), channel_id=1, source_target_pairs={{0,2},{2,0},{4,6},{6,4},{8,10},{10,8},{12,14},{14,12},{16,18},{18,... | collective-permute-start | bytes 983048 | tf_op jit(solution)/shard_map/ppermute | solution.py:25
  70.1 7.1 %collective-permute-start.31 = (bf16[4,10,32,128]{3,2,1,0:T(8,128)(2,1)S(1)}, bf16[4,10,32,128]{3,2,1,0:T(8,128)(2,1)S(1)}, u32[]{:S(2)}, u32[]{:S(2)}) collective-permute-start(bf16[4,10,32,128]{3,2,1,0:T(8,128)(2,1)S(1)} %collective-permute-done.27.refs_12_), channel_id=1, source_target_pairs={{0,8},{2,6},{4,0},{6,14},{8,16},{10,2},{12,4},{14,22},{16,24},{18,... | collective-permute-start | bytes 983048 | tf_op jit(solution)/shard_map/ppermute | solution.py:33
  71.7 6.7 %collective-permute-start.24 = (bf16[4,10,32,128]{3,2,1,0:T(8,128)(2,1)S(1)}, bf16[4,10,32,128]{3,2,1,0:T(8,128)(2,1)S(1)}, u32[]{:S(2)}, u32[]{:S(2)}) collective-permute-start(bf16[4,10,32,128]{3,2,1,0:T(8,128)(2,1)S(1)} %collective-permute-done.23.refs_8_), channel_id=1, source_target_pairs={{0,2},{2,0},{4,6},{6,4},{8,10},{10,8},{12,14},{14,12},{16,18},{18,... | collective-permute-start | bytes 983048 | tf_op jit(solution)/shard_map/ppermute | solution.py:25
  73.6 4.8 %collective-permute-start.28 = (bf16[4,10,32,128]{3,2,1,0:T(8,128)(2,1)S(1)}, bf16[4,10,32,128]{3,2,1,0:T(8,128)(2,1)S(1)}, u32[]{:S(2)}, u32[]{:S(2)}) collective-permute-start(bf16[4,10,32,128]{3,2,1,0:T(8,128)(2,1)S(1)} %collective-permute-done.27.refs_12_), channel_id=1, source_target_pairs={{0,2},{2,0},{4,6},{6,4},{8,10},{10,8},{12,14},{14,12},{16,18},{18,... | collective-permute-start | bytes 983048 | tf_op jit(solution)/shard_map/ppermute | solution.py:25
  73.6 4.7 %collective-permute-start.30 = (bf16[4,10,32,128]{3,2,1,0:T(8,128)(2,1)S(1)}, bf16[4,10,32,128]{3,2,1,0:T(8,128)(2,1)S(1)}, u32[]{:S(2)}, u32[]{:S(2)}) collective-permute-start(bf16[4,10,32,128]{3,2,1,0:T(8,128)(2,1)S(1)} %collective-permute-done.29.refs_14_), channel_id=1, source_target_pairs={{0,2},{2,0},{4,6},{6,4},{8,10},{10,8},{12,14},{14,12},{16,18},{18,... | collective-permute-start | bytes 983048 | tf_op jit(solution)/shard_map/ppermute | solution.py:25
  77.2 1.6 %collective-permute-start.32 = (bf16[4,10,32,128]{3,2,1,0:T(8,128)(2,1)S(1)}, bf16[4,10,32,128]{3,2,1,0:T(8,128)(2,1)S(1)}, u32[]{:S(2)}, u32[]{:S(2)}) collective-permute-start(bf16[4,10,32,128]{3,2,1,0:T(8,128)(2,1)S(1)} %collective-permute-done.31.refs_16_), channel_id=1, source_target_pairs={{0,2},{2,0},{4,6},{6,4},{8,10},{10,8},{12,14},{14,12},{16,18},{18,... | collective-permute-start | bytes 983048 | tf_op jit(solution)/shard_map/ppermute | solution.py:25
  83.6 9.8 %collective-permute-start.33 = (bf16[20,64,128]{2,1,0:T(8,128)(2,1)S(1)}, bf16[20,64,128]{2,1,0:T(8,128)(2,1)S(1)}, u32[]{:S(2)}, u32[]{:S(2)}) collective-permute-start(bf16[20,64,128]{2,1,0:T(8,128)(2,1)S(1)} %get-tuple-element.54), channel_id=1, source_target_pairs={{0,1},{1,0},{2,3},{3,2},{4,5},{5,4},{6,7},{7,6},{8,9},{9,8},{10,11... | collective-permute-start | bytes 983048 | tf_op jit(solution)/shard_map/ppermute | solution.py:210
  (1 other events, 0.7 us)

commit v3 on v0

v3 whole, which is shorter than its diff:
```python
import functools

import jax
import jax.numpy as jnp
import numpy as np
from jax import lax
from jax.experimental import pallas as pl
from jax.experimental.pallas import tpu as pltpu
from jax.sharding import PartitionSpec as P

RING_LIMIT = 16
VMEM_LIMIT = 24 * 1024 * 1024
UNROLL = 10
LEFT_BANDS = 4
JOIN_BANDS = 4
STAGES = ((0, 1, 2), (3,), (4,))
APART = 2
WAITS = {"P2o": ("masked",), "P1x": ("P2o",), "Q1x": ("Q2o",), "Q2o": ("given",), "Q2x": ("other",), "Q3": ("left",), "P4": ("m0",), "m2": ("y0",)}


def in_hbm(value):
    return pltpu.with_memory_space_constraint(value, pltpu.HBM)


def after(value, *others):
    return lax.optimization_barrier((value, *others))[0] if others else value


def chip_ring(chips):
    across = 2 if chips % 2 == 0 else 1
    up = [z * across for z in range(chips // across)]
    down = [z * across + 1 for z in reversed(range(chips // across))] if across == 2 else []
    return up + down


def swap_cores(value, owners):
    return lax.ppermute(value, "sec", [(d, d ^ 1) for d in range(owners)])


def step_round(value, owners):
    order = chip_ring(owners // 2)
    following = {chip: order[(i + 1) % len(order)] for i, chip in enumerate(order)}
    before = {chip: order[i - 1] for i, chip in enumerate(order)}
    pairs = [(d, 2 * (before if d % 2 else following)[d // 2] + d % 2) for d in range(owners)]
    return lax.ppermute(value, "sec", pairs)


def ring_rounds(owners):
    chips = owners // 2
    return chips // 2, (chips - 1) // 2


def ring_sources(owners, rounds):
    chips = owners // 2
    order = chip_ring(chips)
    place = {chip: i for i, chip in enumerate(order)}
    found = np.zeros((owners, 0), np.int32)
    for number in rounds:
        for lane, last in enumerate(ring_rounds(owners)):
            if number > last or (number == 0 and lane):
                continue
            for swapped in range(2):
                column = []
                for d in range(owners):
                    source = d ^ swapped
                    way = 1 if source % 2 else -1
                    chip = order[(place[d // 2] + way * number) % chips]
                    column.append(2 * chip + (source % 2) ^ lane)
                found = np.concatenate([found, np.array(column, np.int32)[:, None]], axis=1)
    return found


def left_kernel(index_ref, *refs, parties, count, base):
    operator_refs, wave_ref = refs[:count], refs[count]
    out_refs = refs[count + 1 : 2 * count + 1]
    operators, waves, arrived = refs[2 * count + 1 :]
    _, terms, _, width, _ = operators.shape
    blocks = waves.shape[0]
    rows = width // parties
    own = index_ref[0]
    copies = [
        pltpu.make_async_copy(ref, operators.at[n], arrived.at[n])
        for n, ref in enumerate(operator_refs)
    ]
    bands = blocks // LEFT_BANDS if blocks % LEFT_BANDS == 0 else blocks
    for n in range(blocks // bands):
        there = pl.ds(n * bands, bands)
        copies.append(
            pltpu.make_async_copy(wave_ref.at[there], waves.at[there], arrived.at[count + n])
        )
    for copy in copies:
        copy.start()
    for copy in copies[:count]:
        copy.wait()

    def one_block(b, carry):
        local = index_ref[base + b]
        strips = [
            operators[
                n, k, local, pl.ds(pl.multiple_of(lax.rem(own + j, parties) * rows, rows), rows), :
            ]
            for n in range(count)
            for k in range(terms)
            for j in range(parties)
        ]
        product = jnp.dot(
            jnp.concatenate(strips, axis=0), waves[b], preferred_element_type=jnp.float32
        ).astype(jnp.bfloat16)
        for n, out_ref in enumerate(out_refs):
            for k in range(terms):
                start = (n * terms + k) * width
                out_ref[b, :, k * width : (k + 1) * width] = product[start : start + width]
        return carry

    for n, copy in enumerate(copies[count:]):
        copy.wait()
        lax.fori_loop(n * bands, (n + 1) * bands, one_block, 0, unroll=UNROLL)


def right_kernel(index_ref, *refs, lefts, spots, parties, stage, bases):
    pieces = len(spots)
    left_refs, piece_refs = refs[:lefts], refs[lefts : lefts + pieces]
    out_refs = refs[lefts + pieces : lefts + pieces + parties]
    held, listed, arrived = refs[lefts + pieces + parties :]
    terms, _, columns, width = held.shape
    blocks, height, _ = left_refs[0].shape
    rows, pack = height // parties, width // columns
    slots = out_refs[0].shape[0] * pack
    shift_base, stage_base, target_base, sector_base = bases

    copies = []
    for number, (piece, (term, slot)) in enumerate(zip(piece_refs, spots)):
        there = held.at[pl.ds(term, piece.shape[0]), pl.ds(slot, piece.shape[1])]
        copies.append(pltpu.make_async_copy(piece, there, arrived.at[number]))
    for copy in copies:
        copy.start()
    if stage is not None:

        def clear(i, carry):
            listed[i] = 0
            return carry

        def enlist(b, count):
            listed[count] = b
            hit = index_ref[stage_base + index_ref[target_base + b]] == stage
            return count + hit.astype(jnp.int32)

        lax.fori_loop(0, slots + 1, clear, 0, unroll=True)
        lax.fori_loop(0, blocks, enlist, jnp.int32(0), unroll=10)
    for copy in copies:
        copy.wait()
    lane = lax.broadcasted_iota(jnp.int32, (height, width), 1) // columns

    def one_group(g, carry):
        chosen = [g * pack + q for q in range(pack)]
        if stage is not None:
            chosen = [listed[i] for i in chosen]
        factors = []
        for b in chosen:
            sector = index_ref[sector_base + b] + index_ref[shift_base + index_ref[target_base + b]]
            factors.append(jnp.concatenate([held[k, sector] for k in range(terms)], axis=1))
        left = jnp.concatenate(
            [jnp.concatenate([ref[b] for b in chosen], axis=0) for ref in left_refs], axis=1
        )
        product = lax.dot_general(
            left,
            jnp.concatenate(factors, axis=0),
            (((1,), (1,)), ((), ())),
            preferred_element_type=jnp.float32,
        ).reshape(pack, height, width)
        value = product[0]
        for q in range(1, pack):
            value = jnp.where(lane == q, product[q], value)
        for j in range(parties):
            out_refs[j][g] = value[j * rows : (j + 1) * rows].astype(out_refs[j].dtype)
        return carry

    lax.fori_loop(0, slots // pack, one_group, 0, unroll=min(UNROLL, slots // pack))


def join_kernel(index_ref, *refs, stages, bases):
    own_refs, other_refs = refs[:stages], refs[stages : 2 * stages]
    out_ref, joined, sent = refs[2 * stages :]
    blocks, rows, width = joined.shape
    stage_base, target_base = bases
    own = index_ref[0]
    upper = lax.broadcasted_iota(jnp.int32, (rows, width), 1) // (width // 2)

    def pick(given, places, stage):
        value = given[0][places[0]]
        for s in range(1, stages):
            value = jnp.where(stage == s, given[s][places[s]], value)
        return value.astype(jnp.float32)

    def one_block(b, counts):
        stage = index_ref[stage_base + index_ref[target_base + b]]
        slot, places, grown = b, [lax.shift_right_logical(b, 1)], []
        for s in range(1, stages):
            hit = stage == s
            slot = jnp.where(hit, counts[s - 1], slot)
            last = own_refs[s].shape[0] - 1
            places.append(jnp.minimum(lax.shift_right_logical(counts[s - 1], 1), last))
            grown.append(counts[s - 1] + hit.astype(jnp.int32))
        side = lax.bitwise_and(slot, 1)
        here = side == own
        mine, given = pick(own_refs, places, stage), pick(other_refs, places, stage)
        moved = pltpu.roll(jnp.where(here, given, mine), width // 2, 1)
        kept = jnp.where(here, mine, given)
        joined[b] = jnp.where(upper == side, kept, moved).astype(joined.dtype)
        return tuple(grown)

    counts = (jnp.int32(0),) * (stages - 1)
    bands = blocks // JOIN_BANDS if blocks % JOIN_BANDS == 0 else blocks
    copies = []
    for n in range(blocks // bands):
        counts = lax.fori_loop(n * bands, (n + 1) * bands, one_block, counts, unroll=10)
        there = pl.ds(n * bands, bands)
        copies.append(pltpu.make_async_copy(joined.at[there], out_ref.at[there], sent.at[n]))
        copies[-1].start()
    for copy in copies:
        copy.wait()


def on_device(wavefunction, left_sector, right_sector, term_mask, left_operators, right_operators):
    owners, parties = lax.axis_size("sec"), lax.axis_size("mpo")
    me, own = lax.axis_index("sec"), lax.axis_index("mpo")
    terms, sectors, width, _ = left_operators.shape
    blocks = wavefunction.shape[0]
    rows = width // parties
    smem = pl.BlockSpec(memory_space=pltpu.SMEM)
    vmem = pl.BlockSpec(memory_space=pltpu.VMEM)
    anywhere = pl.BlockSpec(memory_space=pl.ANY)
    params = pltpu.CompilerParams(vmem_limit_bytes=VMEM_LIMIT)
    by_ring = parties == 2 and owners <= RING_LIMIT and owners % 4 == 0 and blocks % 2 == 0

    def to_party(value, j):
        return lax.ppermute(value, "mpo", [(d, (d + j) % parties) for d in range(parties)])

    lanes = ring_rounds(owners) if by_ring else (0, 0)
    stages = [tuple(r for r in rounds if r <= lanes[0]) for rounds in STAGES] if by_ring else [(0,)]
    stages = [rounds for rounds in stages if rounds]
    sources = [ring_sources(owners, rounds) for rounds in stages] if by_ring else []
    shifts = np.zeros((owners, len(stages), owners), np.int32)
    stage_of = np.zeros((owners, owners), np.int32)
    for s, found in enumerate(sources):
        for d in range(owners):
            shifts[d, s] = -sectors * np.arange(owners)
            for slot, owner in enumerate(found[d]):
                shifts[d, s, owner] = sectors * (slot - owner)
                stage_of[d, owner] = s
    table = np.concatenate([shifts.reshape(owners, -1), stage_of], axis=1)
    stage_base = 1 + len(stages) * owners
    target_base = stage_base + owners
    sector_base = target_base + blocks
    left_base = sector_base + blocks
    index = jnp.concatenate(
        [
            own[None],
            jnp.asarray(table)[me],
            right_sector // sectors,
            right_sector,
            left_sector - me * sectors,
        ]
    ).astype(jnp.int32)

    def left_products(operators):
        return pl.pallas_call(
            functools.partial(
                left_kernel, parties=parties, count=len(operators), base=left_base
            ),
            out_shape=[jax.ShapeDtypeStruct((blocks, width, terms * width), jnp.bfloat16)]
            * len(operators),
            in_specs=[smem] + [anywhere] * (len(operators) + 1),
            out_specs=[vmem] * len(operators),
            scratch_shapes=[
                pltpu.VMEM((len(operators), *operators[0].shape), jnp.bfloat16),
                pltpu.VMEM(wavefunction.shape, jnp.bfloat16),
                pltpu.SemaphoreType.DMA((len(operators) + LEFT_BANDS,)),
            ],
            compiler_params=params,
            cost_estimate=pl.CostEstimate(
                flops=2 * len(operators) * blocks * terms * width**3,
                bytes_accessed=9 * 2**20,
                transcendentals=0,
            ),
            name="left_products",
        )(index, *operators, in_hbm(wavefunction))

    def right_products(lefts, pieces, spots, stage, held, slots):
        pack = width // held[2]
        return pl.pallas_call(
            functools.partial(
                right_kernel,
                lefts=len(lefts),
                spots=spots,
                parties=parties,
                stage=stage or None,
                bases=(1 + (stage or 0) * owners, stage_base, target_base, sector_base),
            ),
            out_shape=[jax.ShapeDtypeStruct((slots // pack, rows, width), jnp.bfloat16)] * parties,
            in_specs=[smem] + [vmem] * len(lefts) + [anywhere] * len(pieces),
            out_specs=[vmem] * parties,
            scratch_shapes=[
                pltpu.VMEM(held, jnp.bfloat16),
                pltpu.SMEM((slots + 1,), jnp.int32),
                pltpu.SemaphoreType.DMA((len(pieces),)),
            ],
            compiler_params=params,
            cost_estimate=pl.CostEstimate(
                flops=2 * slots * held[0] * width**2 * held[2],
                bytes_accessed=12 * 2**20,
                transcendentals=0,
            ),
            name="right_products",
        )(index, *lefts, *pieces)

    mask = term_mask.astype(left_operators.dtype)[:, :, None, None]
    masked = left_operators * mask
    if not by_ring:
        lefts = left_products([masked])
        whole = lax.all_gather(right_operators, "sec", axis=1, tiled=True)
        shape = (terms, owners * sectors, width, width)
        partial = right_products(lefts, [whole], [(0, 0)], None, shape, blocks)
        total = partial[0].astype(jnp.float32)
        for j in range(1, parties):
            total = total + to_party(partial[j], j).astype(jnp.float32)
        return total.astype(jnp.bfloat16)

    columns = width // parties
    mine = lax.dynamic_slice_in_dim(right_operators, columns * own, columns, 2)
    theirs = lax.dynamic_slice_in_dim(right_operators, columns * (1 - own), columns, 2)
    given = to_party(theirs, 1)
    other = to_party(masked, 1)
    lefts = left_products([masked, other])
    done = {"given": [given], "other": [other], "left": lefts, "masked": [masked]}

    def launch(name, value):
        waits = [v for w in WAITS.get(name, ()) for v in done[w]]
        done[name] = [step_round(after(value, *waits), owners)]
        return done[name][0]

    trails = []
    for n, part in enumerate((mine, given)):
        heads = [part, swap_cores(part, owners)]
        trail = {(0, 0): heads[0], (0, 1): heads[1]}
        for number in range(1, APART + 1):
            for lane in range(2):
                if number <= lanes[lane]:
                    heads[lane] = launch("PQ"[lane] + str(number) + "ox"[n], heads[lane])
                    trail[number, lane] = heads[lane]
        trails.append(trail)
    joined = {}
    kept = []
    for s, rounds in enumerate(stages):
        gathered, spots, count = [], [], 0
        for number in rounds:
            for lane in range(2):
                if number > lanes[lane] or (number == 0 and lane):
                    continue
                if number == 0:
                    found = [(n * terms, trail[0, q], q) for n, trail in enumerate(trails) for q in range(2)]
                elif number <= APART:
                    found = [
                        (n * terms, v, q)
                        for n, trail in enumerate(trails)
                        for q, v in enumerate((trail[number, lane], swap_cores(trail[number, lane], owners)))
                    ]
                else:
                    if lane not in joined:
                        joined[lane] = jnp.concatenate([trail[APART, lane] for trail in trails], axis=0)
                    head = joined[lane] = launch("PQ"[lane] + str(number), joined[lane])
                    found = [(0, head, 0), (0, swap_cores(head, owners), 1)]
                for term, piece, q in found:
                    gathered.append(piece)
                    spots.append((term, (count + q) * sectors))
                count += 2
        waits = [v for w in WAITS.get("m" + str(s), ()) for v in done[w]]
        gathered[0] = after(gathered[0], *waits)
        slots = blocks if s == 0 else min(blocks, count * sectors)
        held = (parties * terms, count * sectors, columns, width)
        partial = right_products(lefts, gathered, spots, s, held, slots)
        done["m" + str(s)] = partial
        done["y" + str(s)] = [to_party(partial[1], 1)]
        kept.append((partial[0], done["y" + str(s)][0]))

    return pl.pallas_call(
        functools.partial(join_kernel, stages=len(kept), bases=(stage_base, target_base)),
        out_shape=jax.ShapeDtypeStruct((blocks, rows, width), jnp.bfloat16),
        in_specs=[smem] + [vmem] * (2 * len(kept)),
        out_specs=anywhere,
        scratch_shapes=[
            pltpu.VMEM((blocks, rows, width), jnp.bfloat16),
            pltpu.SemaphoreType.DMA((JOIN_BANDS,)),
        ],
        compiler_params=params,
        cost_estimate=pl.CostEstimate(flops=0, bytes_accessed=4 * 2**20, transcendentals=0),
        name="join_columns",
    )(index, *[pair[0] for pair in kept], *[pair[1] for pair in kept])


def solution(mesh):
    placed = (
        P("sec", None, None),
        P("sec"),
        P("sec"),
        P("mpo", "sec"),
        P("mpo", "sec", None, None),
        P("mpo", "sec", None, None),
    )
    return jax.shard_map(
        on_device, mesh=mesh, in_specs=placed, out_specs=P("sec", "mpo", None), check_vma=False
    )
```

time: 507 us -> 87.6 us (0.17)
  waiting for transfers between devices: 323 us -> 32.8 us
  local copies, waits for them, and re-layouts: 77.7 us -> 3.3 us
  matrix products: 31.3 us -> 0 us
  starting transfers between devices: 58.5 us -> 27.2 us
  Pallas kernels: 0 us -> 20.4 us
  between operations: 13.5 us -> 0.18 us
    all_to_all x3 -> x0, waiting for transfers between devices: 266 us -> none  [the longest x1 170 us: on_device(): lax.all_to_all(outgoing.reshape(owners, sector_count, term_count, block_w...]
    all_to_all x3 -> x0, starting transfers between devices: 58.5 us -> none  [the longest x1 45 us: on_device(): lax.all_to_all(returned, 'sec', split_axis=0, concat_axis=0, tiled=True)]
    reduce_scatter x1 -> x0, waiting for transfers between devices: 56.9 us -> none  [on_device(): lax.psum_scatter(partial_value.astype(jnp.float32).astype(jnp.bfloat16),...]
    ppermute x0 -> x29, waiting for transfers between devices: none -> 32.8 us  [the longest x5 19.7 us: to_party(): lax.ppermute(value, 'mpo', [(d, (d + j) % parties) for d in range(parties)])]
    dot_general x3 -> x0, matrix products: 31.3 us -> none  [the longest x2 25 us: on_device(): jnp.einsum('bij,bcj->bic', flattened[:, number], chosen_right, preferred_...]
    gather x5 -> x0, local copies, waits for them, and re-layouts: 27.8 us -> none  [the longest x2 15.4 us: on_device(): chosen_right = jnp.take(right_operators[number], sector_ids, axis=0)]
    ppermute x0 -> x29, starting transfers between devices: none -> 27.2 us  [the longest x11 17 us: step_round(): return lax.ppermute(value, 'sec', pairs)]
    pallas_call x0 -> x5, Pallas kernels: none -> 20.4 us  [the longest x3 11.1 us: right_products(): pl.pallas_call(functools.partial(right_kernel, lefts=len(lefts), spots=sp...]
  transfers between devices with their start and end apart: 4 -> 29, of which waited for: 3 -> 11; matrix products, arithmetic and copies ran while one was open for 13% -> 6% of each run, Pallas kernels for 0% -> 20%
where the time goes in v3:
time: 87.6 us; the launch traced here: 87.3 us
  waiting for transfers between devices  32.8 us (37%)
  starting transfers between devices  27.2 us (31%)
  Pallas kernels  20.4 us (23%)
  other arithmetic  3.51 us (4%)
  local copies, waits for them, and re-layouts  3.3 us (4%)
    ppermute x5, waiting for transfers between devices, to_party(): lax.ppermute(value, 'mpo', [(d, (d + j) % parties) for d in range(parties)])  19.7 us
    ppermute x11, starting transfers between devices, step_round(): return lax.ppermute(value, 'sec', pairs)  17 us
    ppermute x11, waiting for transfers between devices, step_round(): return lax.ppermute(value, 'sec', pairs)  13 us
    pallas_call x3, Pallas kernels, right_products(): pl.pallas_call(functools.partial(right_kernel, lefts=len(lefts), spots=sp...  11.1 us
    ppermute x5, starting transfers between devices, to_party(): lax.ppermute(value, 'mpo', [(d, (d + j) % parties) for d in range(parties)])  7.91 us
    pallas_call x1, Pallas kernels, left_products(): pl.pallas_call(functools.partial(left_kernel, parties=parties, count=len(...  6.02 us
    pallas_call x1, Pallas kernels, on_device(): pl.pallas_call(functools.partial(join_kernel, stages=len(kept), bases=(st...  3.28 us
    ppermute x13, starting transfers between devices, swap_cores(): return lax.ppermute(value, 'sec', [(d, d ^ 1) for d in range(owners)])  2.31 us
  transfers between devices with their start and end apart: 29, of which 11 were waited for; matrix products, arithmetic and copies ran while one was open for 6% of the time, Pallas kernels for 20%

profile of v3, /device:TPU:0, one launch (start us, length us, event | category | flops | bytes accessed | tf_op | source)
XLA Modules:
  0.0 87.3 jit_solution(12936797739914794583)
XLA Ops:
  0.0 1.1 %constant_dynamic-slice_fusion = (bf16[2,10,64,128]{3,2,1,0:T(8,128)(2,1)S(1)}, bf16[2,10,64,128]{3,2,1,0:T(8,128)(2,1)S(1)}) fusion(bf16[2,10,128,128]{3,2,1,0:T(8,128)(2,1)} %param.12, s32[]{:T(128)S(6)} %select_n.17, s32[]{:T(128)S(6)} %select_n.16), kind=kLoop, calls=%fused_computation.4 | loop fusion | bytes 1310728 | tf_op jit(solution)/shard_map/dynamic_slice | solution.py:331
  1.1 0.5 collective-permute-start.1
  1.6 2.6 %collective-permute-start.4 = (bf16[2,10,64,128]{3,2,1,0:T(8,128)(2,1)S(1)}, bf16[2,10,64,128]{3,2,1,0:T(8,128)(2,1)S(1)}, u32[]{:S(2)}, u32[]{:S(2)}) collective-permute-start(bf16[2,10,64,128]{3,2,1,0:T(8,128)(2,1)S(1)} %get-tuple-element.38.refs_2_), channel_id=1, source_target_pairs={{0,8},{2,6},{4,0},{6,14},{8,16},{10,2},{12,4},{14,22},{16,24},{18,... | collective-permute-start | bytes 983048 | tf_op jit(solution)/shard_map/ppermute | solution.py:45
  4.3 1.5 %collective-permute-start.2 = (bf16[2,10,64,128]{3,2,1,0:T(8,128)(2,1)S(1)}, bf16[2,10,64,128]{3,2,1,0:T(8,128)(2,1)S(1)}, u32[]{:S(2)}, u32[]{:S(2)}) collective-permute-start(bf16[2,10,64,128]{3,2,1,0:T(8,128)(2,1)S(1)} %get-tuple-element.37), channel_id=1, source_target_pairs={{0,1},{1,0},{2,3},{3,2},{4,5},{5,4},{6,7},{7,6},{8,9},{9,8},{10,11... | collective-permute-start | bytes 983048 | tf_op jit(solution)/shard_map/ppermute | solution.py:237
  5.8 0.7 convert_element_type.3
  6.5 1.6 %collective-permute-start.9 = (bf16[2,10,64,128]{3,2,1,0:T(8,128)(2,1)S(1)}, bf16[2,10,64,128]{3,2,1,0:T(8,128)(2,1)}, u32[]{:S(2)}, u32[]{:S(2)}) collective-permute-start(bf16[2,10,64,128]{3,2,1,0:T(8,128)(2,1)S(1)} %collective-permute-done.1.refs_3_), channel_id=1, source_target_pairs={{0,8},{2,6},{4,0},{6,14},{8,16},{10,2},{12,4},{14,22},{16,24},{18,... | collective-permute-start | bytes 983048 | tf_op jit(solution)/shard_map/ppermute | solution.py:45
  8.1 1.2 %broadcast_multiply_fusion.refs_0_ = bf16[2,10,128,128]{3,2,1,0:T(8,128)(2,1)S(1)} fusion(bf16[2,10,128,128]{3,2,1,0:T(8,128)(2,1)} %param.11, bf16[2,10]{1,0:T(2,128)(2,1)S(1)} %convert_element_type.3), kind=kLoop, calls=%fused_computation.2 | loop fusion | flops 327680 | bytes 1310760 | tf_op jit(solution)/shard_map/mul | solution.py:318
  9.3 2.1 %collective-permute-start.6 = (bf16[2,10,64,128]{3,2,1,0:T(8,128)(2,1)S(1)}, bf16[2,10,64,128]{3,2,1,0:T(8,128)(2,1)S(1)}, u32[]{:S(2)}, u32[]{:S(2)}) collective-permute-start(bf16[2,10,64,128]{3,2,1,0:T(8,128)(2,1)S(1)} %collective-permute-done.4.refs_6_), channel_id=1, source_target_pairs={{0,8},{2,6},{4,0},{6,14},{8,16},{10,2},{12,4},{14,22},{16,24},{18,... | collective-permute-start | bytes 983048 | tf_op jit(solution)/shard_map/ppermute | solution.py:45
  11.4 2.6 %collective-permute-done.2.refs_4_ = bf16[2,10,64,128]{3,2,1,0:T(8,128)(2,1)S(1)} collective-permute-done((bf16[2,10,64,128]{3,2,1,0:T(8,128)(2,1)S(1)}, bf16[2,10,64,128]{3,2,1,0:T(8,128)(2,1)S(1)}, u32[]{:S(2)}, u32[]{:S(2)}) %collective-permute-start.2) | collective-permute-done | bytes 327712 | tf_op jit(solution)/shard_map/ppermute | solution.py:237
  14.0 1.3 %collective-permute-start.11 = (bf16[2,10,64,128]{3,2,1,0:T(8,128)(2,1)}, bf16[2,10,64,128]{3,2,1,0:T(8,128)(2,1)S(1)}, u32[]{:S(2)}, u32[]{:S(2)}) collective-permute-start(bf16[2,10,64,128]{3,2,1,0:T(8,128)(2,1)} %collective-permute-done.9.refs_10_), channel_id=1, source_target_pairs={{0,8},{2,6},{4,0},{6,14},{8,16},{10,2},{12,4},{14,22},{16,24},{18,... | collective-permute-start | bytes 983048 | tf_op jit(solution)/shard_map/ppermute | solution.py:45
  15.2 1.2 %collective-permute-start = (bf16[2,10,128,128]{3,2,1,0:T(8,128)(2,1)S(1)}, bf16[2,10,128,128]{3,2,1,0:T(8,128)(2,1)}, u32[]{:S(2)}, u32[]{:S(2)}) collective-permute-start(bf16[2,10,128,128]{3,2,1,0:T(8,128)(2,1)S(1)} %broadcast_multiply_fusion.refs_0_), channel_id=1, source_target_pairs={{0,1},{1,0},{2,3},{3,2},{4,5},{5,4},{6,7},{7,6},{8,9},{9,8},{10,11... | collective-permute-start | bytes 1966088 | tf_op jit(solution)/shard_map/ppermute | solution.py:237
  16.5 0.6 collective-permute-done.6.refs_14_
  17.1 1.6 %collective-permute-start.7 = (bf16[2,10,64,128]{3,2,1,0:T(8,128)(2,1)S(1)}, bf16[2,10,64,128]{3,2,1,0:T(8,128)(2,1)}, u32[]{:S(2)}, u32[]{:S(2)}) collective-permute-start(bf16[2,10,64,128]{3,2,1,0:T(8,128)(2,1)S(1)} %collective-permute-done.2.refs_4_), channel_id=1, source_target_pairs={{0,8},{2,6},{4,0},{6,14},{8,16},{10,2},{12,4},{14,22},{16,24},{18,... | collective-permute-start | bytes 983048 | tf_op jit(solution)/shard_map/ppermute | solution.py:45
  18.7 2.7 %collective-permute-done.11.refs_18_ = bf16[2,10,64,128]{3,2,1,0:T(8,128)(2,1)S(1)} collective-permute-done((bf16[2,10,64,128]{3,2,1,0:T(8,128)(2,1)}, bf16[2,10,64,128]{3,2,1,0:T(8,128)(2,1)S(1)}, u32[]{:S(2)}, u32[]{:S(2)}) %collective-permute-start.11) | collective-permute-done | bytes 327712 | tf_op jit(solution)/shard_map/ppermute | solution.py:45
  21.3 1.2 %collective-permute-start.12 = (bf16[2,10,64,128]{3,2,1,0:T(8,128)(2,1)S(1)}, bf16[2,10,64,128]{3,2,1,0:T(8,128)(2,1)}, u32[]{:S(2)}, u32[]{:S(2)}) collective-permute-start(bf16[2,10,64,128]{3,2,1,0:T(8,128)(2,1)S(1)} %collective-permute-done.3.refs_5_), channel_id=1, source_target_pairs={{0,8},{2,6},{4,0},{6,14},{8,16},{10,2},{12,4},{14,22},{16,24},{18,... | collective-permute-start | bytes 983048 | tf_op jit(solution)/shard_map/ppermute | solution.py:45
  22.5 0.7 copy-done.4
  23.3 1.7 %collective-permute-done.7.refs_8_ = bf16[2,10,64,128]{3,2,1,0:T(8,128)(2,1)} collective-permute-done((bf16[2,10,64,128]{3,2,1,0:T(8,128)(2,1)S(1)}, bf16[2,10,64,128]{3,2,1,0:T(8,128)(2,1)}, u32[]{:S(2)}, u32[]{:S(2)}) %collective-permute-start.7) | collective-permute-done | bytes 327712 | tf_op jit(solution)/shard_map/ppermute | solution.py:45
  24.9 1.2 %collective-permute-start.15 = (bf16[2,10,64,128]{3,2,1,0:T(8,128)(2,1)}, bf16[2,10,64,128]{3,2,1,0:T(8,128)(2,1)S(1)}, u32[]{:S(2)}, u32[]{:S(2)}) collective-permute-start(bf16[2,10,64,128]{3,2,1,0:T(8,128)(2,1)} %collective-permute-done.7.refs_8_), channel_id=1, source_target_pairs={{0,8},{2,6},{4,0},{6,14},{8,16},{10,2},{12,4},{14,22},{16,24},{18,... | collective-permute-start | bytes 983048 | tf_op jit(solution)/shard_map/ppermute | solution.py:45
  26.2 0.5 collective-permute-start.14
  26.7 5.2 %collective-permute-done.refs_1_ = bf16[2,10,128,128]{3,2,1,0:T(8,128)(2,1)} collective-permute-done((bf16[2,10,128,128]{3,2,1,0:T(8,128)(2,1)S(1)}, bf16[2,10,128,128]{3,2,1,0:T(8,128)(2,1)}, u32[]{:S(2)}, u32[]{:S(2)}) %collective-permute-start) | collective-permute-done | bytes 655392 | tf_op jit(solution)/shard_map/ppermute | solution.py:237
  31.8 0.5 collective-permute-start.8
  32.4 1.2 %collective-permute-start.18 = (bf16[2,10,64,128]{3,2,1,0:T(8,128)(2,1)}, bf16[2,10,64,128]{3,2,1,0:T(8,128)(2,1)S(1)}, u32[]{:S(2)}, u32[]{:S(2)}) collective-permute-start(bf16[2,10,64,128]{3,2,1,0:T(8,128)(2,1)} %collective-permute-done.12.refs_12_), channel_id=1, source_target_pairs={{0,8},{2,6},{4,0},{6,14},{8,16},{10,2},{12,4},{14,22},{16,24},{18,... | collective-permute-start | bytes 983048 | tf_op jit(solution)/shard_map/ppermute | solution.py:45
  33.5 0.9 %pad_maximum_fusion = bf16[4,10,64,128]{3,2,1,0:T(8,128)(2,1)} fusion(bf16[2,10,64,128]{3,2,1,0:T(8,128)(2,1)S(1)} %collective-permute-done.15.refs_16_, bf16[2,10,64,128]{3,2,1,0:T(8,128)(2,1)S(1)} %collective-permute-done.6.refs_14_), kind=kLoop, calls=%fused_computation | loop fusion | flops 327680 | bytes 1310720 | tf_op jit(solution)/shard_map/concatenate | solution.py:370
  34.4 1.6 %collective-permute-start.20 = (bf16[4,10,64,128]{3,2,1,0:T(8,128)(2,1)}, bf16[4,10,64,128]{3,2,1,0:T(8,128)(2,1)S(1)}, u32[]{:S(2)}, u32[]{:S(2)}) collective-permute-start(bf16[4,10,64,128]{3,2,1,0:T(8,128)(2,1)} %pad_maximum_fusion), channel_id=1, source_target_pairs={{0,8},{2,6},{4,0},{6,14},{8,16},{10,2},{12,4},{14,22},{16,24},{18,... | collective-permute-start | bytes 1966088 | tf_op jit(solution)/shard_map/ppermute | solution.py:45
  36.0 0.7 and_select_fusion
  36.7 0.1 collective-permute-start.17
  36.7 0.7 fusion
  37.4 0.7 concatenate.9.index_ref
  38.2 0.6 collective-permute-start.13
  38.7 0.1 collective-permute-start.16
  38.8 0.8 collective-permute-done.18.refs_20_
  39.6 6.0 %left_products.1 = (bf16[80,128,256]{2,1,0:T(8,128)(2,1)S(1)}, bf16[80,128,256]{2,1,0:T(8,128)(2,1)S(1)}) custom-call(s32[305]{0:T(512)S(1)} %concatenate.9.index_ref, bf16[2,10,128,128]{3,2,1,0:T(8,128)(2,1)S(1)} %broadcast_multiply_fusion.refs_0_, bf16[2,10,128,128]{3,2,1,0:T(8,128)(2,1)} %collective-permute-done.refs_1_, bf16[80,128,128]{2,1,0:T(8,128)(2,1)} %refs_2_.1), custom_call_target="tpu_custom_call" | custom-call | flops 1342177280 | bytes 9437184 | tf_op jit(solution)/shard_map/left_products/pallas_call | solution.py:267
  45.7 0.1 pad_maximum_fusion.1
  45.7 1.2 %collective-permute-start.22 = (bf16[4,10,64,128]{3,2,1,0:T(8,128)(2,1)S(1)}, bf16[4,10,64,128]{3,2,1,0:T(8,128)(2,1)S(1)}, u32[]{:S(2)}, u32[]{:S(2)}) collective-permute-start(bf16[4,10,64,128]{3,2,1,0:T(8,128)(2,1)S(1)} %pad_maximum_fusion.1), channel_id=1, source_target_pairs={{0,8},{2,6},{4,0},{6,14},{8,16},{10,2},{12,4},{14,22},{16,24},{18,... | collective-permute-start | bytes 1966088 | tf_op jit(solution)/shard_map/ppermute | solution.py:45
  47.0 6.3 %right_products.3 = (bf16[40,64,128]{2,1,0:T(8,128)(2,1)S(1)}, bf16[40,64,128]{2,1,0:T(8,128)(2,1)S(1)}) custom-call(s32[305]{0:T(512)S(1)} %concatenate.9.index_ref, bf16[80,128,256]{2,1,0:T(8,128)(2,1)S(1)} %get-tuple-element.21.refs_0_, bf16[80,128,256]{2,1,0:T(8,128)(2,1)S(1)} %get-tuple-element.22.refs_1_, ...), custom_call_target="tpu_custom_call" | custom-call | flops 671088640 | bytes 12582912 | tf_op jit(solution)/shard_map/right_products/pallas_call | solution.py:291
  53.3 1.6 %collective-permute-start.24 = (bf16[4,10,64,128]{3,2,1,0:T(8,128)(2,1)S(1)}, bf16[4,10,64,128]{3,2,1,0:T(8,128)(2,1)S(1)}, u32[]{:S(2)}, u32[]{:S(2)}) collective-permute-start(bf16[4,10,64,128]{3,2,1,0:T(8,128)(2,1)S(1)} %collective-permute-done.20.refs_2_), channel_id=1, source_target_pairs={{0,8},{2,6},{4,0},{6,14},{8,16},{10,2},{12,4},{14,22},{16,24},{18,... | collective-permute-start | bytes 1966088 | tf_op jit(solution)/shard_map/ppermute | solution.py:45
  54.9 0.1 collective-permute-start.21
  54.9 1.5 %collective-permute-done.22.refs_4_ = bf16[4,10,64,128]{3,2,1,0:T(8,128)(2,1)S(1)} collective-permute-done((bf16[4,10,64,128]{3,2,1,0:T(8,128)(2,1)S(1)}, bf16[4,10,64,128]{3,2,1,0:T(8,128)(2,1)S(1)}, u32[]{:S(2)}, u32[]{:S(2)}) %collective-permute-start.22) | collective-permute-done | bytes 655392 | tf_op jit(solution)/shard_map/ppermute | solution.py:45
  56.4 1.7 %collective-permute-start.25 = (bf16[40,64,128]{2,1,0:T(8,128)(2,1)S(1)}, bf16[40,64,128]{2,1,0:T(8,128)(2,1)S(1)}, u32[]{:S(2)}, u32[]{:S(2)}) collective-permute-start(bf16[40,64,128]{2,1,0:T(8,128)(2,1)S(1)} %get-tuple-element.31), channel_id=1, source_target_pairs={{0,1},{1,0},{2,3},{3,2},{4,5},{5,4},{6,7},{7,6},{8,9},{9,8},{10,11... | collective-permute-start | bytes 1966088 | tf_op jit(solution)/shard_map/ppermute | solution.py:237
  58.1 5.8 %collective-permute-done.24.refs_2_ = bf16[4,10,64,128]{3,2,1,0:T(8,128)(2,1)S(1)} collective-permute-done((bf16[4,10,64,128]{3,2,1,0:T(8,128)(2,1)S(1)}, bf16[4,10,64,128]{3,2,1,0:T(8,128)(2,1)S(1)}, u32[]{:S(2)}, u32[]{:S(2)}) %collective-permute-start.24) | collective-permute-done | bytes 655392 | tf_op jit(solution)/shard_map/ppermute | solution.py:45
  63.9 2.9 %right_products.4 = (bf16[20,64,128]{2,1,0:T(8,128)(2,1)S(1)}, bf16[20,64,128]{2,1,0:T(8,128)(2,1)S(1)}) custom-call(s32[305]{0:T(512)S(1)} %concatenate.9.index_ref, bf16[80,128,256]{2,1,0:T(8,128)(2,1)S(1)} %get-tuple-element.21.refs_0_, bf16[80,128,256]{2,1,0:T(8,128)(2,1)S(1)} %get-tuple-element.22.refs_1_, ...), custom_call_target="tpu_custom_call" | custom-call | flops 335544320 | bytes 12582912 | tf_op jit(solution)/shard_map/right_products/pallas_call | solution.py:291
  66.9 1.6 %collective-permute-start.27 = (bf16[20,64,128]{2,1,0:T(8,128)(2,1)S(1)}, bf16[20,64,128]{2,1,0:T(8,128)(2,1)S(1)}, u32[]{:S(2)}, u32[]{:S(2)}) collective-permute-start(bf16[20,64,128]{2,1,0:T(8,128)(2,1)S(1)} %get-tuple-element.35), channel_id=1, source_target_pairs={{0,1},{1,0},{2,3},{3,2},{4,5},{5,4},{6,7},{7,6},{8,9},{9,8},{10,11... | collective-permute-start | bytes 983048 | tf_op jit(solution)/shard_map/ppermute | solution.py:237
  68.5 5.4 %collective-permute-done.25.refs_3_ = bf16[40,64,128]{2,1,0:T(8,128)(2,1)S(1)} collective-permute-done((bf16[40,64,128]{2,1,0:T(8,128)(2,1)S(1)}, bf16[40,64,128]{2,1,0:T(8,128)(2,1)S(1)}, u32[]{:S(2)}, u32[]{:S(2)}) %collective-permute-start.25) | collective-permute-done | bytes 655392 | tf_op jit(solution)/shard_map/ppermute | solution.py:237
  73.9 1.9 %right_products.5 = (bf16[10,64,128]{2,1,0:T(8,128)(2,1)S(1)}, bf16[10,64,128]{2,1,0:T(8,128)(2,1)S(1)}) custom-call(s32[305]{0:T(512)S(1)} %concatenate.9.index_ref, bf16[80,128,256]{2,1,0:T(8,128)(2,1)S(1)} %get-tuple-element.21.refs_0_, bf16[80,128,256]{2,1,0:T(8,128)(2,1)S(1)} %get-tuple-element.22.refs_1_, ...), custom_call_target="tpu_custom_call" | custom-call | flops 167772160 | bytes 12582912 | tf_op jit(solution)/shard_map/right_products/pallas_call | solution.py:291
  75.8 1.8 %collective-permute-start.28 = (bf16[10,64,128]{2,1,0:T(8,128)(2,1)S(1)}, bf16[10,64,128]{2,1,0:T(8,128)(2,1)S(1)}, u32[]{:S(2)}, u32[]{:S(2)}) collective-permute-start(bf16[10,64,128]{2,1,0:T(8,128)(2,1)S(1)} %get-tuple-element.36), channel_id=1, source_target_pairs={{0,1},{1,0},{2,3},{3,2},{4,5},{5,4},{6,7},{7,6},{8,9},{9,8},{10,11... | collective-permute-start | bytes 491528 | tf_op jit(solution)/shard_map/ppermute | solution.py:237
  77.6 3.3 %collective-permute-done.27.refs_4_ = bf16[20,64,128]{2,1,0:T(8,128)(2,1)S(1)} collective-permute-done((bf16[20,64,128]{2,1,0:T(8,128)(2,1)S(1)}, bf16[20,64,128]{2,1,0:T(8,128)(2,1)S(1)}, u32[]{:S(2)}, u32[]{:S(2)}) %collective-permute-start.27) | collective-permute-done | bytes 327712 | tf_op jit(solution)/shard_map/ppermute | solution.py:237
  80.9 3.1 %collective-permute-done.28.refs_5_ = bf16[10,64,128]{2,1,0:T(8,128)(2,1)S(1)} collective-permute-done((bf16[10,64,128]{2,1,0:T(8,128)(2,1)S(1)}, bf16[10,64,128]{2,1,0:T(8,128)(2,1)S(1)}, u32[]{:S(2)}, u32[]{:S(2)}) %collective-permute-start.28) | collective-permute-done | bytes 163872 | tf_op jit(solution)/shard_map/ppermute | solution.py:237
  84.1 3.3 %join_columns.1 = bf16[80,64,128]{2,1,0:T(8,128)(2,1)} custom-call(s32[305]{0:T(512)S(1)} %concatenate.9.index_ref, bf16[40,64,128]{2,1,0:T(8,128)(2,1)S(1)} %get-tuple-element.28.refs_0_, bf16[20,64,128]{2,1,0:T(8,128)(2,1)S(1)} %get-tuple-element.30.refs_1_, bf16[10,64,128]{2,1,0:T(8,128)(2,1)S(1)} %get-tuple-element.34.refs_2_, ...), custom_call_target="tpu_custom_call" | custom-call | bytes 4194304 | tf_op jit(solution)/shard_map/join_columns/pallas_call | solution.py:386
  (35 shorter events, 0.1 us)
Async XLA Ops:
  1.1 5.4 %collective-permute-start.1 = (bf16[2,10,64,128]{3,2,1,0:T(8,128)(2,1)S(1)}, bf16[2,10,64,128]{3,2,1,0:T(8,128)(2,1)S(1)}, u32[]{:S(2)}, u32[]{:S(2)}) collective-permute-start(bf16[2,10,64,128]{3,2,1,0:T(8,128)(2,1)S(1)} %get-tuple-element.38.refs_2_), channel_id=1, source_target_pairs={{0,2},{2,0},{4,6},{6,4},{8,10},{10,8},{12,14},{14,12},{16,18},{18,... | collective-permute-start | bytes 983048 | tf_op jit(solution)/shard_map/ppermute | solution.py:37
  1.6 7.6 %collective-permute-start.4 = (bf16[2,10,64,128]{3,2,1,0:T(8,128)(2,1)S(1)}, bf16[2,10,64,128]{3,2,1,0:T(8,128)(2,1)S(1)}, u32[]{:S(2)}, u32[]{:S(2)}) collective-permute-start(bf16[2,10,64,128]{3,2,1,0:T(8,128)(2,1)S(1)} %get-tuple-element.38.refs_2_), channel_id=1, source_target_pairs={{0,8},{2,6},{4,0},{6,14},{8,16},{10,2},{12,4},{14,22},{16,24},{18,... | collective-permute-start | bytes 983048 | tf_op jit(solution)/shard_map/ppermute | solution.py:45
  4.3 9.7 %collective-permute-start.2 = (bf16[2,10,64,128]{3,2,1,0:T(8,128)(2,1)S(1)}, bf16[2,10,64,128]{3,2,1,0:T(8,128)(2,1)S(1)}, u32[]{:S(2)}, u32[]{:S(2)}) collective-permute-start(bf16[2,10,64,128]{3,2,1,0:T(8,128)(2,1)S(1)} %get-tuple-element.37), channel_id=1, source_target_pairs={{0,1},{1,0},{2,3},{3,2},{4,5},{5,4},{6,7},{7,6},{8,9},{9,8},{10,11... | collective-permute-start | bytes 983048 | tf_op jit(solution)/shard_map/ppermute | solution.py:237
  6.5 7.5 %collective-permute-start.9 = (bf16[2,10,64,128]{3,2,1,0:T(8,128)(2,1)S(1)}, bf16[2,10,64,128]{3,2,1,0:T(8,128)(2,1)}, u32[]{:S(2)}, u32[]{:S(2)}) collective-permute-start(bf16[2,10,64,128]{3,2,1,0:T(8,128)(2,1)S(1)} %collective-permute-done.1.refs_3_), channel_id=1, source_target_pairs={{0,8},{2,6},{4,0},{6,14},{8,16},{10,2},{12,4},{14,22},{16,24},{18,... | collective-permute-start | bytes 983048 | tf_op jit(solution)/shard_map/ppermute | solution.py:45
  9.3 25.1 %copy-start = (bf16[2,10,64,128]{3,2,1,0:T(8,128)(2,1)}, bf16[2,10,64,128]{3,2,1,0:T(8,128)(2,1)S(1)}, u32[]{:S(2)}) copy-start(bf16[2,10,64,128]{3,2,1,0:T(8,128)(2,1)S(1)} %collective-permute-done.4.refs_6_) | copy-start | bytes 983044
  9.3 7.8 %collective-permute-start.6 = (bf16[2,10,64,128]{3,2,1,0:T(8,128)(2,1)S(1)}, bf16[2,10,64,128]{3,2,1,0:T(8,128)(2,1)S(1)}, u32[]{:S(2)}, u32[]{:S(2)}) collective-permute-start(bf16[2,10,64,128]{3,2,1,0:T(8,128)(2,1)S(1)} %collective-permute-done.4.refs_6_), channel_id=1, source_target_pairs={{0,8},{2,6},{4,0},{6,14},{8,16},{10,2},{12,4},{14,22},{16,24},{18,... | collective-permute-start | bytes 983048 | tf_op jit(solution)/shard_map/ppermute | solution.py:45
  14.0 20.4 %copy-start.2 = (bf16[2,10,64,128]{3,2,1,0:T(8,128)(2,1)}, bf16[2,10,64,128]{3,2,1,0:T(8,128)(2,1)S(1)}, u32[]{:S(2)}) copy-start(bf16[2,10,64,128]{3,2,1,0:T(8,128)(2,1)S(1)} %collective-permute-done.2.refs_4_) | copy-start | bytes 983044
  14.0 4.7 %collective-permute-start.3 = (bf16[2,10,64,128]{3,2,1,0:T(8,128)(2,1)S(1)}, bf16[2,10,64,128]{3,2,1,0:T(8,128)(2,1)S(1)}, u32[]{:S(2)}, u32[]{:S(2)}) collective-permute-start(bf16[2,10,64,128]{3,2,1,0:T(8,128)(2,1)S(1)} %collective-permute-done.2.refs_4_), channel_id=1, source_target_pairs={{0,2},{2,0},{4,6},{6,4},{8,10},{10,8},{12,14},{14,12},{16,18},{18,... | collective-permute-start | bytes 983048 | tf_op jit(solution)/shard_map/ppermute | solution.py:37
  14.0 7.3 %collective-permute-start.11 = (bf16[2,10,64,128]{3,2,1,0:T(8,128)(2,1)}, bf16[2,10,64,128]{3,2,1,0:T(8,128)(2,1)S(1)}, u32[]{:S(2)}, u32[]{:S(2)}) collective-permute-start(bf16[2,10,64,128]{3,2,1,0:T(8,128)(2,1)} %collective-permute-done.9.refs_10_), channel_id=1, source_target_pairs={{0,8},{2,6},{4,0},{6,14},{8,16},{10,2},{12,4},{14,22},{16,24},{18,... | collective-permute-start | bytes 983048 | tf_op jit(solution)/shard_map/ppermute | solution.py:45
  15.2 16.6 %collective-permute-start = (bf16[2,10,128,128]{3,2,1,0:T(8,128)(2,1)S(1)}, bf16[2,10,128,128]{3,2,1,0:T(8,128)(2,1)}, u32[]{:S(2)}, u32[]{:S(2)}) collective-permute-start(bf16[2,10,128,128]{3,2,1,0:T(8,128)(2,1)S(1)} %broadcast_multiply_fusion.refs_0_), channel_id=1, source_target_pairs={{0,1},{1,0},{2,3},{3,2},{4,5},{5,4},{6,7},{7,6},{8,9},{9,8},{10,11... | collective-permute-start | bytes 1966088 | tf_op jit(solution)/shard_map/ppermute | solution.py:237
  17.1 7.9 %collective-permute-start.7 = (bf16[2,10,64,128]{3,2,1,0:T(8,128)(2,1)S(1)}, bf16[2,10,64,128]{3,2,1,0:T(8,128)(2,1)}, u32[]{:S(2)}, u32[]{:S(2)}) collective-permute-start(bf16[2,10,64,128]{3,2,1,0:T(8,128)(2,1)S(1)} %collective-permute-done.2.refs_4_), channel_id=1, source_target_pairs={{0,8},{2,6},{4,0},{6,14},{8,16},{10,2},{12,4},{14,22},{16,24},{18,... | collective-permute-start | bytes 983048 | tf_op jit(solution)/shard_map/ppermute | solution.py:45
  21.3 10.5 %collective-permute-start.12 = (bf16[2,10,64,128]{3,2,1,0:T(8,128)(2,1)S(1)}, bf16[2,10,64,128]{3,2,1,0:T(8,128)(2,1)}, u32[]{:S(2)}, u32[]{:S(2)}) collective-permute-start(bf16[2,10,64,128]{3,2,1,0:T(8,128)(2,1)S(1)} %collective-permute-done.3.refs_5_), channel_id=1, source_target_pairs={{0,8},{2,6},{4,0},{6,14},{8,16},{10,2},{12,4},{14,22},{16,24},{18,... | collective-permute-start | bytes 983048 | tf_op jit(solution)/shard_map/ppermute | solution.py:45
  22.5 0.7 copy-start.4
  24.9 7.4 %collective-permute-start.15 = (bf16[2,10,64,128]{3,2,1,0:T(8,128)(2,1)}, bf16[2,10,64,128]{3,2,1,0:T(8,128)(2,1)S(1)}, u32[]{:S(2)}, u32[]{:S(2)}) collective-permute-start(bf16[2,10,64,128]{3,2,1,0:T(8,128)(2,1)} %collective-permute-done.7.refs_8_), channel_id=1, source_target_pairs={{0,8},{2,6},{4,0},{6,14},{8,16},{10,2},{12,4},{14,22},{16,24},{18,... | collective-permute-start | bytes 983048 | tf_op jit(solution)/shard_map/ppermute | solution.py:45
  26.1 8.3 %collective-permute-start.5 = (bf16[2,10,64,128]{3,2,1,0:T(8,128)(2,1)S(1)}, bf16[2,10,64,128]{3,2,1,0:T(8,128)(2,1)}, u32[]{:S(2)}, u32[]{:S(2)}) collective-permute-start(bf16[2,10,64,128]{3,2,1,0:T(8,128)(2,1)S(1)} %collective-permute-done.4.refs_6_), channel_id=1, source_target_pairs={{0,2},{2,0},{4,6},{6,4},{8,10},{10,8},{12,14},{14,12},{16,18},{18,... | collective-permute-start | bytes 983048 | tf_op jit(solution)/shard_map/ppermute | solution.py:37
  26.2 10.5 %collective-permute-start.14 = (bf16[2,10,64,128]{3,2,1,0:T(8,128)(2,1)S(1)}, bf16[2,10,64,128]{3,2,1,0:T(8,128)(2,1)}, u32[]{:S(2)}, u32[]{:S(2)}) collective-permute-start(bf16[2,10,64,128]{3,2,1,0:T(8,128)(2,1)S(1)} %collective-permute-done.6.refs_14_), channel_id=1, source_target_pairs={{0,2},{2,0},{4,6},{6,4},{8,10},{10,8},{12,14},{14,12},{16,18},{18,... | collective-permute-start | bytes 983048 | tf_op jit(solution)/shard_map/ppermute | solution.py:37
  31.8 6.4 %collective-permute-start.10 = (bf16[2,10,64,128]{3,2,1,0:T(8,128)(2,1)}, bf16[2,10,64,128]{3,2,1,0:T(8,128)(2,1)}, u32[]{:S(2)}, u32[]{:S(2)}) collective-permute-start(bf16[2,10,64,128]{3,2,1,0:T(8,128)(2,1)} %collective-permute-done.9.refs_10_), channel_id=1, source_target_pairs={{0,2},{2,0},{4,6},{6,4},{8,10},{10,8},{12,14},{14,12},{16,18},{18,... | collective-permute-start | bytes 983048 | tf_op jit(solution)/shard_map/ppermute | solution.py:37
  31.8 6.9 %collective-permute-start.8 = (bf16[2,10,64,128]{3,2,1,0:T(8,128)(2,1)}, bf16[2,10,64,128]{3,2,1,0:T(8,128)(2,1)}, u32[]{:S(2)}, u32[]{:S(2)}) collective-permute-start(bf16[2,10,64,128]{3,2,1,0:T(8,128)(2,1)} %collective-permute-done.7.refs_8_), channel_id=1, source_target_pairs={{0,2},{2,0},{4,6},{6,4},{8,10},{10,8},{12,14},{14,12},{16,18},{18,... | collective-permute-start | bytes 983048 | tf_op jit(solution)/shard_map/ppermute | solution.py:37
  32.4 7.3 %collective-permute-start.18 = (bf16[2,10,64,128]{3,2,1,0:T(8,128)(2,1)}, bf16[2,10,64,128]{3,2,1,0:T(8,128)(2,1)S(1)}, u32[]{:S(2)}, u32[]{:S(2)}) collective-permute-start(bf16[2,10,64,128]{3,2,1,0:T(8,128)(2,1)} %collective-permute-done.12.refs_12_), channel_id=1, source_target_pairs={{0,8},{2,6},{4,0},{6,14},{8,16},{10,2},{12,4},{14,22},{16,24},{18,... | collective-permute-start | bytes 983048 | tf_op jit(solution)/shard_map/ppermute | solution.py:45
  34.4 18.9 %collective-permute-start.20 = (bf16[4,10,64,128]{3,2,1,0:T(8,128)(2,1)}, bf16[4,10,64,128]{3,2,1,0:T(8,128)(2,1)S(1)}, u32[]{:S(2)}, u32[]{:S(2)}) collective-permute-start(bf16[4,10,64,128]{3,2,1,0:T(8,128)(2,1)} %pad_maximum_fusion), channel_id=1, source_target_pairs={{0,8},{2,6},{4,0},{6,14},{8,16},{10,2},{12,4},{14,22},{16,24},{18,... | collective-permute-start | bytes 1966088 | tf_op jit(solution)/shard_map/ppermute | solution.py:45
  36.7 9.1 %collective-permute-start.17 = (bf16[2,10,64,128]{3,2,1,0:T(8,128)(2,1)S(1)}, bf16[2,10,64,128]{3,2,1,0:T(8,128)(2,1)}, u32[]{:S(2)}, u32[]{:S(2)}) collective-permute-start(bf16[2,10,64,128]{3,2,1,0:T(8,128)(2,1)S(1)} %collective-permute-done.11.refs_18_), channel_id=1, source_target_pairs={{0,2},{2,0},{4,6},{6,4},{8,10},{10,8},{12,14},{14,12},{16,18},{18,... | collective-permute-start | bytes 983048 | tf_op jit(solution)/shard_map/ppermute | solution.py:37
  38.2 8.8 %copy-start.1 = (bf16[2,10,64,128]{3,2,1,0:T(8,128)(2,1)S(1)}, bf16[2,10,64,128]{3,2,1,0:T(8,128)(2,1)}, u32[]{:S(2)}) copy-start(bf16[2,10,64,128]{3,2,1,0:T(8,128)(2,1)} %copy-done) | copy-start | bytes 983044
  38.2 8.8 %copy-start.3 = (bf16[2,10,64,128]{3,2,1,0:T(8,128)(2,1)S(1)}, bf16[2,10,64,128]{3,2,1,0:T(8,128)(2,1)}, u32[]{:S(2)}) copy-start(bf16[2,10,64,128]{3,2,1,0:T(8,128)(2,1)} %copy-done.2) | copy-start | bytes 983044
  38.2 8.8 %copy-start.5 = (bf16[2,10,64,128]{3,2,1,0:T(8,128)(2,1)S(1)}, bf16[2,10,64,128]{3,2,1,0:T(8,128)(2,1)}, u32[]{:S(2)}) copy-start(bf16[2,10,64,128]{3,2,1,0:T(8,128)(2,1)} %copy-done.4) | copy-start | bytes 983044
  38.2 8.8 %collective-permute-start.13 = (bf16[2,10,64,128]{3,2,1,0:T(8,128)(2,1)}, bf16[2,10,64,128]{3,2,1,0:T(8,128)(2,1)S(1)}, u32[]{:S(2)}, u32[]{:S(2)}) collective-permute-start(bf16[2,10,64,128]{3,2,1,0:T(8,128)(2,1)} %collective-permute-done.12.refs_12_), channel_id=1, source_target_pairs={{0,2},{2,0},{4,6},{6,4},{8,10},{10,8},{12,14},{14,12},{16,18},{18,... | collective-permute-start | bytes 983048 | tf_op jit(solution)/shard_map/ppermute | solution.py:37
  38.7 8.2 %collective-permute-start.16 = (bf16[2,10,64,128]{3,2,1,0:T(8,128)(2,1)S(1)}, bf16[2,10,64,128]{3,2,1,0:T(8,128)(2,1)S(1)}, u32[]{:S(2)}, u32[]{:S(2)}) collective-permute-start(bf16[2,10,64,128]{3,2,1,0:T(8,128)(2,1)S(1)} %collective-permute-done.15.refs_16_), channel_id=1, source_target_pairs={{0,2},{2,0},{4,6},{6,4},{8,10},{10,8},{12,14},{14,12},{16,18},{18,... | collective-permute-start | bytes 983048 | tf_op jit(solution)/shard_map/ppermute | solution.py:37
  39.6 7.3 %collective-permute-start.19 = (bf16[2,10,64,128]{3,2,1,0:T(8,128)(2,1)S(1)}, bf16[2,10,64,128]{3,2,1,0:T(8,128)(2,1)S(1)}, u32[]{:S(2)}, u32[]{:S(2)}) collective-permute-start(bf16[2,10,64,128]{3,2,1,0:T(8,128)(2,1)S(1)} %collective-permute-done.18.refs_20_), channel_id=1, source_target_pairs={{0,2},{2,0},{4,6},{6,4},{8,10},{10,8},{12,14},{14,12},{16,18},{18,... | collective-permute-start | bytes 983048 | tf_op jit(solution)/shard_map/ppermute | solution.py:37
  45.7 10.6 %collective-permute-start.22 = (bf16[4,10,64,128]{3,2,1,0:T(8,128)(2,1)S(1)}, bf16[4,10,64,128]{3,2,1,0:T(8,128)(2,1)S(1)}, u32[]{:S(2)}, u32[]{:S(2)}) collective-permute-start(bf16[4,10,64,128]{3,2,1,0:T(8,128)(2,1)S(1)} %pad_maximum_fusion.1), channel_id=1, source_target_pairs={{0,8},{2,6},{4,0},{6,14},{8,16},{10,2},{12,4},{14,22},{16,24},{18,... | collective-permute-start | bytes 1966088 | tf_op jit(solution)/shard_map/ppermute | solution.py:45
  53.3 10.6 %collective-permute-start.24 = (bf16[4,10,64,128]{3,2,1,0:T(8,128)(2,1)S(1)}, bf16[4,10,64,128]{3,2,1,0:T(8,128)(2,1)S(1)}, u32[]{:S(2)}, u32[]{:S(2)}) collective-permute-start(bf16[4,10,64,128]{3,2,1,0:T(8,128)(2,1)S(1)} %collective-permute-done.20.refs_2_), channel_id=1, source_target_pairs={{0,8},{2,6},{4,0},{6,14},{8,16},{10,2},{12,4},{14,22},{16,24},{18,... | collective-permute-start | bytes 1966088 | tf_op jit(solution)/shard_map/ppermute | solution.py:45
  54.9 9.1 %collective-permute-start.21 = (bf16[4,10,64,128]{3,2,1,0:T(8,128)(2,1)S(1)}, bf16[4,10,64,128]{3,2,1,0:T(8,128)(2,1)S(1)}, u32[]{:S(2)}, u32[]{:S(2)}) collective-permute-start(bf16[4,10,64,128]{3,2,1,0:T(8,128)(2,1)S(1)} %collective-permute-done.20.refs_2_), channel_id=1, source_target_pairs={{0,2},{2,0},{4,6},{6,4},{8,10},{10,8},{12,14},{14,12},{16,18},{18,... | collective-permute-start | bytes 1966088 | tf_op jit(solution)/shard_map/ppermute | solution.py:37
  56.4 7.6 %collective-permute-start.23 = (bf16[4,10,64,128]{3,2,1,0:T(8,128)(2,1)S(1)}, bf16[4,10,64,128]{3,2,1,0:T(8,128)(2,1)S(1)}, u32[]{:S(2)}, u32[]{:S(2)}) collective-permute-start(bf16[4,10,64,128]{3,2,1,0:T(8,128)(2,1)S(1)} %collective-permute-done.22.refs_4_), channel_id=1, source_target_pairs={{0,2},{2,0},{4,6},{6,4},{8,10},{10,8},{12,14},{14,12},{16,18},{18,... | collective-permute-start | bytes 1966088 | tf_op jit(solution)/shard_map/ppermute | solution.py:37
  56.4 17.5 %collective-permute-start.25 = (bf16[40,64,128]{2,1,0:T(8,128)(2,1)S(1)}, bf16[40,64,128]{2,1,0:T(8,128)(2,1)S(1)}, u32[]{:S(2)}, u32[]{:S(2)}) collective-permute-start(bf16[40,64,128]{2,1,0:T(8,128)(2,1)S(1)} %get-tuple-element.31), channel_id=1, source_target_pairs={{0,1},{1,0},{2,3},{3,2},{4,5},{5,4},{6,7},{7,6},{8,9},{9,8},{10,11... | collective-permute-start | bytes 1966088 | tf_op jit(solution)/shard_map/ppermute | solution.py:237
  63.9 10.0 %collective-permute-start.26 = (bf16[4,10,64,128]{3,2,1,0:T(8,128)(2,1)S(1)}, bf16[4,10,64,128]{3,2,1,0:T(8,128)(2,1)S(1)}, u32[]{:S(2)}, u32[]{:S(2)}) collective-permute-start(bf16[4,10,64,128]{3,2,1,0:T(8,128)(2,1)S(1)} %collective-permute-done.24.refs_2_), channel_id=1, source_target_pairs={{0,2},{2,0},{4,6},{6,4},{8,10},{10,8},{12,14},{14,12},{16,18},{18,... | collective-permute-start | bytes 1966088 | tf_op jit(solution)/shard_map/ppermute | solution.py:37
  66.9 14.1 %collective-permute-start.27 = (bf16[20,64,128]{2,1,0:T(8,128)(2,1)S(1)}, bf16[20,64,128]{2,1,0:T(8,128)(2,1)S(1)}, u32[]{:S(2)}, u32[]{:S(2)}) collective-permute-start(bf16[20,64,128]{2,1,0:T(8,128)(2,1)S(1)} %get-tuple-element.35), channel_id=1, source_target_pairs={{0,1},{1,0},{2,3},{3,2},{4,5},{5,4},{6,7},{7,6},{8,9},{9,8},{10,11... | collective-permute-start | bytes 983048 | tf_op jit(solution)/shard_map/ppermute | solution.py:237
  75.8 8.3 %collective-permute-start.28 = (bf16[10,64,128]{2,1,0:T(8,128)(2,1)S(1)}, bf16[10,64,128]{2,1,0:T(8,128)(2,1)S(1)}, u32[]{:S(2)}, u32[]{:S(2)}) collective-permute-start(bf16[10,64,128]{2,1,0:T(8,128)(2,1)S(1)} %get-tuple-element.36), channel_id=1, source_target_pairs={{0,1},{1,0},{2,3},{3,2},{4,5},{5,4},{6,7},{7,6},{8,9},{9,8},{10,11... | collective-permute-start | bytes 491528 | tf_op jit(solution)/shard_map/ppermute | solution.py:237

commit v4 on v3

--- a/solution.py
+++ b/solution.py
@@ -15,7 +15,7 @@
 JOIN_BANDS = 4
 STAGES = ((0, 1, 2), (3,), (4,))
 APART = 2
-WAITS = {"P2o": ("masked",), "P1x": ("P2o",), "Q1x": ("Q2o",), "Q2o": ("given",), "Q2x": ("other",), "Q3": ("left",), "P4": ("m0",), "m2": ("y0",)}
+WAITS = {"P2o": ('masked',), "P1x": ('P2o',), "Q1x": ('Q2o',), "Q2o": ('given',), "P4": ('m0',), "P2x": ('index', 'other'), "P3": ('Q2x', 'left'), "m1": ('y0',)}
 
 
 def in_hbm(value):
@@ -88,10 +88,12 @@
         copies.append(
             pltpu.make_async_copy(wave_ref.at[there], waves.at[there], arrived.at[count + n])
         )
-    for copy in copies:
+    for copy in copies[: count + 1]:
         copy.start()
     for copy in copies[:count]:
         copy.wait()
+    for copy in copies[count + 1 :]:
+        copy.start()
 
     def one_block(b, carry):
         local = index_ref[base + b]
@@ -114,7 +116,7 @@
 
     for n, copy in enumerate(copies[count:]):
         copy.wait()
-        lax.fori_loop(n * bands, (n + 1) * bands, one_block, 0, unroll=UNROLL)
+        lax.fori_loop(n * bands, (n + 1) * bands, one_block, 0, unroll=2 * UNROLL)
 
 
 def right_kernel(index_ref, *refs, lefts, spots, parties, stage, bases):
@@ -175,7 +177,7 @@
             out_refs[j][g] = value[j * rows : (j + 1) * rows].astype(out_refs[j].dtype)
         return carry
 
-    lax.fori_loop(0, slots // pack, one_group, 0, unroll=min(UNROLL, slots // pack))
+    lax.fori_loop(0, slots // pack, one_group, 0, unroll=min(2 * UNROLL, slots // pack))
 
 
 def join_kernel(index_ref, *refs, stages, bases):
@@ -332,7 +334,7 @@
     given = to_party(theirs, 1)
     other = to_party(masked, 1)
     lefts = left_products([masked, other])
-    done = {"given": [given], "other": [other], "left": lefts, "masked": [masked]}
+    done = {"given": [given], "other": [other], "left": lefts, "masked": [masked], "index": [index]}
 
     def launch(name, value):
         waits = [v for w in WAITS.get(name, ()) for v in done[w]]
@@ -369,7 +371,8 @@
                     if lane not in joined:
                         joined[lane] = jnp.concatenate([trail[APART, lane] for trail in trails], axis=0)
                     head = joined[lane] = launch("PQ"[lane] + str(number), joined[lane])
-                    found = [(0, head, 0), (0, swap_cores(head, owners), 1)]
+                    waits = [v for w in WAITS.get("S" + str(number) + "PQ"[lane], ()) for v in done[w]]
+                    found = [(0, head, 0), (0, swap_cores(after(head, *waits), owners), 1)]
                 for term, piece, q in found:
                     gathered.append(piece)
                     spots.append((term, (count + q) * sectors))

time: 87.6 us -> 84.1 us (0.960)
  starting transfers between devices: 27.2 us -> 22.3 us
  waiting for transfers between devices: 32.8 us -> 37.2 us
  Pallas kernels: 20.4 us -> 18.9 us
    ppermute x11, waiting for transfers between devices: 13 us -> 20.2 us  [step_round(): return lax.ppermute(value, 'sec', pairs)]
    ppermute x11, starting transfers between devices: 17 us -> 12.8 us  [step_round(): return lax.ppermute(value, 'sec', pairs)]
    ppermute x5, waiting for transfers between devices: 19.7 us -> 16.5 us  [to_party(): lax.ppermute(value, 'mpo', [(d, (d + j) % parties) for d in range(parties)])]
    ppermute x5, starting transfers between devices: 7.91 us -> 6.88 us  [to_party(): lax.ppermute(value, 'mpo', [(d, (d + j) % parties) for d in range(parties)])]
    pallas_call x3, Pallas kernels: 11.1 us -> 10.1 us  [right_products(): pl.pallas_call(functools.partial(right_kernel, lefts=len(lefts), spots=sp...]
  transfers between devices with their start and end apart: 29 -> 29, of which waited for: 11 -> 13; matrix products, arithmetic and copies ran while one was open for 6% -> 5% of each run, Pallas kernels for 20% -> 19%
where the time goes in v4:
time: 84.1 us; the launch traced here: 83.8 us
  waiting for transfers between devices  37.2 us (44%)
  starting transfers between devices  22.3 us (27%)
  Pallas kernels  18.9 us (22%)
  other arithmetic  2.68 us (3%)
  local copies, waits for them, and re-layouts  2.55 us (3%)
    ppermute x11, waiting for transfers between devices, step_round(): return lax.ppermute(value, 'sec', pairs)  20.2 us
    ppermute x5, waiting for transfers between devices, to_party(): lax.ppermute(value, 'mpo', [(d, (d + j) % parties) for d in range(parties)])  16.5 us
    ppermute x11, starting transfers between devices, step_round(): return lax.ppermute(value, 'sec', pairs)  12.8 us
    pallas_call x3, Pallas kernels, right_products(): pl.pallas_call(functools.partial(right_kernel, lefts=len(lefts), spots=sp...  10.1 us
    ppermute x5, starting transfers between devices, to_party(): lax.ppermute(value, 'mpo', [(d, (d + j) % parties) for d in range(parties)])  6.88 us
    pallas_call x1, Pallas kernels, left_products(): pl.pallas_call(functools.partial(left_kernel, parties=parties, count=len(...  5.53 us
    pallas_call x1, Pallas kernels, on_device(): pl.pallas_call(functools.partial(join_kernel, stages=len(kept), bases=(st...  3.28 us
    ppermute x13, starting transfers between devices, swap_cores(): return lax.ppermute(value, 'sec', [(d, d ^ 1) for d in range(owners)])  2.63 us
  transfers between devices with their start and end apart: 29, of which 13 were waited for; matrix products, arithmetic and copies ran while one was open for 5% of the time, Pallas kernels for 19%

profile of v4, /device:TPU:0, one launch (start us, length us, event | category | flops | bytes accessed | tf_op | source)
XLA Modules:
  0.0 83.8 jit_solution(6405789055828642429)
XLA Ops:
  0.0 1.1 %constant_dynamic-slice_fusion = (bf16[2,10,64,128]{3,2,1,0:T(8,128)(2,1)S(1)}, bf16[2,10,64,128]{3,2,1,0:T(8,128)(2,1)S(1)}) fusion(bf16[2,10,128,128]{3,2,1,0:T(8,128)(2,1)} %param.12, s32[]{:T(128)S(6)} %select_n.17, s32[]{:T(128)S(6)} %select_n.16), kind=kLoop, calls=%fused_computation.4 | loop fusion | bytes 1310728 | tf_op jit(solution)/shard_map/dynamic_slice | solution.py:333
  1.1 0.5 collective-permute-start.1
  1.6 2.6 %collective-permute-start.4 = (bf16[2,10,64,128]{3,2,1,0:T(8,128)(2,1)S(1)}, bf16[2,10,64,128]{3,2,1,0:T(8,128)(2,1)S(1)}, u32[]{:S(2)}, u32[]{:S(2)}) collective-permute-start(bf16[2,10,64,128]{3,2,1,0:T(8,128)(2,1)S(1)} %get-tuple-element.38.refs_2_), channel_id=1, source_target_pairs={{0,8},{2,6},{4,0},{6,14},{8,16},{10,2},{12,4},{14,22},{16,24},{18,... | collective-permute-start | bytes 983048 | tf_op jit(solution)/shard_map/ppermute | solution.py:45
  4.3 1.5 %collective-permute-start.2 = (bf16[2,10,64,128]{3,2,1,0:T(8,128)(2,1)S(1)}, bf16[2,10,64,128]{3,2,1,0:T(8,128)(2,1)S(1)}, u32[]{:S(2)}, u32[]{:S(2)}) collective-permute-start(bf16[2,10,64,128]{3,2,1,0:T(8,128)(2,1)S(1)} %get-tuple-element.37), channel_id=1, source_target_pairs={{0,1},{1,0},{2,3},{3,2},{4,5},{5,4},{6,7},{7,6},{8,9},{9,8},{10,11... | collective-permute-start | bytes 983048 | tf_op jit(solution)/shard_map/ppermute | solution.py:239
  5.8 0.7 convert_element_type.3
  6.5 1.6 %collective-permute-start.9 = (bf16[2,10,64,128]{3,2,1,0:T(8,128)(2,1)S(1)}, bf16[2,10,64,128]{3,2,1,0:T(8,128)(2,1)S(1)}, u32[]{:S(2)}, u32[]{:S(2)}) collective-permute-start(bf16[2,10,64,128]{3,2,1,0:T(8,128)(2,1)S(1)} %collective-permute-done.1.refs_3_), channel_id=1, source_target_pairs={{0,8},{2,6},{4,0},{6,14},{8,16},{10,2},{12,4},{14,22},{16,24},{18,... | collective-permute-start | bytes 983048 | tf_op jit(solution)/shard_map/ppermute | solution.py:45
  8.1 1.2 %broadcast_multiply_fusion.refs_0_ = bf16[2,10,128,128]{3,2,1,0:T(8,128)(2,1)S(1)} fusion(bf16[2,10,128,128]{3,2,1,0:T(8,128)(2,1)} %param.11, bf16[2,10]{1,0:T(2,128)(2,1)S(1)} %convert_element_type.3), kind=kLoop, calls=%fused_computation.2 | loop fusion | flops 327680 | bytes 1310760 | tf_op jit(solution)/shard_map/mul | solution.py:320
  9.3 2.1 %collective-permute-start.6 = (bf16[2,10,64,128]{3,2,1,0:T(8,128)(2,1)S(1)}, bf16[2,10,64,128]{3,2,1,0:T(8,128)(2,1)S(1)}, u32[]{:S(2)}, u32[]{:S(2)}) collective-permute-start(bf16[2,10,64,128]{3,2,1,0:T(8,128)(2,1)S(1)} %collective-permute-done.4.refs_6_), channel_id=1, source_target_pairs={{0,8},{2,6},{4,0},{6,14},{8,16},{10,2},{12,4},{14,22},{16,24},{18,... | collective-permute-start | bytes 983048 | tf_op jit(solution)/shard_map/ppermute | solution.py:45
  11.4 1.5 %collective-permute-start = (bf16[2,10,128,128]{3,2,1,0:T(8,128)(2,1)S(1)}, bf16[2,10,128,128]{3,2,1,0:T(8,128)(2,1)}, u32[]{:S(2)}, u32[]{:S(2)}) collective-permute-start(bf16[2,10,128,128]{3,2,1,0:T(8,128)(2,1)S(1)} %broadcast_multiply_fusion.refs_0_), channel_id=1, source_target_pairs={{0,1},{1,0},{2,3},{3,2},{4,5},{5,4},{6,7},{7,6},{8,9},{9,8},{10,11... | collective-permute-start | bytes 1966088 | tf_op jit(solution)/shard_map/ppermute | solution.py:239
  12.9 1.8 %collective-permute-done.2.refs_4_ = bf16[2,10,64,128]{3,2,1,0:T(8,128)(2,1)S(1)} collective-permute-done((bf16[2,10,64,128]{3,2,1,0:T(8,128)(2,1)S(1)}, bf16[2,10,64,128]{3,2,1,0:T(8,128)(2,1)S(1)}, u32[]{:S(2)}, u32[]{:S(2)}) %collective-permute-start.2) | collective-permute-done | bytes 327712 | tf_op jit(solution)/shard_map/ppermute | solution.py:239
  14.7 0.4 collective-permute-start.11
  15.1 1.9 %collective-permute-done.6.refs_14_ = bf16[2,10,64,128]{3,2,1,0:T(8,128)(2,1)S(1)} collective-permute-done((bf16[2,10,64,128]{3,2,1,0:T(8,128)(2,1)S(1)}, bf16[2,10,64,128]{3,2,1,0:T(8,128)(2,1)S(1)}, u32[]{:S(2)}, u32[]{:S(2)}) %collective-permute-start.6) | collective-permute-done | bytes 327712 | tf_op jit(solution)/shard_map/ppermute | solution.py:45
  17.1 1.6 %collective-permute-start.7 = (bf16[2,10,64,128]{3,2,1,0:T(8,128)(2,1)S(1)}, bf16[2,10,64,128]{3,2,1,0:T(8,128)(2,1)}, u32[]{:S(2)}, u32[]{:S(2)}) collective-permute-start(bf16[2,10,64,128]{3,2,1,0:T(8,128)(2,1)S(1)} %collective-permute-done.2.refs_4_), channel_id=1, source_target_pairs={{0,8},{2,6},{4,0},{6,14},{8,16},{10,2},{12,4},{14,22},{16,24},{18,... | collective-permute-start | bytes 983048 | tf_op jit(solution)/shard_map/ppermute | solution.py:45
  18.7 0.7 fusion
  19.3 2.4 %collective-permute-done.11.refs_18_ = bf16[2,10,64,128]{3,2,1,0:T(8,128)(2,1)S(1)} collective-permute-done((bf16[2,10,64,128]{3,2,1,0:T(8,128)(2,1)S(1)}, bf16[2,10,64,128]{3,2,1,0:T(8,128)(2,1)S(1)}, u32[]{:S(2)}, u32[]{:S(2)}) %collective-permute-start.11) | collective-permute-done | bytes 327712 | tf_op jit(solution)/shard_map/ppermute | solution.py:45
  21.8 0.4 collective-permute-start.12
  22.2 0.7 and_select_fusion
  22.9 0.7 concatenate.9.index_ref
  23.6 4.5 %collective-permute-done.refs_1_ = bf16[2,10,128,128]{3,2,1,0:T(8,128)(2,1)} collective-permute-done((bf16[2,10,128,128]{3,2,1,0:T(8,128)(2,1)S(1)}, bf16[2,10,128,128]{3,2,1,0:T(8,128)(2,1)}, u32[]{:S(2)}, u32[]{:S(2)}) %collective-permute-start) | collective-permute-done | bytes 655392 | tf_op jit(solution)/shard_map/ppermute | solution.py:239
  28.1 0.4 collective-permute-start.15
  28.5 0.5 collective-permute-done.12.refs_12_
  29.0 1.3 %collective-permute-start.18 = (bf16[2,10,64,128]{3,2,1,0:T(8,128)(2,1)}, bf16[2,10,64,128]{3,2,1,0:T(8,128)(2,1)S(1)}, u32[]{:S(2)}, u32[]{:S(2)}) collective-permute-start(bf16[2,10,64,128]{3,2,1,0:T(8,128)(2,1)} %collective-permute-done.12.refs_12_), channel_id=1, source_target_pairs={{0,8},{2,6},{4,0},{6,14},{8,16},{10,2},{12,4},{14,22},{16,24},{18,... | collective-permute-start | bytes 983048 | tf_op jit(solution)/shard_map/ppermute | solution.py:45
  30.2 0.2 collective-permute-start.5
  30.4 0.4 collective-permute-start.10
  30.8 0.2 collective-permute-start.14
  30.9 5.5 %left_products.1 = (bf16[80,128,256]{2,1,0:T(8,128)(2,1)S(1)}, bf16[80,128,256]{2,1,0:T(8,128)(2,1)S(1)}) custom-call(s32[305]{0:T(512)S(1)} %concatenate.9.index_ref, bf16[2,10,128,128]{3,2,1,0:T(8,128)(2,1)S(1)} %broadcast_multiply_fusion.refs_0_, bf16[2,10,128,128]{3,2,1,0:T(8,128)(2,1)} %collective-permute-done.refs_1_, bf16[80,128,128]{2,1,0:T(8,128)(2,1)} %refs_2_.1), custom_call_target="tpu_custom_call" | custom-call | flops 1342177280 | bytes 9437184 | tf_op jit(solution)/shard_map/left_products/pallas_call | solution.py:269
  36.5 0.4 collective-permute-start.8
  36.9 2.0 %collective-permute-done.18.refs_20_ = bf16[2,10,64,128]{3,2,1,0:T(8,128)(2,1)S(1)} collective-permute-done((bf16[2,10,64,128]{3,2,1,0:T(8,128)(2,1)}, bf16[2,10,64,128]{3,2,1,0:T(8,128)(2,1)S(1)}, u32[]{:S(2)}, u32[]{:S(2)}) %collective-permute-start.18) | collective-permute-done | bytes 327712 | tf_op jit(solution)/shard_map/ppermute | solution.py:45
  38.9 0.4 collective-permute-start.20
  39.3 0.5 collective-permute-start.13
  39.8 0.1 collective-permute-start.16
  39.9 0.4 collective-permute-start.19
  40.4 0.5 collective-permute-done.17.refs_19_
  40.9 1.7 %collective-permute-start.23 = (bf16[4,10,64,128]{3,2,1,0:T(8,128)(2,1)S(1)}, bf16[4,10,64,128]{3,2,1,0:T(8,128)(2,1)S(1)}, u32[]{:S(2)}, u32[]{:S(2)}) collective-permute-start(bf16[4,10,64,128]{3,2,1,0:T(8,128)(2,1)S(1)} %pad_maximum_fusion.1), channel_id=1, source_target_pairs={{0,8},{2,6},{4,0},{6,14},{8,16},{10,2},{12,4},{14,22},{16,24},{18,... | collective-permute-start | bytes 1966088 | tf_op jit(solution)/shard_map/ppermute | solution.py:45
  42.7 5.5 %right_products.3 = (bf16[40,64,128]{2,1,0:T(8,128)(2,1)S(1)}, bf16[40,64,128]{2,1,0:T(8,128)(2,1)S(1)}) custom-call(s32[305]{0:T(512)S(1)} %concatenate.9.index_ref, bf16[80,128,256]{2,1,0:T(8,128)(2,1)S(1)} %get-tuple-element.21.refs_0_, bf16[80,128,256]{2,1,0:T(8,128)(2,1)S(1)} %get-tuple-element.22.refs_1_, ...), custom_call_target="tpu_custom_call" | custom-call | flops 671088640 | bytes 12582912 | tf_op jit(solution)/shard_map/right_products/pallas_call | solution.py:293
  48.2 1.3 %collective-permute-done.20.refs_2_ = bf16[4,10,64,128]{3,2,1,0:T(8,128)(2,1)S(1)} collective-permute-done((bf16[4,10,64,128]{3,2,1,0:T(8,128)(2,1)S(1)}, bf16[4,10,64,128]{3,2,1,0:T(8,128)(2,1)S(1)}, u32[]{:S(2)}, u32[]{:S(2)}) %collective-permute-start.20) | collective-permute-done | bytes 655392 | tf_op jit(solution)/shard_map/ppermute | solution.py:45
  49.5 0.4 collective-permute-start.25
  49.9 1.7 %collective-permute-start.21 = (bf16[40,64,128]{2,1,0:T(8,128)(2,1)S(1)}, bf16[40,64,128]{2,1,0:T(8,128)(2,1)S(1)}, u32[]{:S(2)}, u32[]{:S(2)}) collective-permute-start(bf16[40,64,128]{2,1,0:T(8,128)(2,1)S(1)} %get-tuple-element.30), channel_id=1, source_target_pairs={{0,1},{1,0},{2,3},{3,2},{4,5},{5,4},{6,7},{7,6},{8,9},{9,8},{10,11... | collective-permute-start | bytes 1966088 | tf_op jit(solution)/shard_map/ppermute | solution.py:239
  51.6 5.0 %collective-permute-done.23.refs_4_ = bf16[4,10,64,128]{3,2,1,0:T(8,128)(2,1)S(1)} collective-permute-done((bf16[4,10,64,128]{3,2,1,0:T(8,128)(2,1)S(1)}, bf16[4,10,64,128]{3,2,1,0:T(8,128)(2,1)S(1)}, u32[]{:S(2)}, u32[]{:S(2)}) %collective-permute-start.23) | collective-permute-done | bytes 655392 | tf_op jit(solution)/shard_map/ppermute | solution.py:45
  56.5 7.0 %collective-permute-done.25.refs_2_ = bf16[4,10,64,128]{3,2,1,0:T(8,128)(2,1)S(1)} collective-permute-done((bf16[4,10,64,128]{3,2,1,0:T(8,128)(2,1)S(1)}, bf16[4,10,64,128]{3,2,1,0:T(8,128)(2,1)S(1)}, u32[]{:S(2)}, u32[]{:S(2)}) %collective-permute-start.25) | collective-permute-done | bytes 655392 | tf_op jit(solution)/shard_map/ppermute | solution.py:45
  63.6 2.5 %collective-permute-done.21.refs_3_ = bf16[40,64,128]{2,1,0:T(8,128)(2,1)S(1)} collective-permute-done((bf16[40,64,128]{2,1,0:T(8,128)(2,1)S(1)}, bf16[40,64,128]{2,1,0:T(8,128)(2,1)S(1)}, u32[]{:S(2)}, u32[]{:S(2)}) %collective-permute-start.21) | collective-permute-done | bytes 655392 | tf_op jit(solution)/shard_map/ppermute | solution.py:239
  66.0 2.8 %right_products.4 = (bf16[20,64,128]{2,1,0:T(8,128)(2,1)S(1)}, bf16[20,64,128]{2,1,0:T(8,128)(2,1)S(1)}) custom-call(s32[305]{0:T(512)S(1)} %concatenate.9.index_ref, bf16[80,128,256]{2,1,0:T(8,128)(2,1)S(1)} %get-tuple-element.21.refs_0_, bf16[80,128,256]{2,1,0:T(8,128)(2,1)S(1)} %get-tuple-element.22.refs_1_, ...), custom_call_target="tpu_custom_call" | custom-call | flops 335544320 | bytes 12582912 | tf_op jit(solution)/shard_map/right_products/pallas_call | solution.py:293
  68.8 1.6 %collective-permute-start.27 = (bf16[20,64,128]{2,1,0:T(8,128)(2,1)S(1)}, bf16[20,64,128]{2,1,0:T(8,128)(2,1)S(1)}, u32[]{:S(2)}, u32[]{:S(2)}) collective-permute-start(bf16[20,64,128]{2,1,0:T(8,128)(2,1)S(1)} %get-tuple-element.35), channel_id=1, source_target_pairs={{0,1},{1,0},{2,3},{3,2},{4,5},{5,4},{6,7},{7,6},{8,9},{9,8},{10,11... | collective-permute-start | bytes 983048 | tf_op jit(solution)/shard_map/ppermute | solution.py:239
  70.4 1.9 %right_products.5 = (bf16[10,64,128]{2,1,0:T(8,128)(2,1)S(1)}, bf16[10,64,128]{2,1,0:T(8,128)(2,1)S(1)}) custom-call(s32[305]{0:T(512)S(1)} %concatenate.9.index_ref, bf16[80,128,256]{2,1,0:T(8,128)(2,1)S(1)} %get-tuple-element.21.refs_0_, bf16[80,128,256]{2,1,0:T(8,128)(2,1)S(1)} %get-tuple-element.22.refs_1_, ...), custom_call_target="tpu_custom_call" | custom-call | flops 167772160 | bytes 12582912 | tf_op jit(solution)/shard_map/right_products/pallas_call | solution.py:293
  72.3 0.6 collective-permute-start.28
  72.8 6.0 %collective-permute-done.27.refs_4_ = bf16[20,64,128]{2,1,0:T(8,128)(2,1)S(1)} collective-permute-done((bf16[20,64,128]{2,1,0:T(8,128)(2,1)S(1)}, bf16[20,64,128]{2,1,0:T(8,128)(2,1)S(1)}, u32[]{:S(2)}, u32[]{:S(2)}) %collective-permute-start.27) | collective-permute-done | bytes 327712 | tf_op jit(solution)/shard_map/ppermute | solution.py:239
  78.8 1.8 %collective-permute-done.28.refs_5_ = bf16[10,64,128]{2,1,0:T(8,128)(2,1)S(1)} collective-permute-done((bf16[10,64,128]{2,1,0:T(8,128)(2,1)S(1)}, bf16[10,64,128]{2,1,0:T(8,128)(2,1)S(1)}, u32[]{:S(2)}, u32[]{:S(2)}) %collective-permute-start.28) | collective-permute-done | bytes 163872 | tf_op jit(solution)/shard_map/ppermute | solution.py:239
  80.5 3.3 %join_columns.1 = bf16[80,64,128]{2,1,0:T(8,128)(2,1)} custom-call(s32[305]{0:T(512)S(1)} %concatenate.9.index_ref, bf16[40,64,128]{2,1,0:T(8,128)(2,1)S(1)} %get-tuple-element.28.refs_0_, bf16[20,64,128]{2,1,0:T(8,128)(2,1)S(1)} %get-tuple-element.32.refs_1_, bf16[10,64,128]{2,1,0:T(8,128)(2,1)S(1)} %get-tuple-element.34.refs_2_, ...), custom_call_target="tpu_custom_call" | custom-call | bytes 4194304 | tf_op jit(solution)/shard_map/join_columns/pallas_call | solution.py:389
  (23 shorter events, 0.2 us)
Async XLA Ops:
  1.1 5.4 %collective-permute-start.1 = (bf16[2,10,64,128]{3,2,1,0:T(8,128)(2,1)S(1)}, bf16[2,10,64,128]{3,2,1,0:T(8,128)(2,1)S(1)}, u32[]{:S(2)}, u32[]{:S(2)}) collective-permute-start(bf16[2,10,64,128]{3,2,1,0:T(8,128)(2,1)S(1)} %get-tuple-element.38.refs_2_), channel_id=1, source_target_pairs={{0,2},{2,0},{4,6},{6,4},{8,10},{10,8},{12,14},{14,12},{16,18},{18,... | collective-permute-start | bytes 983048 | tf_op jit(solution)/shard_map/ppermute | solution.py:37
  1.6 7.6 %collective-permute-start.4 = (bf16[2,10,64,128]{3,2,1,0:T(8,128)(2,1)S(1)}, bf16[2,10,64,128]{3,2,1,0:T(8,128)(2,1)S(1)}, u32[]{:S(2)}, u32[]{:S(2)}) collective-permute-start(bf16[2,10,64,128]{3,2,1,0:T(8,128)(2,1)S(1)} %get-tuple-element.38.refs_2_), channel_id=1, source_target_pairs={{0,8},{2,6},{4,0},{6,14},{8,16},{10,2},{12,4},{14,22},{16,24},{18,... | collective-permute-start | bytes 983048 | tf_op jit(solution)/shard_map/ppermute | solution.py:45
  4.3 10.4 %collective-permute-start.2 = (bf16[2,10,64,128]{3,2,1,0:T(8,128)(2,1)S(1)}, bf16[2,10,64,128]{3,2,1,0:T(8,128)(2,1)S(1)}, u32[]{:S(2)}, u32[]{:S(2)}) collective-permute-start(bf16[2,10,64,128]{3,2,1,0:T(8,128)(2,1)S(1)} %get-tuple-element.37), channel_id=1, source_target_pairs={{0,1},{1,0},{2,3},{3,2},{4,5},{5,4},{6,7},{7,6},{8,9},{9,8},{10,11... | collective-permute-start | bytes 983048 | tf_op jit(solution)/shard_map/ppermute | solution.py:239
  6.5 8.2 %collective-permute-start.9 = (bf16[2,10,64,128]{3,2,1,0:T(8,128)(2,1)S(1)}, bf16[2,10,64,128]{3,2,1,0:T(8,128)(2,1)S(1)}, u32[]{:S(2)}, u32[]{:S(2)}) collective-permute-start(bf16[2,10,64,128]{3,2,1,0:T(8,128)(2,1)S(1)} %collective-permute-done.1.refs_3_), channel_id=1, source_target_pairs={{0,8},{2,6},{4,0},{6,14},{8,16},{10,2},{12,4},{14,22},{16,24},{18,... | collective-permute-start | bytes 983048 | tf_op jit(solution)/shard_map/ppermute | solution.py:45
  9.3 7.8 %collective-permute-start.6 = (bf16[2,10,64,128]{3,2,1,0:T(8,128)(2,1)S(1)}, bf16[2,10,64,128]{3,2,1,0:T(8,128)(2,1)S(1)}, u32[]{:S(2)}, u32[]{:S(2)}) collective-permute-start(bf16[2,10,64,128]{3,2,1,0:T(8,128)(2,1)S(1)} %collective-permute-done.4.refs_6_), channel_id=1, source_target_pairs={{0,8},{2,6},{4,0},{6,14},{8,16},{10,2},{12,4},{14,22},{16,24},{18,... | collective-permute-start | bytes 983048 | tf_op jit(solution)/shard_map/ppermute | solution.py:45
  11.4 16.8 %collective-permute-start = (bf16[2,10,128,128]{3,2,1,0:T(8,128)(2,1)S(1)}, bf16[2,10,128,128]{3,2,1,0:T(8,128)(2,1)}, u32[]{:S(2)}, u32[]{:S(2)}) collective-permute-start(bf16[2,10,128,128]{3,2,1,0:T(8,128)(2,1)S(1)} %broadcast_multiply_fusion.refs_0_), channel_id=1, source_target_pairs={{0,1},{1,0},{2,3},{3,2},{4,5},{5,4},{6,7},{7,6},{8,9},{9,8},{10,11... | collective-permute-start | bytes 1966088 | tf_op jit(solution)/shard_map/ppermute | solution.py:239
  14.7 4.6 %collective-permute-start.3 = (bf16[2,10,64,128]{3,2,1,0:T(8,128)(2,1)S(1)}, bf16[2,10,64,128]{3,2,1,0:T(8,128)(2,1)S(1)}, u32[]{:S(2)}, u32[]{:S(2)}) collective-permute-start(bf16[2,10,64,128]{3,2,1,0:T(8,128)(2,1)S(1)} %collective-permute-done.2.refs_4_), channel_id=1, source_target_pairs={{0,2},{2,0},{4,6},{6,4},{8,10},{10,8},{12,14},{14,12},{16,18},{18,... | collective-permute-start | bytes 983048 | tf_op jit(solution)/shard_map/ppermute | solution.py:37
  14.7 7.1 %collective-permute-start.11 = (bf16[2,10,64,128]{3,2,1,0:T(8,128)(2,1)S(1)}, bf16[2,10,64,128]{3,2,1,0:T(8,128)(2,1)S(1)}, u32[]{:S(2)}, u32[]{:S(2)}) collective-permute-start(bf16[2,10,64,128]{3,2,1,0:T(8,128)(2,1)S(1)} %collective-permute-done.9.refs_10_), channel_id=1, source_target_pairs={{0,8},{2,6},{4,0},{6,14},{8,16},{10,2},{12,4},{14,22},{16,24},{18,... | collective-permute-start | bytes 983048 | tf_op jit(solution)/shard_map/ppermute | solution.py:45
  17.1 11.1 %collective-permute-start.7 = (bf16[2,10,64,128]{3,2,1,0:T(8,128)(2,1)S(1)}, bf16[2,10,64,128]{3,2,1,0:T(8,128)(2,1)}, u32[]{:S(2)}, u32[]{:S(2)}) collective-permute-start(bf16[2,10,64,128]{3,2,1,0:T(8,128)(2,1)S(1)} %collective-permute-done.2.refs_4_), channel_id=1, source_target_pairs={{0,8},{2,6},{4,0},{6,14},{8,16},{10,2},{12,4},{14,22},{16,24},{18,... | collective-permute-start | bytes 983048 | tf_op jit(solution)/shard_map/ppermute | solution.py:45
  21.8 7.2 %collective-permute-start.12 = (bf16[2,10,64,128]{3,2,1,0:T(8,128)(2,1)S(1)}, bf16[2,10,64,128]{3,2,1,0:T(8,128)(2,1)}, u32[]{:S(2)}, u32[]{:S(2)}) collective-permute-start(bf16[2,10,64,128]{3,2,1,0:T(8,128)(2,1)S(1)} %collective-permute-done.3.refs_5_), channel_id=1, source_target_pairs={{0,8},{2,6},{4,0},{6,14},{8,16},{10,2},{12,4},{14,22},{16,24},{18,... | collective-permute-start | bytes 983048 | tf_op jit(solution)/shard_map/ppermute | solution.py:45
  28.1 8.3 %collective-permute-start.15 = (bf16[2,10,64,128]{3,2,1,0:T(8,128)(2,1)}, bf16[2,10,64,128]{3,2,1,0:T(8,128)(2,1)S(1)}, u32[]{:S(2)}, u32[]{:S(2)}) collective-permute-start(bf16[2,10,64,128]{3,2,1,0:T(8,128)(2,1)} %collective-permute-done.7.refs_8_), channel_id=1, source_target_pairs={{0,8},{2,6},{4,0},{6,14},{8,16},{10,2},{12,4},{14,22},{16,24},{18,... | collective-permute-start | bytes 983048 | tf_op jit(solution)/shard_map/ppermute | solution.py:45
  29.0 10.0 %collective-permute-start.18 = (bf16[2,10,64,128]{3,2,1,0:T(8,128)(2,1)}, bf16[2,10,64,128]{3,2,1,0:T(8,128)(2,1)S(1)}, u32[]{:S(2)}, u32[]{:S(2)}) collective-permute-start(bf16[2,10,64,128]{3,2,1,0:T(8,128)(2,1)} %collective-permute-done.12.refs_12_), channel_id=1, source_target_pairs={{0,8},{2,6},{4,0},{6,14},{8,16},{10,2},{12,4},{14,22},{16,24},{18,... | collective-permute-start | bytes 983048 | tf_op jit(solution)/shard_map/ppermute | solution.py:45
  30.2 9.1 %collective-permute-start.5 = (bf16[2,10,64,128]{3,2,1,0:T(8,128)(2,1)S(1)}, bf16[2,10,64,128]{3,2,1,0:T(8,128)(2,1)S(1)}, u32[]{:S(2)}, u32[]{:S(2)}) collective-permute-start(bf16[2,10,64,128]{3,2,1,0:T(8,128)(2,1)S(1)} %collective-permute-done.4.refs_6_), channel_id=1, source_target_pairs={{0,2},{2,0},{4,6},{6,4},{8,10},{10,8},{12,14},{14,12},{16,18},{18,... | collective-permute-start | bytes 983048 | tf_op jit(solution)/shard_map/ppermute | solution.py:37
  30.4 8.9 %collective-permute-start.10 = (bf16[2,10,64,128]{3,2,1,0:T(8,128)(2,1)S(1)}, bf16[2,10,64,128]{3,2,1,0:T(8,128)(2,1)S(1)}, u32[]{:S(2)}, u32[]{:S(2)}) collective-permute-start(bf16[2,10,64,128]{3,2,1,0:T(8,128)(2,1)S(1)} %collective-permute-done.9.refs_10_), channel_id=1, source_target_pairs={{0,2},{2,0},{4,6},{6,4},{8,10},{10,8},{12,14},{14,12},{16,18},{18,... | collective-permute-start | bytes 983048 | tf_op jit(solution)/shard_map/ppermute | solution.py:37
  30.8 9.1 %collective-permute-start.14 = (bf16[2,10,64,128]{3,2,1,0:T(8,128)(2,1)S(1)}, bf16[2,10,64,128]{3,2,1,0:T(8,128)(2,1)S(1)}, u32[]{:S(2)}, u32[]{:S(2)}) collective-permute-start(bf16[2,10,64,128]{3,2,1,0:T(8,128)(2,1)S(1)} %collective-permute-done.6.refs_14_), channel_id=1, source_target_pairs={{0,2},{2,0},{4,6},{6,4},{8,10},{10,8},{12,14},{14,12},{16,18},{18,... | collective-permute-start | bytes 983048 | tf_op jit(solution)/shard_map/ppermute | solution.py:37
  36.5 3.4 %collective-permute-start.8 = (bf16[2,10,64,128]{3,2,1,0:T(8,128)(2,1)}, bf16[2,10,64,128]{3,2,1,0:T(8,128)(2,1)S(1)}, u32[]{:S(2)}, u32[]{:S(2)}) collective-permute-start(bf16[2,10,64,128]{3,2,1,0:T(8,128)(2,1)} %collective-permute-done.7.refs_8_), channel_id=1, source_target_pairs={{0,2},{2,0},{4,6},{6,4},{8,10},{10,8},{12,14},{14,12},{16,18},{18,... | collective-permute-start | bytes 983048 | tf_op jit(solution)/shard_map/ppermute | solution.py:37
  38.9 10.6 %collective-permute-start.20 = (bf16[4,10,64,128]{3,2,1,0:T(8,128)(2,1)S(1)}, bf16[4,10,64,128]{3,2,1,0:T(8,128)(2,1)S(1)}, u32[]{:S(2)}, u32[]{:S(2)}) collective-permute-start(bf16[4,10,64,128]{3,2,1,0:T(8,128)(2,1)S(1)} %pad_maximum_fusion), channel_id=1, source_target_pairs={{0,8},{2,6},{4,0},{6,14},{8,16},{10,2},{12,4},{14,22},{16,24},{18,... | collective-permute-start | bytes 1966088 | tf_op jit(solution)/shard_map/ppermute | solution.py:45
  39.3 1.6 %collective-permute-start.17 = (bf16[2,10,64,128]{3,2,1,0:T(8,128)(2,1)S(1)}, bf16[2,10,64,128]{3,2,1,0:T(8,128)(2,1)S(1)}, u32[]{:S(2)}, u32[]{:S(2)}) collective-permute-start(bf16[2,10,64,128]{3,2,1,0:T(8,128)(2,1)S(1)} %collective-permute-done.11.refs_18_), channel_id=1, source_target_pairs={{0,2},{2,0},{4,6},{6,4},{8,10},{10,8},{12,14},{14,12},{16,18},{18,... | collective-permute-start | bytes 983048 | tf_op jit(solution)/shard_map/ppermute | solution.py:37
  39.3 3.4 %collective-permute-start.13 = (bf16[2,10,64,128]{3,2,1,0:T(8,128)(2,1)}, bf16[2,10,64,128]{3,2,1,0:T(8,128)(2,1)S(1)}, u32[]{:S(2)}, u32[]{:S(2)}) collective-permute-start(bf16[2,10,64,128]{3,2,1,0:T(8,128)(2,1)} %collective-permute-done.12.refs_12_), channel_id=1, source_target_pairs={{0,2},{2,0},{4,6},{6,4},{8,10},{10,8},{12,14},{14,12},{16,18},{18,... | collective-permute-start | bytes 983048 | tf_op jit(solution)/shard_map/ppermute | solution.py:37
  39.8 2.9 %collective-permute-start.16 = (bf16[2,10,64,128]{3,2,1,0:T(8,128)(2,1)S(1)}, bf16[2,10,64,128]{3,2,1,0:T(8,128)(2,1)S(1)}, u32[]{:S(2)}, u32[]{:S(2)}) collective-permute-start(bf16[2,10,64,128]{3,2,1,0:T(8,128)(2,1)S(1)} %collective-permute-done.15.refs_16_), channel_id=1, source_target_pairs={{0,2},{2,0},{4,6},{6,4},{8,10},{10,8},{12,14},{14,12},{16,18},{18,... | collective-permute-start | bytes 983048 | tf_op jit(solution)/shard_map/ppermute | solution.py:37
  39.9 2.8 %collective-permute-start.19 = (bf16[2,10,64,128]{3,2,1,0:T(8,128)(2,1)S(1)}, bf16[2,10,64,128]{3,2,1,0:T(8,128)(2,1)S(1)}, u32[]{:S(2)}, u32[]{:S(2)}) collective-permute-start(bf16[2,10,64,128]{3,2,1,0:T(8,128)(2,1)S(1)} %collective-permute-done.18.refs_20_), channel_id=1, source_target_pairs={{0,2},{2,0},{4,6},{6,4},{8,10},{10,8},{12,14},{14,12},{16,18},{18,... | collective-permute-start | bytes 983048 | tf_op jit(solution)/shard_map/ppermute | solution.py:37
  40.9 15.6 %collective-permute-start.23 = (bf16[4,10,64,128]{3,2,1,0:T(8,128)(2,1)S(1)}, bf16[4,10,64,128]{3,2,1,0:T(8,128)(2,1)S(1)}, u32[]{:S(2)}, u32[]{:S(2)}) collective-permute-start(bf16[4,10,64,128]{3,2,1,0:T(8,128)(2,1)S(1)} %pad_maximum_fusion.1), channel_id=1, source_target_pairs={{0,8},{2,6},{4,0},{6,14},{8,16},{10,2},{12,4},{14,22},{16,24},{18,... | collective-permute-start | bytes 1966088 | tf_op jit(solution)/shard_map/ppermute | solution.py:45
  49.5 14.0 %collective-permute-start.25 = (bf16[4,10,64,128]{3,2,1,0:T(8,128)(2,1)S(1)}, bf16[4,10,64,128]{3,2,1,0:T(8,128)(2,1)S(1)}, u32[]{:S(2)}, u32[]{:S(2)}) collective-permute-start(bf16[4,10,64,128]{3,2,1,0:T(8,128)(2,1)S(1)} %collective-permute-done.20.refs_2_), channel_id=1, source_target_pairs={{0,8},{2,6},{4,0},{6,14},{8,16},{10,2},{12,4},{14,22},{16,24},{18,... | collective-permute-start | bytes 1966088 | tf_op jit(solution)/shard_map/ppermute | solution.py:45
  49.9 16.1 %collective-permute-start.21 = (bf16[40,64,128]{2,1,0:T(8,128)(2,1)S(1)}, bf16[40,64,128]{2,1,0:T(8,128)(2,1)S(1)}, u32[]{:S(2)}, u32[]{:S(2)}) collective-permute-start(bf16[40,64,128]{2,1,0:T(8,128)(2,1)S(1)} %get-tuple-element.30), channel_id=1, source_target_pairs={{0,1},{1,0},{2,3},{3,2},{4,5},{5,4},{6,7},{7,6},{8,9},{9,8},{10,11... | collective-permute-start | bytes 1966088 | tf_op jit(solution)/shard_map/ppermute | solution.py:239
  51.6 14.4 %collective-permute-start.22 = (bf16[4,10,64,128]{3,2,1,0:T(8,128)(2,1)S(1)}, bf16[4,10,64,128]{3,2,1,0:T(8,128)(2,1)S(1)}, u32[]{:S(2)}, u32[]{:S(2)}) collective-permute-start(bf16[4,10,64,128]{3,2,1,0:T(8,128)(2,1)S(1)} %collective-permute-done.20.refs_2_), channel_id=1, source_target_pairs={{0,2},{2,0},{4,6},{6,4},{8,10},{10,8},{12,14},{14,12},{16,18},{18,... | collective-permute-start | bytes 1966088 | tf_op jit(solution)/shard_map/ppermute | solution.py:37
  56.5 9.5 %collective-permute-start.24 = (bf16[4,10,64,128]{3,2,1,0:T(8,128)(2,1)S(1)}, bf16[4,10,64,128]{3,2,1,0:T(8,128)(2,1)S(1)}, u32[]{:S(2)}, u32[]{:S(2)}) collective-permute-start(bf16[4,10,64,128]{3,2,1,0:T(8,128)(2,1)S(1)} %collective-permute-done.23.refs_4_), channel_id=1, source_target_pairs={{0,2},{2,0},{4,6},{6,4},{8,10},{10,8},{12,14},{14,12},{16,18},{18,... | collective-permute-start | bytes 1966088 | tf_op jit(solution)/shard_map/ppermute | solution.py:37
  63.6 6.8 %collective-permute-start.26 = (bf16[4,10,64,128]{3,2,1,0:T(8,128)(2,1)S(1)}, bf16[4,10,64,128]{3,2,1,0:T(8,128)(2,1)S(1)}, u32[]{:S(2)}, u32[]{:S(2)}) collective-permute-start(bf16[4,10,64,128]{3,2,1,0:T(8,128)(2,1)S(1)} %collective-permute-done.25.refs_2_), channel_id=1, source_target_pairs={{0,2},{2,0},{4,6},{6,4},{8,10},{10,8},{12,14},{14,12},{16,18},{18,... | collective-permute-start | bytes 1966088 | tf_op jit(solution)/shard_map/ppermute | solution.py:37
  68.8 10.0 %collective-permute-start.27 = (bf16[20,64,128]{2,1,0:T(8,128)(2,1)S(1)}, bf16[20,64,128]{2,1,0:T(8,128)(2,1)S(1)}, u32[]{:S(2)}, u32[]{:S(2)}) collective-permute-start(bf16[20,64,128]{2,1,0:T(8,128)(2,1)S(1)} %get-tuple-element.35), channel_id=1, source_target_pairs={{0,1},{1,0},{2,3},{3,2},{4,5},{5,4},{6,7},{7,6},{8,9},{9,8},{10,11... | collective-permute-start | bytes 983048 | tf_op jit(solution)/shard_map/ppermute | solution.py:239
  72.3 8.3 %collective-permute-start.28 = (bf16[10,64,128]{2,1,0:T(8,128)(2,1)S(1)}, bf16[10,64,128]{2,1,0:T(8,128)(2,1)S(1)}, u32[]{:S(2)}, u32[]{:S(2)}) collective-permute-start(bf16[10,64,128]{2,1,0:T(8,128)(2,1)S(1)} %get-tuple-element.36), channel_id=1, source_target_pairs={{0,1},{1,0},{2,3},{3,2},{4,5},{5,4},{6,7},{7,6},{8,9},{9,8},{10,11... | collective-permute-start | bytes 491528 | tf_op jit(solution)/shard_map/ppermute | solution.py:239

commit v5 on v4

--- a/solution.py
+++ b/solution.py
@@ -11,11 +11,11 @@
 RING_LIMIT = 16
 VMEM_LIMIT = 24 * 1024 * 1024
 UNROLL = 10
-LEFT_BANDS = 4
+LEFT_BANDS = 5
 JOIN_BANDS = 4
 STAGES = ((0, 1, 2), (3,), (4,))
 APART = 2
-WAITS = {"P2o": ('masked',), "P1x": ('P2o',), "Q1x": ('Q2o',), "Q2o": ('given',), "P4": ('m0',), "P2x": ('index', 'other'), "P3": ('Q2x', 'left'), "m1": ('y0',)}
+WAITS = {"P2o": ('masked',), "P1x": ('P2o',), "Q1x": ('Q2o',), "P2x": ('index', 'other'), "P3": ('Q2x', 'left'), "P4": ('m0',), "m1": ('y0',)}
 
 
 def in_hbm(value):
@@ -116,7 +116,7 @@
 
     for n, copy in enumerate(copies[count:]):
         copy.wait()
-        lax.fori_loop(n * bands, (n + 1) * bands, one_block, 0, unroll=2 * UNROLL)
+        lax.fori_loop(n * bands, (n + 1) * bands, one_block, 0, unroll=16)
 
 
 def right_kernel(index_ref, *refs, lefts, spots, parties, stage, bases):
@@ -177,7 +177,7 @@
             out_refs[j][g] = value[j * rows : (j + 1) * rows].astype(out_refs[j].dtype)
         return carry
 
-    lax.fori_loop(0, slots // pack, one_group, 0, unroll=min(2 * UNROLL, slots // pack))
+    lax.fori_loop(0, slots // pack, one_group, 0, unroll=min(4 * UNROLL, slots // pack))
 
 
 def join_kernel(index_ref, *refs, stages, bases):
@@ -215,7 +215,7 @@
     bands = blocks // JOIN_BANDS if blocks % JOIN_BANDS == 0 else blocks
     copies = []
     for n in range(blocks // bands):
-        counts = lax.fori_loop(n * bands, (n + 1) * bands, one_block, counts, unroll=10)
+        counts = lax.fori_loop(n * bands, (n + 1) * bands, one_block, counts, unroll=20)
         there = pl.ds(n * bands, bands)
         copies.append(pltpu.make_async_copy(joined.at[there], out_ref.at[there], sent.at[n]))
         copies[-1].start()

time: 84.1 us -> 83.7 us (level)
  no operation moved by 1% of the time
where the time goes in v5:
time: 83.7 us; the launch traced here: 83.4 us
  waiting for transfers between devices  37.2 us (44%)
  starting transfers between devices  22.3 us (27%)
  Pallas kernels  18.4 us (22%)
  other arithmetic  2.68 us (3%)
  local copies, waits for them, and re-layouts  2.55 us (3%)
    ppermute x11, waiting for transfers between devices, step_round(): return lax.ppermute(value, 'sec', pairs)  20.1 us
    ppermute x5, waiting for transfers between devices, to_party(): lax.ppermute(value, 'mpo', [(d, (d + j) % parties) for d in range(parties)])  16.5 us
    ppermute x11, starting transfers between devices, step_round(): return lax.ppermute(value, 'sec', pairs)  12.8 us
    pallas_call x3, Pallas kernels, right_products(): pl.pallas_call(functools.partial(right_kernel, lefts=len(lefts), spots=sp...  9.94 us
    ppermute x5, starting transfers between devices, to_party(): lax.ppermute(value, 'mpo', [(d, (d + j) % parties) for d in range(parties)])  6.88 us
    pallas_call x1, Pallas kernels, left_products(): pl.pallas_call(functools.partial(left_kernel, parties=parties, count=len(...  5.77 us
    pallas_call x1, Pallas kernels, on_device(): pl.pallas_call(functools.partial(join_kernel, stages=len(kept), bases=(st...  2.68 us
    ppermute x13, starting transfers between devices, swap_cores(): return lax.ppermute(value, 'sec', [(d, d ^ 1) for d in range(owners)])  2.64 us
  transfers between devices with their start and end apart: 29, of which 13 were waited for; matrix products, arithmetic and copies ran while one was open for 5% of the time, Pallas kernels for 19%

profile of v5, /device:TPU:0, one launch (start us, length us, event | category | flops | bytes accessed | tf_op | source)
XLA Modules:
  0.0 83.4 jit_solution(11870867706342934597)
XLA Ops:
  0.0 1.1 %constant_dynamic-slice_fusion = (bf16[2,10,64,128]{3,2,1,0:T(8,128)(2,1)S(1)}, bf16[2,10,64,128]{3,2,1,0:T(8,128)(2,1)S(1)}) fusion(bf16[2,10,128,128]{3,2,1,0:T(8,128)(2,1)} %param.12, s32[]{:T(128)S(6)} %select_n.17, s32[]{:T(128)S(6)} %select_n.16), kind=kLoop, calls=%fused_computation.4 | loop fusion | bytes 1310728 | tf_op jit(solution)/shard_map/dynamic_slice | solution.py:333
  1.1 0.5 collective-permute-start.1
  1.6 2.6 %collective-permute-start.4 = (bf16[2,10,64,128]{3,2,1,0:T(8,128)(2,1)S(1)}, bf16[2,10,64,128]{3,2,1,0:T(8,128)(2,1)S(1)}, u32[]{:S(2)}, u32[]{:S(2)}) collective-permute-start(bf16[2,10,64,128]{3,2,1,0:T(8,128)(2,1)S(1)} %get-tuple-element.36.refs_2_), channel_id=1, source_target_pairs={{0,8},{2,6},{4,0},{6,14},{8,16},{10,2},{12,4},{14,22},{16,24},{18,... | collective-permute-start | bytes 983048 | tf_op jit(solution)/shard_map/ppermute | solution.py:45
  4.3 1.5 %collective-permute-start.2 = (bf16[2,10,64,128]{3,2,1,0:T(8,128)(2,1)S(1)}, bf16[2,10,64,128]{3,2,1,0:T(8,128)(2,1)S(1)}, u32[]{:S(2)}, u32[]{:S(2)}) collective-permute-start(bf16[2,10,64,128]{3,2,1,0:T(8,128)(2,1)S(1)} %get-tuple-element.35), channel_id=1, source_target_pairs={{0,1},{1,0},{2,3},{3,2},{4,5},{5,4},{6,7},{7,6},{8,9},{9,8},{10,11... | collective-permute-start | bytes 983048 | tf_op jit(solution)/shard_map/ppermute | solution.py:239
  5.8 0.7 convert_element_type.3
  6.5 1.6 %collective-permute-start.9 = (bf16[2,10,64,128]{3,2,1,0:T(8,128)(2,1)S(1)}, bf16[2,10,64,128]{3,2,1,0:T(8,128)(2,1)S(1)}, u32[]{:S(2)}, u32[]{:S(2)}) collective-permute-start(bf16[2,10,64,128]{3,2,1,0:T(8,128)(2,1)S(1)} %collective-permute-done.1.refs_3_), channel_id=1, source_target_pairs={{0,8},{2,6},{4,0},{6,14},{8,16},{10,2},{12,4},{14,22},{16,24},{18,... | collective-permute-start | bytes 983048 | tf_op jit(solution)/shard_map/ppermute | solution.py:45
  8.1 1.2 %broadcast_multiply_fusion.refs_0_ = bf16[2,10,128,128]{3,2,1,0:T(8,128)(2,1)S(1)} fusion(bf16[2,10,128,128]{3,2,1,0:T(8,128)(2,1)} %param.11, bf16[2,10]{1,0:T(2,128)(2,1)S(1)} %convert_element_type.3), kind=kLoop, calls=%fused_computation.2 | loop fusion | flops 327680 | bytes 1310760 | tf_op jit(solution)/shard_map/mul | solution.py:320
  9.3 2.1 %collective-permute-start.6 = (bf16[2,10,64,128]{3,2,1,0:T(8,128)(2,1)S(1)}, bf16[2,10,64,128]{3,2,1,0:T(8,128)(2,1)S(1)}, u32[]{:S(2)}, u32[]{:S(2)}) collective-permute-start(bf16[2,10,64,128]{3,2,1,0:T(8,128)(2,1)S(1)} %collective-permute-done.4.refs_6_), channel_id=1, source_target_pairs={{0,8},{2,6},{4,0},{6,14},{8,16},{10,2},{12,4},{14,22},{16,24},{18,... | collective-permute-start | bytes 983048 | tf_op jit(solution)/shard_map/ppermute | solution.py:45
  11.4 1.5 %collective-permute-start = (bf16[2,10,128,128]{3,2,1,0:T(8,128)(2,1)S(1)}, bf16[2,10,128,128]{3,2,1,0:T(8,128)(2,1)}, u32[]{:S(2)}, u32[]{:S(2)}) collective-permute-start(bf16[2,10,128,128]{3,2,1,0:T(8,128)(2,1)S(1)} %broadcast_multiply_fusion.refs_0_), channel_id=1, source_target_pairs={{0,1},{1,0},{2,3},{3,2},{4,5},{5,4},{6,7},{7,6},{8,9},{9,8},{10,11... | collective-permute-start | bytes 1966088 | tf_op jit(solution)/shard_map/ppermute | solution.py:239
  12.9 1.8 %collective-permute-done.2.refs_4_ = bf16[2,10,64,128]{3,2,1,0:T(8,128)(2,1)S(1)} collective-permute-done((bf16[2,10,64,128]{3,2,1,0:T(8,128)(2,1)S(1)}, bf16[2,10,64,128]{3,2,1,0:T(8,128)(2,1)S(1)}, u32[]{:S(2)}, u32[]{:S(2)}) %collective-permute-start.2) | collective-permute-done | bytes 327712 | tf_op jit(solution)/shard_map/ppermute | solution.py:239
  14.7 0.4 collective-permute-start.11
  15.1 1.9 %collective-permute-done.6.refs_14_ = bf16[2,10,64,128]{3,2,1,0:T(8,128)(2,1)S(1)} collective-permute-done((bf16[2,10,64,128]{3,2,1,0:T(8,128)(2,1)S(1)}, bf16[2,10,64,128]{3,2,1,0:T(8,128)(2,1)S(1)}, u32[]{:S(2)}, u32[]{:S(2)}) %collective-permute-start.6) | collective-permute-done | bytes 327712 | tf_op jit(solution)/shard_map/ppermute | solution.py:45
  17.1 1.6 %collective-permute-start.7 = (bf16[2,10,64,128]{3,2,1,0:T(8,128)(2,1)S(1)}, bf16[2,10,64,128]{3,2,1,0:T(8,128)(2,1)}, u32[]{:S(2)}, u32[]{:S(2)}) collective-permute-start(bf16[2,10,64,128]{3,2,1,0:T(8,128)(2,1)S(1)} %collective-permute-done.2.refs_4_), channel_id=1, source_target_pairs={{0,8},{2,6},{4,0},{6,14},{8,16},{10,2},{12,4},{14,22},{16,24},{18,... | collective-permute-start | bytes 983048 | tf_op jit(solution)/shard_map/ppermute | solution.py:45
  18.7 0.7 fusion
  19.3 2.4 %collective-permute-done.11.refs_18_ = bf16[2,10,64,128]{3,2,1,0:T(8,128)(2,1)S(1)} collective-permute-done((bf16[2,10,64,128]{3,2,1,0:T(8,128)(2,1)S(1)}, bf16[2,10,64,128]{3,2,1,0:T(8,128)(2,1)S(1)}, u32[]{:S(2)}, u32[]{:S(2)}) %collective-permute-start.11) | collective-permute-done | bytes 327712 | tf_op jit(solution)/shard_map/ppermute | solution.py:45
  21.8 0.4 collective-permute-start.12
  22.2 0.7 and_select_fusion
  22.9 0.7 concatenate.9.index_ref
  23.6 4.5 %collective-permute-done.refs_1_ = bf16[2,10,128,128]{3,2,1,0:T(8,128)(2,1)} collective-permute-done((bf16[2,10,128,128]{3,2,1,0:T(8,128)(2,1)S(1)}, bf16[2,10,128,128]{3,2,1,0:T(8,128)(2,1)}, u32[]{:S(2)}, u32[]{:S(2)}) %collective-permute-start) | collective-permute-done | bytes 655392 | tf_op jit(solution)/shard_map/ppermute | solution.py:239
  28.1 0.4 collective-permute-start.15
  28.5 0.5 collective-permute-done.12.refs_12_
  29.0 1.3 %collective-permute-start.18 = (bf16[2,10,64,128]{3,2,1,0:T(8,128)(2,1)}, bf16[2,10,64,128]{3,2,1,0:T(8,128)(2,1)S(1)}, u32[]{:S(2)}, u32[]{:S(2)}) collective-permute-start(bf16[2,10,64,128]{3,2,1,0:T(8,128)(2,1)} %collective-permute-done.12.refs_12_), channel_id=1, source_target_pairs={{0,8},{2,6},{4,0},{6,14},{8,16},{10,2},{12,4},{14,22},{16,24},{18,... | collective-permute-start | bytes 983048 | tf_op jit(solution)/shard_map/ppermute | solution.py:45
  30.2 0.2 collective-permute-start.5
  30.4 0.4 collective-permute-start.10
  30.8 0.2 collective-permute-start.14
  30.9 5.8 %left_products.1 = (bf16[80,128,256]{2,1,0:T(8,128)(2,1)S(1)}, bf16[80,128,256]{2,1,0:T(8,128)(2,1)S(1)}) custom-call(s32[305]{0:T(512)S(1)} %concatenate.9.index_ref, bf16[2,10,128,128]{3,2,1,0:T(8,128)(2,1)S(1)} %broadcast_multiply_fusion.refs_0_, bf16[2,10,128,128]{3,2,1,0:T(8,128)(2,1)} %collective-permute-done.refs_1_, bf16[80,128,128]{2,1,0:T(8,128)(2,1)} %refs_2_.1), custom_call_target="tpu_custom_call" | custom-call | flops 1342177280 | bytes 9437184 | tf_op jit(solution)/shard_map/left_products/pallas_call | solution.py:269
  36.7 0.4 collective-permute-start.8
  37.2 1.7 %collective-permute-done.18.refs_20_ = bf16[2,10,64,128]{3,2,1,0:T(8,128)(2,1)S(1)} collective-permute-done((bf16[2,10,64,128]{3,2,1,0:T(8,128)(2,1)}, bf16[2,10,64,128]{3,2,1,0:T(8,128)(2,1)S(1)}, u32[]{:S(2)}, u32[]{:S(2)}) %collective-permute-start.18) | collective-permute-done | bytes 327712 | tf_op jit(solution)/shard_map/ppermute | solution.py:45
  38.9 0.4 collective-permute-start.20
  39.3 0.5 collective-permute-start.13
  39.8 0.1 collective-permute-start.16
  39.9 0.4 collective-permute-start.19
  40.4 0.5 collective-permute-done.17.refs_19_
  40.9 1.7 %collective-permute-start.23 = (bf16[4,10,64,128]{3,2,1,0:T(8,128)(2,1)S(1)}, bf16[4,10,64,128]{3,2,1,0:T(8,128)(2,1)S(1)}, u32[]{:S(2)}, u32[]{:S(2)}) collective-permute-start(bf16[4,10,64,128]{3,2,1,0:T(8,128)(2,1)S(1)} %pad_maximum_fusion.1), channel_id=1, source_target_pairs={{0,8},{2,6},{4,0},{6,14},{8,16},{10,2},{12,4},{14,22},{16,24},{18,... | collective-permute-start | bytes 1966088 | tf_op jit(solution)/shard_map/ppermute | solution.py:45
  42.7 5.3 %right_products.3 = (bf16[40,64,128]{2,1,0:T(8,128)(2,1)S(1)}, bf16[40,64,128]{2,1,0:T(8,128)(2,1)S(1)}) custom-call(s32[305]{0:T(512)S(1)} %concatenate.9.index_ref, bf16[80,128,256]{2,1,0:T(8,128)(2,1)S(1)} %get-tuple-element.20.refs_0_, bf16[80,128,256]{2,1,0:T(8,128)(2,1)S(1)} %get-tuple-element.21.refs_1_, ...), custom_call_target="tpu_custom_call" | custom-call | flops 671088640 | bytes 12582912 | tf_op jit(solution)/shard_map/right_products/pallas_call | solution.py:293
  48.0 1.5 %collective-permute-done.20.refs_2_ = bf16[4,10,64,128]{3,2,1,0:T(8,128)(2,1)S(1)} collective-permute-done((bf16[4,10,64,128]{3,2,1,0:T(8,128)(2,1)S(1)}, bf16[4,10,64,128]{3,2,1,0:T(8,128)(2,1)S(1)}, u32[]{:S(2)}, u32[]{:S(2)}) %collective-permute-start.20) | collective-permute-done | bytes 655392 | tf_op jit(solution)/shard_map/ppermute | solution.py:45
  49.5 0.4 collective-permute-start.25
  49.9 1.7 %collective-permute-start.21 = (bf16[40,64,128]{2,1,0:T(8,128)(2,1)S(1)}, bf16[40,64,128]{2,1,0:T(8,128)(2,1)S(1)}, u32[]{:S(2)}, u32[]{:S(2)}) collective-permute-start(bf16[40,64,128]{2,1,0:T(8,128)(2,1)S(1)} %get-tuple-element.28), channel_id=1, source_target_pairs={{0,1},{1,0},{2,3},{3,2},{4,5},{5,4},{6,7},{7,6},{8,9},{9,8},{10,11... | collective-permute-start | bytes 1966088 | tf_op jit(solution)/shard_map/ppermute | solution.py:239
  51.6 5.0 %collective-permute-done.23.refs_4_ = bf16[4,10,64,128]{3,2,1,0:T(8,128)(2,1)S(1)} collective-permute-done((bf16[4,10,64,128]{3,2,1,0:T(8,128)(2,1)S(1)}, bf16[4,10,64,128]{3,2,1,0:T(8,128)(2,1)S(1)}, u32[]{:S(2)}, u32[]{:S(2)}) %collective-permute-start.23) | collective-permute-done | bytes 655392 | tf_op jit(solution)/shard_map/ppermute | solution.py:45
  56.5 7.0 %collective-permute-done.25.refs_2_ = bf16[4,10,64,128]{3,2,1,0:T(8,128)(2,1)S(1)} collective-permute-done((bf16[4,10,64,128]{3,2,1,0:T(8,128)(2,1)S(1)}, bf16[4,10,64,128]{3,2,1,0:T(8,128)(2,1)S(1)}, u32[]{:S(2)}, u32[]{:S(2)}) %collective-permute-start.25) | collective-permute-done | bytes 655392 | tf_op jit(solution)/shard_map/ppermute | solution.py:45
  63.6 2.5 %collective-permute-done.21.refs_3_ = bf16[40,64,128]{2,1,0:T(8,128)(2,1)S(1)} collective-permute-done((bf16[40,64,128]{2,1,0:T(8,128)(2,1)S(1)}, bf16[40,64,128]{2,1,0:T(8,128)(2,1)S(1)}, u32[]{:S(2)}, u32[]{:S(2)}) %collective-permute-start.21) | collective-permute-done | bytes 655392 | tf_op jit(solution)/shard_map/ppermute | solution.py:239
  66.0 2.8 %right_products.4 = (bf16[20,64,128]{2,1,0:T(8,128)(2,1)S(1)}, bf16[20,64,128]{2,1,0:T(8,128)(2,1)S(1)}) custom-call(s32[305]{0:T(512)S(1)} %concatenate.9.index_ref, bf16[80,128,256]{2,1,0:T(8,128)(2,1)S(1)} %get-tuple-element.20.refs_0_, bf16[80,128,256]{2,1,0:T(8,128)(2,1)S(1)} %get-tuple-element.21.refs_1_, ...), custom_call_target="tpu_custom_call" | custom-call | flops 335544320 | bytes 12582912 | tf_op jit(solution)/shard_map/right_products/pallas_call | solution.py:293
  68.8 1.6 %collective-permute-start.27 = (bf16[20,64,128]{2,1,0:T(8,128)(2,1)S(1)}, bf16[20,64,128]{2,1,0:T(8,128)(2,1)S(1)}, u32[]{:S(2)}, u32[]{:S(2)}) collective-permute-start(bf16[20,64,128]{2,1,0:T(8,128)(2,1)S(1)} %get-tuple-element.33), channel_id=1, source_target_pairs={{0,1},{1,0},{2,3},{3,2},{4,5},{5,4},{6,7},{7,6},{8,9},{9,8},{10,11... | collective-permute-start | bytes 983048 | tf_op jit(solution)/shard_map/ppermute | solution.py:239
  70.4 1.9 %right_products.5 = (bf16[10,64,128]{2,1,0:T(8,128)(2,1)S(1)}, bf16[10,64,128]{2,1,0:T(8,128)(2,1)S(1)}) custom-call(s32[305]{0:T(512)S(1)} %concatenate.9.index_ref, bf16[80,128,256]{2,1,0:T(8,128)(2,1)S(1)} %get-tuple-element.20.refs_0_, bf16[80,128,256]{2,1,0:T(8,128)(2,1)S(1)} %get-tuple-element.21.refs_1_, ...), custom_call_target="tpu_custom_call" | custom-call | flops 167772160 | bytes 12582912 | tf_op jit(solution)/shard_map/right_products/pallas_call | solution.py:293
  72.3 0.6 collective-permute-start.28
  72.8 6.0 %collective-permute-done.27.refs_4_ = bf16[20,64,128]{2,1,0:T(8,128)(2,1)S(1)} collective-permute-done((bf16[20,64,128]{2,1,0:T(8,128)(2,1)S(1)}, bf16[20,64,128]{2,1,0:T(8,128)(2,1)S(1)}, u32[]{:S(2)}, u32[]{:S(2)}) %collective-permute-start.27) | collective-permute-done | bytes 327712 | tf_op jit(solution)/shard_map/ppermute | solution.py:239
  78.8 1.8 %collective-permute-done.28.refs_5_ = bf16[10,64,128]{2,1,0:T(8,128)(2,1)S(1)} collective-permute-done((bf16[10,64,128]{2,1,0:T(8,128)(2,1)S(1)}, bf16[10,64,128]{2,1,0:T(8,128)(2,1)S(1)}, u32[]{:S(2)}, u32[]{:S(2)}) %collective-permute-start.28) | collective-permute-done | bytes 163872 | tf_op jit(solution)/shard_map/ppermute | solution.py:239
  80.6 2.7 %join_columns.1 = bf16[80,64,128]{2,1,0:T(8,128)(2,1)} custom-call(s32[305]{0:T(512)S(1)} %concatenate.9.index_ref, bf16[40,64,128]{2,1,0:T(8,128)(2,1)S(1)} %get-tuple-element.26.refs_0_, bf16[20,64,128]{2,1,0:T(8,128)(2,1)S(1)} %get-tuple-element.30.refs_1_, bf16[10,64,128]{2,1,0:T(8,128)(2,1)S(1)} %get-tuple-element.32.refs_2_, ...), custom_call_target="tpu_custom_call" | custom-call | bytes 4194304 | tf_op jit(solution)/shard_map/join_columns/pallas_call | solution.py:389
  (23 shorter events, 0.2 us)
Async XLA Ops:
  1.1 5.4 %collective-permute-start.1 = (bf16[2,10,64,128]{3,2,1,0:T(8,128)(2,1)S(1)}, bf16[2,10,64,128]{3,2,1,0:T(8,128)(2,1)S(1)}, u32[]{:S(2)}, u32[]{:S(2)}) collective-permute-start(bf16[2,10,64,128]{3,2,1,0:T(8,128)(2,1)S(1)} %get-tuple-element.36.refs_2_), channel_id=1, source_target_pairs={{0,2},{2,0},{4,6},{6,4},{8,10},{10,8},{12,14},{14,12},{16,18},{18,... | collective-permute-start | bytes 983048 | tf_op jit(solution)/shard_map/ppermute | solution.py:37
  1.6 7.6 %collective-permute-start.4 = (bf16[2,10,64,128]{3,2,1,0:T(8,128)(2,1)S(1)}, bf16[2,10,64,128]{3,2,1,0:T(8,128)(2,1)S(1)}, u32[]{:S(2)}, u32[]{:S(2)}) collective-permute-start(bf16[2,10,64,128]{3,2,1,0:T(8,128)(2,1)S(1)} %get-tuple-element.36.refs_2_), channel_id=1, source_target_pairs={{0,8},{2,6},{4,0},{6,14},{8,16},{10,2},{12,4},{14,22},{16,24},{18,... | collective-permute-start | bytes 983048 | tf_op jit(solution)/shard_map/ppermute | solution.py:45
  4.3 10.4 %collective-permute-start.2 = (bf16[2,10,64,128]{3,2,1,0:T(8,128)(2,1)S(1)}, bf16[2,10,64,128]{3,2,1,0:T(8,128)(2,1)S(1)}, u32[]{:S(2)}, u32[]{:S(2)}) collective-permute-start(bf16[2,10,64,128]{3,2,1,0:T(8,128)(2,1)S(1)} %get-tuple-element.35), channel_id=1, source_target_pairs={{0,1},{1,0},{2,3},{3,2},{4,5},{5,4},{6,7},{7,6},{8,9},{9,8},{10,11... | collective-permute-start | bytes 983048 | tf_op jit(solution)/shard_map/ppermute | solution.py:239
  6.5 8.2 %collective-permute-start.9 = (bf16[2,10,64,128]{3,2,1,0:T(8,128)(2,1)S(1)}, bf16[2,10,64,128]{3,2,1,0:T(8,128)(2,1)S(1)}, u32[]{:S(2)}, u32[]{:S(2)}) collective-permute-start(bf16[2,10,64,128]{3,2,1,0:T(8,128)(2,1)S(1)} %collective-permute-done.1.refs_3_), channel_id=1, source_target_pairs={{0,8},{2,6},{4,0},{6,14},{8,16},{10,2},{12,4},{14,22},{16,24},{18,... | collective-permute-start | bytes 983048 | tf_op jit(solution)/shard_map/ppermute | solution.py:45
  9.3 7.8 %collective-permute-start.6 = (bf16[2,10,64,128]{3,2,1,0:T(8,128)(2,1)S(1)}, bf16[2,10,64,128]{3,2,1,0:T(8,128)(2,1)S(1)}, u32[]{:S(2)}, u32[]{:S(2)}) collective-permute-start(bf16[2,10,64,128]{3,2,1,0:T(8,128)(2,1)S(1)} %collective-permute-done.4.refs_6_), channel_id=1, source_target_pairs={{0,8},{2,6},{4,0},{6,14},{8,16},{10,2},{12,4},{14,22},{16,24},{18,... | collective-permute-start | bytes 983048 | tf_op jit(solution)/shard_map/ppermute | solution.py:45
  11.4 16.8 %collective-permute-start = (bf16[2,10,128,128]{3,2,1,0:T(8,128)(2,1)S(1)}, bf16[2,10,128,128]{3,2,1,0:T(8,128)(2,1)}, u32[]{:S(2)}, u32[]{:S(2)}) collective-permute-start(bf16[2,10,128,128]{3,2,1,0:T(8,128)(2,1)S(1)} %broadcast_multiply_fusion.refs_0_), channel_id=1, source_target_pairs={{0,1},{1,0},{2,3},{3,2},{4,5},{5,4},{6,7},{7,6},{8,9},{9,8},{10,11... | collective-permute-start | bytes 1966088 | tf_op jit(solution)/shard_map/ppermute | solution.py:239
  14.7 4.6 %collective-permute-start.3 = (bf16[2,10,64,128]{3,2,1,0:T(8,128)(2,1)S(1)}, bf16[2,10,64,128]{3,2,1,0:T(8,128)(2,1)S(1)}, u32[]{:S(2)}, u32[]{:S(2)}) collective-permute-start(bf16[2,10,64,128]{3,2,1,0:T(8,128)(2,1)S(1)} %collective-permute-done.2.refs_4_), channel_id=1, source_target_pairs={{0,2},{2,0},{4,6},{6,4},{8,10},{10,8},{12,14},{14,12},{16,18},{18,... | collective-permute-start | bytes 983048 | tf_op jit(solution)/shard_map/ppermute | solution.py:37
  14.7 7.1 %collective-permute-start.11 = (bf16[2,10,64,128]{3,2,1,0:T(8,128)(2,1)S(1)}, bf16[2,10,64,128]{3,2,1,0:T(8,128)(2,1)S(1)}, u32[]{:S(2)}, u32[]{:S(2)}) collective-permute-start(bf16[2,10,64,128]{3,2,1,0:T(8,128)(2,1)S(1)} %collective-permute-done.9.refs_10_), channel_id=1, source_target_pairs={{0,8},{2,6},{4,0},{6,14},{8,16},{10,2},{12,4},{14,22},{16,24},{18,... | collective-permute-start | bytes 983048 | tf_op jit(solution)/shard_map/ppermute | solution.py:45
  17.1 11.1 %collective-permute-start.7 = (bf16[2,10,64,128]{3,2,1,0:T(8,128)(2,1)S(1)}, bf16[2,10,64,128]{3,2,1,0:T(8,128)(2,1)}, u32[]{:S(2)}, u32[]{:S(2)}) collective-permute-start(bf16[2,10,64,128]{3,2,1,0:T(8,128)(2,1)S(1)} %collective-permute-done.2.refs_4_), channel_id=1, source_target_pairs={{0,8},{2,6},{4,0},{6,14},{8,16},{10,2},{12,4},{14,22},{16,24},{18,... | collective-permute-start | bytes 983048 | tf_op jit(solution)/shard_map/ppermute | solution.py:45
  21.8 7.2 %collective-permute-start.12 = (bf16[2,10,64,128]{3,2,1,0:T(8,128)(2,1)S(1)}, bf16[2,10,64,128]{3,2,1,0:T(8,128)(2,1)}, u32[]{:S(2)}, u32[]{:S(2)}) collective-permute-start(bf16[2,10,64,128]{3,2,1,0:T(8,128)(2,1)S(1)} %collective-permute-done.3.refs_5_), channel_id=1, source_target_pairs={{0,8},{2,6},{4,0},{6,14},{8,16},{10,2},{12,4},{14,22},{16,24},{18,... | collective-permute-start | bytes 983048 | tf_op jit(solution)/shard_map/ppermute | solution.py:45
  28.1 8.6 %collective-permute-start.15 = (bf16[2,10,64,128]{3,2,1,0:T(8,128)(2,1)}, bf16[2,10,64,128]{3,2,1,0:T(8,128)(2,1)S(1)}, u32[]{:S(2)}, u32[]{:S(2)}) collective-permute-start(bf16[2,10,64,128]{3,2,1,0:T(8,128)(2,1)} %collective-permute-done.7.refs_8_), channel_id=1, source_target_pairs={{0,8},{2,6},{4,0},{6,14},{8,16},{10,2},{12,4},{14,22},{16,24},{18,... | collective-permute-start | bytes 983048 | tf_op jit(solution)/shard_map/ppermute | solution.py:45
  29.0 10.0 %collective-permute-start.18 = (bf16[2,10,64,128]{3,2,1,0:T(8,128)(2,1)}, bf16[2,10,64,128]{3,2,1,0:T(8,128)(2,1)S(1)}, u32[]{:S(2)}, u32[]{:S(2)}) collective-permute-start(bf16[2,10,64,128]{3,2,1,0:T(8,128)(2,1)} %collective-permute-done.12.refs_12_), channel_id=1, source_target_pairs={{0,8},{2,6},{4,0},{6,14},{8,16},{10,2},{12,4},{14,22},{16,24},{18,... | collective-permute-start | bytes 983048 | tf_op jit(solution)/shard_map/ppermute | solution.py:45
  30.2 9.1 %collective-permute-start.5 = (bf16[2,10,64,128]{3,2,1,0:T(8,128)(2,1)S(1)}, bf16[2,10,64,128]{3,2,1,0:T(8,128)(2,1)S(1)}, u32[]{:S(2)}, u32[]{:S(2)}) collective-permute-start(bf16[2,10,64,128]{3,2,1,0:T(8,128)(2,1)S(1)} %collective-permute-done.4.refs_6_), channel_id=1, source_target_pairs={{0,2},{2,0},{4,6},{6,4},{8,10},{10,8},{12,14},{14,12},{16,18},{18,... | collective-permute-start | bytes 983048 | tf_op jit(solution)/shard_map/ppermute | solution.py:37
  30.4 8.9 %collective-permute-start.10 = (bf16[2,10,64,128]{3,2,1,0:T(8,128)(2,1)S(1)}, bf16[2,10,64,128]{3,2,1,0:T(8,128)(2,1)S(1)}, u32[]{:S(2)}, u32[]{:S(2)}) collective-permute-start(bf16[2,10,64,128]{3,2,1,0:T(8,128)(2,1)S(1)} %collective-permute-done.9.refs_10_), channel_id=1, source_target_pairs={{0,2},{2,0},{4,6},{6,4},{8,10},{10,8},{12,14},{14,12},{16,18},{18,... | collective-permute-start | bytes 983048 | tf_op jit(solution)/shard_map/ppermute | solution.py:37
  30.8 9.1 %collective-permute-start.14 = (bf16[2,10,64,128]{3,2,1,0:T(8,128)(2,1)S(1)}, bf16[2,10,64,128]{3,2,1,0:T(8,128)(2,1)S(1)}, u32[]{:S(2)}, u32[]{:S(2)}) collective-permute-start(bf16[2,10,64,128]{3,2,1,0:T(8,128)(2,1)S(1)} %collective-permute-done.6.refs_14_), channel_id=1, source_target_pairs={{0,2},{2,0},{4,6},{6,4},{8,10},{10,8},{12,14},{14,12},{16,18},{18,... | collective-permute-start | bytes 983048 | tf_op jit(solution)/shard_map/ppermute | solution.py:37
  36.7 3.2 %collective-permute-start.8 = (bf16[2,10,64,128]{3,2,1,0:T(8,128)(2,1)}, bf16[2,10,64,128]{3,2,1,0:T(8,128)(2,1)S(1)}, u32[]{:S(2)}, u32[]{:S(2)}) collective-permute-start(bf16[2,10,64,128]{3,2,1,0:T(8,128)(2,1)} %collective-permute-done.7.refs_8_), channel_id=1, source_target_pairs={{0,2},{2,0},{4,6},{6,4},{8,10},{10,8},{12,14},{14,12},{16,18},{18,... | collective-permute-start | bytes 983048 | tf_op jit(solution)/shard_map/ppermute | solution.py:37
  38.9 10.6 %collective-permute-start.20 = (bf16[4,10,64,128]{3,2,1,0:T(8,128)(2,1)S(1)}, bf16[4,10,64,128]{3,2,1,0:T(8,128)(2,1)S(1)}, u32[]{:S(2)}, u32[]{:S(2)}) collective-permute-start(bf16[4,10,64,128]{3,2,1,0:T(8,128)(2,1)S(1)} %pad_maximum_fusion), channel_id=1, source_target_pairs={{0,8},{2,6},{4,0},{6,14},{8,16},{10,2},{12,4},{14,22},{16,24},{18,... | collective-permute-start | bytes 1966088 | tf_op jit(solution)/shard_map/ppermute | solution.py:45
  39.3 1.6 %collective-permute-start.17 = (bf16[2,10,64,128]{3,2,1,0:T(8,128)(2,1)S(1)}, bf16[2,10,64,128]{3,2,1,0:T(8,128)(2,1)S(1)}, u32[]{:S(2)}, u32[]{:S(2)}) collective-permute-start(bf16[2,10,64,128]{3,2,1,0:T(8,128)(2,1)S(1)} %collective-permute-done.11.refs_18_), channel_id=1, source_target_pairs={{0,2},{2,0},{4,6},{6,4},{8,10},{10,8},{12,14},{14,12},{16,18},{18,... | collective-permute-start | bytes 983048 | tf_op jit(solution)/shard_map/ppermute | solution.py:37
  39.3 3.4 %collective-permute-start.13 = (bf16[2,10,64,128]{3,2,1,0:T(8,128)(2,1)}, bf16[2,10,64,128]{3,2,1,0:T(8,128)(2,1)S(1)}, u32[]{:S(2)}, u32[]{:S(2)}) collective-permute-start(bf16[2,10,64,128]{3,2,1,0:T(8,128)(2,1)} %collective-permute-done.12.refs_12_), channel_id=1, source_target_pairs={{0,2},{2,0},{4,6},{6,4},{8,10},{10,8},{12,14},{14,12},{16,18},{18,... | collective-permute-start | bytes 983048 | tf_op jit(solution)/shard_map/ppermute | solution.py:37
  39.8 2.9 %collective-permute-start.16 = (bf16[2,10,64,128]{3,2,1,0:T(8,128)(2,1)S(1)}, bf16[2,10,64,128]{3,2,1,0:T(8,128)(2,1)S(1)}, u32[]{:S(2)}, u32[]{:S(2)}) collective-permute-start(bf16[2,10,64,128]{3,2,1,0:T(8,128)(2,1)S(1)} %collective-permute-done.15.refs_16_), channel_id=1, source_target_pairs={{0,2},{2,0},{4,6},{6,4},{8,10},{10,8},{12,14},{14,12},{16,18},{18,... | collective-permute-start | bytes 983048 | tf_op jit(solution)/shard_map/ppermute | solution.py:37
  39.9 2.8 %collective-permute-start.19 = (bf16[2,10,64,128]{3,2,1,0:T(8,128)(2,1)S(1)}, bf16[2,10,64,128]{3,2,1,0:T(8,128)(2,1)S(1)}, u32[]{:S(2)}, u32[]{:S(2)}) collective-permute-start(bf16[2,10,64,128]{3,2,1,0:T(8,128)(2,1)S(1)} %collective-permute-done.18.refs_20_), channel_id=1, source_target_pairs={{0,2},{2,0},{4,6},{6,4},{8,10},{10,8},{12,14},{14,12},{16,18},{18,... | collective-permute-start | bytes 983048 | tf_op jit(solution)/shard_map/ppermute | solution.py:37
  40.9 15.6 %collective-permute-start.23 = (bf16[4,10,64,128]{3,2,1,0:T(8,128)(2,1)S(1)}, bf16[4,10,64,128]{3,2,1,0:T(8,128)(2,1)S(1)}, u32[]{:S(2)}, u32[]{:S(2)}) collective-permute-start(bf16[4,10,64,128]{3,2,1,0:T(8,128)(2,1)S(1)} %pad_maximum_fusion.1), channel_id=1, source_target_pairs={{0,8},{2,6},{4,0},{6,14},{8,16},{10,2},{12,4},{14,22},{16,24},{18,... | collective-permute-start | bytes 1966088 | tf_op jit(solution)/shard_map/ppermute | solution.py:45
  49.5 14.0 %collective-permute-start.25 = (bf16[4,10,64,128]{3,2,1,0:T(8,128)(2,1)S(1)}, bf16[4,10,64,128]{3,2,1,0:T(8,128)(2,1)S(1)}, u32[]{:S(2)}, u32[]{:S(2)}) collective-permute-start(bf16[4,10,64,128]{3,2,1,0:T(8,128)(2,1)S(1)} %collective-permute-done.20.refs_2_), channel_id=1, source_target_pairs={{0,8},{2,6},{4,0},{6,14},{8,16},{10,2},{12,4},{14,22},{16,24},{18,... | collective-permute-start | bytes 1966088 | tf_op jit(solution)/shard_map/ppermute | solution.py:45
  49.9 16.2 %collective-permute-start.21 = (bf16[40,64,128]{2,1,0:T(8,128)(2,1)S(1)}, bf16[40,64,128]{2,1,0:T(8,128)(2,1)S(1)}, u32[]{:S(2)}, u32[]{:S(2)}) collective-permute-start(bf16[40,64,128]{2,1,0:T(8,128)(2,1)S(1)} %get-tuple-element.28), channel_id=1, source_target_pairs={{0,1},{1,0},{2,3},{3,2},{4,5},{5,4},{6,7},{7,6},{8,9},{9,8},{10,11... | collective-permute-start | bytes 1966088 | tf_op jit(solution)/shard_map/ppermute | solution.py:239
  51.6 14.5 %collective-permute-start.22 = (bf16[4,10,64,128]{3,2,1,0:T(8,128)(2,1)S(1)}, bf16[4,10,64,128]{3,2,1,0:T(8,128)(2,1)S(1)}, u32[]{:S(2)}, u32[]{:S(2)}) collective-permute-start(bf16[4,10,64,128]{3,2,1,0:T(8,128)(2,1)S(1)} %collective-permute-done.20.refs_2_), channel_id=1, source_target_pairs={{0,2},{2,0},{4,6},{6,4},{8,10},{10,8},{12,14},{14,12},{16,18},{18,... | collective-permute-start | bytes 1966088 | tf_op jit(solution)/shard_map/ppermute | solution.py:37
  56.5 9.5 %collective-permute-start.24 = (bf16[4,10,64,128]{3,2,1,0:T(8,128)(2,1)S(1)}, bf16[4,10,64,128]{3,2,1,0:T(8,128)(2,1)S(1)}, u32[]{:S(2)}, u32[]{:S(2)}) collective-permute-start(bf16[4,10,64,128]{3,2,1,0:T(8,128)(2,1)S(1)} %collective-permute-done.23.refs_4_), channel_id=1, source_target_pairs={{0,2},{2,0},{4,6},{6,4},{8,10},{10,8},{12,14},{14,12},{16,18},{18,... | collective-permute-start | bytes 1966088 | tf_op jit(solution)/shard_map/ppermute | solution.py:37
  63.6 6.8 %collective-permute-start.26 = (bf16[4,10,64,128]{3,2,1,0:T(8,128)(2,1)S(1)}, bf16[4,10,64,128]{3,2,1,0:T(8,128)(2,1)S(1)}, u32[]{:S(2)}, u32[]{:S(2)}) collective-permute-start(bf16[4,10,64,128]{3,2,1,0:T(8,128)(2,1)S(1)} %collective-permute-done.25.refs_2_), channel_id=1, source_target_pairs={{0,2},{2,0},{4,6},{6,4},{8,10},{10,8},{12,14},{14,12},{16,18},{18,... | collective-permute-start | bytes 1966088 | tf_op jit(solution)/shard_map/ppermute | solution.py:37
  68.8 10.0 %collective-permute-start.27 = (bf16[20,64,128]{2,1,0:T(8,128)(2,1)S(1)}, bf16[20,64,128]{2,1,0:T(8,128)(2,1)S(1)}, u32[]{:S(2)}, u32[]{:S(2)}) collective-permute-start(bf16[20,64,128]{2,1,0:T(8,128)(2,1)S(1)} %get-tuple-element.33), channel_id=1, source_target_pairs={{0,1},{1,0},{2,3},{3,2},{4,5},{5,4},{6,7},{7,6},{8,9},{9,8},{10,11... | collective-permute-start | bytes 983048 | tf_op jit(solution)/shard_map/ppermute | solution.py:239
  72.3 8.3 %collective-permute-start.28 = (bf16[10,64,128]{2,1,0:T(8,128)(2,1)S(1)}, bf16[10,64,128]{2,1,0:T(8,128)(2,1)S(1)}, u32[]{:S(2)}, u32[]{:S(2)}) collective-permute-start(bf16[10,64,128]{2,1,0:T(8,128)(2,1)S(1)} %get-tuple-element.34), channel_id=1, source_target_pairs={{0,1},{1,0},{2,3},{3,2},{4,5},{5,4},{6,7},{7,6},{8,9},{9,8},{10,11... | collective-permute-start | bytes 491528 | tf_op jit(solution)/shard_map/ppermute | solution.py:239

commit v6 on v5

--- a/solution.py
+++ b/solution.py
@@ -361,6 +361,11 @@
                     continue
                 if number == 0:
                     found = [(n * terms, trail[0, q], q) for n, trail in enumerate(trails) for q in range(2)]
+                elif number == APART and number < lanes[lane]:
+                    head = joined[lane] = jnp.concatenate(
+                        [trail[number, lane] for trail in trails], axis=0
+                    )
+                    found = [(0, head, 0), (0, swap_cores(head, owners), 1)]
                 elif number <= APART:
                     found = [
                         (n * terms, v, q)

time: 83.7 us -> 94.8 us (1.13)
  waiting for transfers between devices: 37.2 us -> 46.2 us
  local copies, waits for them, and re-layouts: 2.55 us -> 4.63 us
    ppermute x5, waiting for transfers between devices: 16.5 us -> 22.1 us  [to_party(): lax.ppermute(value, 'mpo', [(d, (d + j) % parties) for d in range(parties)])]
    ppermute x11, waiting for transfers between devices: 20.1 us -> 22.8 us  [step_round(): return lax.ppermute(value, 'sec', pairs)]
    unnamed x0 -> x2, local copies, waits for them, and re-layouts: none -> 1.99 us
    ppermute x11, starting transfers between devices: 12.8 us -> 14.3 us  [step_round(): return lax.ppermute(value, 'sec', pairs)]
    ppermute x13 -> x11, starting transfers between devices: 2.64 us -> 1.98 us  [swap_cores(): return lax.ppermute(value, 'sec', [(d, d ^ 1) for d in range(owners)])]
  transfers between devices with their start and end apart: 29 -> 27, of which waited for: 13 -> 14; matrix products, arithmetic and copies ran while one was open for 5% -> 6% of each run, Pallas kernels for 19% -> 16%
where the time goes in v6:
time: 94.8 us; the launch traced here: 94.5 us
  waiting for transfers between devices  46.2 us (49%)
  starting transfers between devices  23 us (24%)
  Pallas kernels  17.8 us (19%)
  local copies, waits for them, and re-layouts  4.63 us (5%)
  other arithmetic  2.56 us (3%)
    ppermute x11, waiting for transfers between devices, step_round(): return lax.ppermute(value, 'sec', pairs)  22.8 us
    ppermute x5, waiting for transfers between devices, to_party(): lax.ppermute(value, 'mpo', [(d, (d + j) % parties) for d in range(parties)])  22.1 us
    ppermute x11, starting transfers between devices, step_round(): return lax.ppermute(value, 'sec', pairs)  14.3 us
    pallas_call x3, Pallas kernels, right_products(): pl.pallas_call(functools.partial(right_kernel, lefts=len(lefts), spots=sp...  9.36 us
    ppermute x5, starting transfers between devices, to_party(): lax.ppermute(value, 'mpo', [(d, (d + j) % parties) for d in range(parties)])  6.71 us
    pallas_call x1, Pallas kernels, left_products(): pl.pallas_call(functools.partial(left_kernel, parties=parties, count=len(...  5.77 us
    pallas_call x1, Pallas kernels, on_device(): pl.pallas_call(functools.partial(join_kernel, stages=len(kept), bases=(st...  2.68 us
    unnamed x2, local copies, waits for them, and re-layouts  1.99 us
  transfers between devices with their start and end apart: 27, of which 14 were waited for; matrix products, arithmetic and copies ran while one was open for 6% of the time, Pallas kernels for 16%

profile of v6, /device:TPU:0, one launch (start us, length us, event | category | flops | bytes accessed | tf_op | source)
XLA Modules:
  0.0 94.5 jit_solution(2864643693900161599)
XLA Ops:
  0.0 1.1 %constant_dynamic-slice_fusion = (bf16[2,10,64,128]{3,2,1,0:T(8,128)(2,1)S(1)}, bf16[2,10,64,128]{3,2,1,0:T(8,128)(2,1)S(1)}) fusion(bf16[2,10,128,128]{3,2,1,0:T(8,128)(2,1)} %param.12, s32[]{:T(128)S(6)} %select_n.17, s32[]{:T(128)S(6)} %select_n.16), kind=kLoop, calls=%fused_computation.6 | loop fusion | bytes 1310728 | tf_op jit(solution)/shard_map/dynamic_slice | solution.py:333
  1.1 0.5 collective-permute-start.1
  1.7 2.6 %collective-permute-start.4 = (bf16[2,10,64,128]{3,2,1,0:T(8,128)(2,1)S(1)}, bf16[2,10,64,128]{3,2,1,0:T(8,128)(2,1)S(1)}, u32[]{:S(2)}, u32[]{:S(2)}) collective-permute-start(bf16[2,10,64,128]{3,2,1,0:T(8,128)(2,1)S(1)} %get-tuple-element.36.refs_2_), channel_id=1, source_target_pairs={{0,8},{2,6},{4,0},{6,14},{8,16},{10,2},{12,4},{14,22},{16,24},{18,... | collective-permute-start | bytes 983048 | tf_op jit(solution)/shard_map/ppermute | solution.py:45
  4.3 1.5 %collective-permute-start.2 = (bf16[2,10,64,128]{3,2,1,0:T(8,128)(2,1)S(1)}, bf16[2,10,64,128]{3,2,1,0:T(8,128)(2,1)S(1)}, u32[]{:S(2)}, u32[]{:S(2)}) collective-permute-start(bf16[2,10,64,128]{3,2,1,0:T(8,128)(2,1)S(1)} %get-tuple-element.35), channel_id=1, source_target_pairs={{0,1},{1,0},{2,3},{3,2},{4,5},{5,4},{6,7},{7,6},{8,9},{9,8},{10,11... | collective-permute-start | bytes 983048 | tf_op jit(solution)/shard_map/ppermute | solution.py:239
  5.8 1.6 %collective-permute-start.9 = (bf16[2,10,64,128]{3,2,1,0:T(8,128)(2,1)S(1)}, bf16[2,10,64,128]{3,2,1,0:T(8,128)(2,1)S(1)}, u32[]{:S(2)}, u32[]{:S(2)}) collective-permute-start(bf16[2,10,64,128]{3,2,1,0:T(8,128)(2,1)S(1)} %collective-permute-done.1.refs_3_), channel_id=1, source_target_pairs={{0,8},{2,6},{4,0},{6,14},{8,16},{10,2},{12,4},{14,22},{16,24},{18,... | collective-permute-start | bytes 983048 | tf_op jit(solution)/shard_map/ppermute | solution.py:45
  7.4 0.7 convert_element_type.3
  8.1 1.2 %broadcast_multiply_fusion.refs_0_ = bf16[2,10,128,128]{3,2,1,0:T(8,128)(2,1)S(1)} fusion(bf16[2,10,128,128]{3,2,1,0:T(8,128)(2,1)} %param.11, bf16[2,10]{1,0:T(2,128)(2,1)S(1)} %convert_element_type.3), kind=kLoop, calls=%fused_computation | loop fusion | flops 327680 | bytes 1310760 | tf_op jit(solution)/shard_map/mul | solution.py:320
  9.3 2.1 %collective-permute-start.6 = (bf16[2,10,64,128]{3,2,1,0:T(8,128)(2,1)S(1)}, bf16[2,10,64,128]{3,2,1,0:T(8,128)(2,1)}, u32[]{:S(2)}, u32[]{:S(2)}) collective-permute-start(bf16[2,10,64,128]{3,2,1,0:T(8,128)(2,1)S(1)} %collective-permute-done.4.refs_6_), channel_id=1, source_target_pairs={{0,8},{2,6},{4,0},{6,14},{8,16},{10,2},{12,4},{14,22},{16,24},{18,... | collective-permute-start | bytes 983048 | tf_op jit(solution)/shard_map/ppermute | solution.py:45
  11.4 2.6 %collective-permute-done.2.refs_4_ = bf16[2,10,64,128]{3,2,1,0:T(8,128)(2,1)S(1)} collective-permute-done((bf16[2,10,64,128]{3,2,1,0:T(8,128)(2,1)S(1)}, bf16[2,10,64,128]{3,2,1,0:T(8,128)(2,1)S(1)}, u32[]{:S(2)}, u32[]{:S(2)}) %collective-permute-start.2) | collective-permute-done | bytes 327712 | tf_op jit(solution)/shard_map/ppermute | solution.py:239
  14.0 0.9 collective-permute-start.11
  14.9 1.5 %collective-permute-start = (bf16[2,10,128,128]{3,2,1,0:T(8,128)(2,1)S(1)}, bf16[2,10,128,128]{3,2,1,0:T(8,128)(2,1)}, u32[]{:S(2)}, u32[]{:S(2)}) collective-permute-start(bf16[2,10,128,128]{3,2,1,0:T(8,128)(2,1)S(1)} %broadcast_multiply_fusion.refs_0_), channel_id=1, source_target_pairs={{0,1},{1,0},{2,3},{3,2},{4,5},{5,4},{6,7},{7,6},{8,9},{9,8},{10,11... | collective-permute-start | bytes 1966088 | tf_op jit(solution)/shard_map/ppermute | solution.py:239
  16.4 0.1 collective-permute-done.6
  16.5 2.0 %collective-permute-start.7 = (bf16[2,10,64,128]{3,2,1,0:T(8,128)(2,1)S(1)}, bf16[2,10,64,128]{3,2,1,0:T(8,128)(2,1)S(1)}, u32[]{:S(2)}, u32[]{:S(2)}) collective-permute-start(bf16[2,10,64,128]{3,2,1,0:T(8,128)(2,1)S(1)} %collective-permute-done.2.refs_4_), channel_id=1, source_target_pairs={{0,8},{2,6},{4,0},{6,14},{8,16},{10,2},{12,4},{14,22},{16,24},{18,... | collective-permute-start | bytes 983048 | tf_op jit(solution)/shard_map/ppermute | solution.py:45
  18.5 2.6 %collective-permute-done.11 = bf16[2,10,64,128]{3,2,1,0:T(8,128)(2,1)} collective-permute-done((bf16[2,10,64,128]{3,2,1,0:T(8,128)(2,1)S(1)}, bf16[2,10,64,128]{3,2,1,0:T(8,128)(2,1)}, u32[]{:S(2)}, u32[]{:S(2)}) %collective-permute-start.11) | collective-permute-done | bytes 327712 | tf_op jit(solution)/shard_map/ppermute | solution.py:45
  21.2 0.9 collective-permute-start.12
  22.1 0.7 fusion
  22.7 0.7 and_select_fusion
  23.4 0.7 concatenate.9.index_ref
  24.2 7.7 %collective-permute-done.refs_1_ = bf16[2,10,128,128]{3,2,1,0:T(8,128)(2,1)} collective-permute-done((bf16[2,10,128,128]{3,2,1,0:T(8,128)(2,1)S(1)}, bf16[2,10,128,128]{3,2,1,0:T(8,128)(2,1)}, u32[]{:S(2)}, u32[]{:S(2)}) %collective-permute-start) | collective-permute-done | bytes 655392 | tf_op jit(solution)/shard_map/ppermute | solution.py:239
  31.8 1.2 %collective-permute-start.14 = (bf16[2,10,64,128]{3,2,1,0:T(8,128)(2,1)S(1)}, bf16[2,10,64,128]{3,2,1,0:T(8,128)(2,1)S(1)}, u32[]{:S(2)}, u32[]{:S(2)}) collective-permute-start(bf16[2,10,64,128]{3,2,1,0:T(8,128)(2,1)S(1)} %collective-permute-done.7.refs_8_), channel_id=1, source_target_pairs={{0,8},{2,6},{4,0},{6,14},{8,16},{10,2},{12,4},{14,22},{16,24},{18,... | collective-permute-start | bytes 983048 | tf_op jit(solution)/shard_map/ppermute | solution.py:45
  33.0 0.1 collective-permute-start.5
  33.1 0.4 collective-permute-start.10
  33.5 0.4 collective-permute-start.16
  33.9 1.0 %constant_dynamic-update-slice_fusion.1 = bf16[4,10,64,128]{3,2,1,0:T(8,128)(2,1)S(1)} fusion(bf16[2,10,64,128]{3,2,1,0:T(8,128)(2,1)} %collective-permute-done.6), kind=kLoop, calls=%fused_computation.2 | loop fusion | bytes 655360
  34.9 1.0 %constant_dynamic-update-slice_fusion.3 = bf16[4,10,64,128]{3,2,1,0:T(8,128)(2,1)S(1)} fusion(bf16[2,10,64,128]{3,2,1,0:T(8,128)(2,1)} %collective-permute-done.11), kind=kLoop, calls=%fused_computation.4 | loop fusion | bytes 655360
  35.9 3.0 %collective-permute-done.14 = bf16[2,10,64,128]{3,2,1,0:T(8,128)(2,1)S(1)} collective-permute-done((bf16[2,10,64,128]{3,2,1,0:T(8,128)(2,1)S(1)}, bf16[2,10,64,128]{3,2,1,0:T(8,128)(2,1)S(1)}, u32[]{:S(2)}, u32[]{:S(2)}) %collective-permute-start.14) | collective-permute-done | bytes 327712 | tf_op jit(solution)/shard_map/ppermute | solution.py:45
  39.0 3.4 %collective-permute-done.16 = bf16[2,10,64,128]{3,2,1,0:T(8,128)(2,1)S(1)} collective-permute-done((bf16[2,10,64,128]{3,2,1,0:T(8,128)(2,1)S(1)}, bf16[2,10,64,128]{3,2,1,0:T(8,128)(2,1)S(1)}, u32[]{:S(2)}, u32[]{:S(2)}) %collective-permute-start.16) | collective-permute-done | bytes 327712 | tf_op jit(solution)/shard_map/ppermute | solution.py:45
  42.5 0.1 collective-permute-start.17
  42.6 5.8 %left_products.1 = (bf16[80,128,256]{2,1,0:T(8,128)(2,1)S(1)}, bf16[80,128,256]{2,1,0:T(8,128)(2,1)S(1)}) custom-call(s32[305]{0:T(512)S(1)} %concatenate.9.index_ref, bf16[2,10,128,128]{3,2,1,0:T(8,128)(2,1)S(1)} %broadcast_multiply_fusion.refs_0_, bf16[2,10,128,128]{3,2,1,0:T(8,128)(2,1)} %collective-permute-done.refs_1_, bf16[80,128,128]{2,1,0:T(8,128)(2,1)} %refs_2_.1), custom_call_target="tpu_custom_call" | custom-call | flops 1342177280 | bytes 9437184 | tf_op jit(solution)/shard_map/left_products/pallas_call | solution.py:269
  48.3 1.2 %collective-permute-start.18 = (bf16[4,10,64,128]{3,2,1,0:T(8,128)(2,1)S(1)}, bf16[4,10,64,128]{3,2,1,0:T(8,128)(2,1)S(1)}, u32[]{:S(2)}, u32[]{:S(2)}) collective-permute-start(bf16[4,10,64,128]{3,2,1,0:T(8,128)(2,1)S(1)} %constant_dynamic-update-slice_fusion.refs_14_), channel_id=1, source_target_pairs={{0,8},{2,6},{4,0},{6,14},{8,16},{10,2},{12,4},{14,22},{16,24},{18,... | collective-permute-start | bytes 1966088 | tf_op jit(solution)/shard_map/ppermute | solution.py:45
  49.5 0.7 collective-permute-start.8
  50.3 1.2 %collective-permute-done.8.refs_9_ = bf16[2,10,64,128]{3,2,1,0:T(8,128)(2,1)S(1)} collective-permute-done((bf16[2,10,64,128]{3,2,1,0:T(8,128)(2,1)S(1)}, bf16[2,10,64,128]{3,2,1,0:T(8,128)(2,1)S(1)}, u32[]{:S(2)}, u32[]{:S(2)}) %collective-permute-start.8) | collective-permute-done | bytes 327712 | tf_op jit(solution)/shard_map/ppermute | solution.py:37
  51.5 0.4 collective-permute-start.21
  51.9 0.1 collective-permute-done.13.refs_13_
  52.0 4.7 %right_products.3 = (bf16[40,64,128]{2,1,0:T(8,128)(2,1)S(1)}, bf16[40,64,128]{2,1,0:T(8,128)(2,1)S(1)}) custom-call(s32[305]{0:T(512)S(1)} %concatenate.9.index_ref, bf16[80,128,256]{2,1,0:T(8,128)(2,1)S(1)} %get-tuple-element.20.refs_0_, bf16[80,128,256]{2,1,0:T(8,128)(2,1)S(1)} %get-tuple-element.21.refs_1_, ...), custom_call_target="tpu_custom_call" | custom-call | flops 671088640 | bytes 12582912 | tf_op jit(solution)/shard_map/right_products/pallas_call | solution.py:293
  56.8 2.2 %collective-permute-done.18.refs_2_ = bf16[4,10,64,128]{3,2,1,0:T(8,128)(2,1)S(1)} collective-permute-done((bf16[4,10,64,128]{3,2,1,0:T(8,128)(2,1)S(1)}, bf16[4,10,64,128]{3,2,1,0:T(8,128)(2,1)S(1)}, u32[]{:S(2)}, u32[]{:S(2)}) %collective-permute-start.18) | collective-permute-done | bytes 655392 | tf_op jit(solution)/shard_map/ppermute | solution.py:45
  59.0 1.2 %collective-permute-start.23 = (bf16[4,10,64,128]{3,2,1,0:T(8,128)(2,1)S(1)}, bf16[4,10,64,128]{3,2,1,0:T(8,128)(2,1)S(1)}, u32[]{:S(2)}, u32[]{:S(2)}) collective-permute-start(bf16[4,10,64,128]{3,2,1,0:T(8,128)(2,1)S(1)} %collective-permute-done.18.refs_2_), channel_id=1, source_target_pairs={{0,8},{2,6},{4,0},{6,14},{8,16},{10,2},{12,4},{14,22},{16,24},{18,... | collective-permute-start | bytes 1966088 | tf_op jit(solution)/shard_map/ppermute | solution.py:45
  60.1 1.5 %collective-permute-start.19 = (bf16[40,64,128]{2,1,0:T(8,128)(2,1)S(1)}, bf16[40,64,128]{2,1,0:T(8,128)(2,1)S(1)}, u32[]{:S(2)}, u32[]{:S(2)}) collective-permute-start(bf16[40,64,128]{2,1,0:T(8,128)(2,1)S(1)} %get-tuple-element.28), channel_id=1, source_target_pairs={{0,1},{1,0},{2,3},{3,2},{4,5},{5,4},{6,7},{7,6},{8,9},{9,8},{10,11... | collective-permute-start | bytes 1966088 | tf_op jit(solution)/shard_map/ppermute | solution.py:239
  61.6 4.3 %collective-permute-done.21.refs_4_ = bf16[4,10,64,128]{3,2,1,0:T(8,128)(2,1)S(1)} collective-permute-done((bf16[4,10,64,128]{3,2,1,0:T(8,128)(2,1)S(1)}, bf16[4,10,64,128]{3,2,1,0:T(8,128)(2,1)S(1)}, u32[]{:S(2)}, u32[]{:S(2)}) %collective-permute-start.21) | collective-permute-done | bytes 655392 | tf_op jit(solution)/shard_map/ppermute | solution.py:45
  66.0 7.0 %collective-permute-done.23.refs_2_ = bf16[4,10,64,128]{3,2,1,0:T(8,128)(2,1)S(1)} collective-permute-done((bf16[4,10,64,128]{3,2,1,0:T(8,128)(2,1)S(1)}, bf16[4,10,64,128]{3,2,1,0:T(8,128)(2,1)S(1)}, u32[]{:S(2)}, u32[]{:S(2)}) %collective-permute-start.23) | collective-permute-done | bytes 655392 | tf_op jit(solution)/shard_map/ppermute | solution.py:45
  73.0 3.6 %collective-permute-done.19.refs_3_ = bf16[40,64,128]{2,1,0:T(8,128)(2,1)S(1)} collective-permute-done((bf16[40,64,128]{2,1,0:T(8,128)(2,1)S(1)}, bf16[40,64,128]{2,1,0:T(8,128)(2,1)S(1)}, u32[]{:S(2)}, u32[]{:S(2)}) %collective-permute-start.19) | collective-permute-done | bytes 655392 | tf_op jit(solution)/shard_map/ppermute | solution.py:239
  76.6 2.8 %right_products.4 = (bf16[20,64,128]{2,1,0:T(8,128)(2,1)S(1)}, bf16[20,64,128]{2,1,0:T(8,128)(2,1)S(1)}) custom-call(s32[305]{0:T(512)S(1)} %concatenate.9.index_ref, bf16[80,128,256]{2,1,0:T(8,128)(2,1)S(1)} %get-tuple-element.20.refs_0_, bf16[80,128,256]{2,1,0:T(8,128)(2,1)S(1)} %get-tuple-element.21.refs_1_, ...), custom_call_target="tpu_custom_call" | custom-call | flops 335544320 | bytes 12582912 | tf_op jit(solution)/shard_map/right_products/pallas_call | solution.py:293
  79.4 1.6 %collective-permute-start.25 = (bf16[20,64,128]{2,1,0:T(8,128)(2,1)S(1)}, bf16[20,64,128]{2,1,0:T(8,128)(2,1)S(1)}, u32[]{:S(2)}, u32[]{:S(2)}) collective-permute-start(bf16[20,64,128]{2,1,0:T(8,128)(2,1)S(1)} %get-tuple-element.33), channel_id=1, source_target_pairs={{0,1},{1,0},{2,3},{3,2},{4,5},{5,4},{6,7},{7,6},{8,9},{9,8},{10,11... | collective-permute-start | bytes 983048 | tf_op jit(solution)/shard_map/ppermute | solution.py:239
  81.0 1.9 %right_products.5 = (bf16[10,64,128]{2,1,0:T(8,128)(2,1)S(1)}, bf16[10,64,128]{2,1,0:T(8,128)(2,1)S(1)}) custom-call(s32[305]{0:T(512)S(1)} %concatenate.9.index_ref, bf16[80,128,256]{2,1,0:T(8,128)(2,1)S(1)} %get-tuple-element.20.refs_0_, bf16[80,128,256]{2,1,0:T(8,128)(2,1)S(1)} %get-tuple-element.21.refs_1_, ...), custom_call_target="tpu_custom_call" | custom-call | flops 167772160 | bytes 12582912 | tf_op jit(solution)/shard_map/right_products/pallas_call | solution.py:293
  82.9 0.6 collective-permute-start.26
  83.4 6.4 %collective-permute-done.25.refs_4_ = bf16[20,64,128]{2,1,0:T(8,128)(2,1)S(1)} collective-permute-done((bf16[20,64,128]{2,1,0:T(8,128)(2,1)S(1)}, bf16[20,64,128]{2,1,0:T(8,128)(2,1)S(1)}, u32[]{:S(2)}, u32[]{:S(2)}) %collective-permute-start.25) | collective-permute-done | bytes 327712 | tf_op jit(solution)/shard_map/ppermute | solution.py:239
  89.9 1.8 %collective-permute-done.26.refs_5_ = bf16[10,64,128]{2,1,0:T(8,128)(2,1)S(1)} collective-permute-done((bf16[10,64,128]{2,1,0:T(8,128)(2,1)S(1)}, bf16[10,64,128]{2,1,0:T(8,128)(2,1)S(1)}, u32[]{:S(2)}, u32[]{:S(2)}) %collective-permute-start.26) | collective-permute-done | bytes 163872 | tf_op jit(solution)/shard_map/ppermute | solution.py:239
  91.6 2.7 %join_columns.1 = bf16[80,64,128]{2,1,0:T(8,128)(2,1)} custom-call(s32[305]{0:T(512)S(1)} %concatenate.9.index_ref, bf16[40,64,128]{2,1,0:T(8,128)(2,1)S(1)} %get-tuple-element.26.refs_0_, bf16[20,64,128]{2,1,0:T(8,128)(2,1)S(1)} %get-tuple-element.30.refs_1_, bf16[10,64,128]{2,1,0:T(8,128)(2,1)S(1)} %get-tuple-element.32.refs_2_, ...), custom_call_target="tpu_custom_call" | custom-call | bytes 4194304 | tf_op jit(solution)/shard_map/join_columns/pallas_call | solution.py:394
  (21 shorter events, 0.3 us)
Async XLA Ops:
  1.1 4.7 %collective-permute-start.1 = (bf16[2,10,64,128]{3,2,1,0:T(8,128)(2,1)S(1)}, bf16[2,10,64,128]{3,2,1,0:T(8,128)(2,1)S(1)}, u32[]{:S(2)}, u32[]{:S(2)}) collective-permute-start(bf16[2,10,64,128]{3,2,1,0:T(8,128)(2,1)S(1)} %get-tuple-element.36.refs_2_), channel_id=1, source_target_pairs={{0,2},{2,0},{4,6},{6,4},{8,10},{10,8},{12,14},{14,12},{16,18},{18,... | collective-permute-start | bytes 983048 | tf_op jit(solution)/shard_map/ppermute | solution.py:37
  1.7 7.6 %collective-permute-start.4 = (bf16[2,10,64,128]{3,2,1,0:T(8,128)(2,1)S(1)}, bf16[2,10,64,128]{3,2,1,0:T(8,128)(2,1)S(1)}, u32[]{:S(2)}, u32[]{:S(2)}) collective-permute-start(bf16[2,10,64,128]{3,2,1,0:T(8,128)(2,1)S(1)} %get-tuple-element.36.refs_2_), channel_id=1, source_target_pairs={{0,8},{2,6},{4,0},{6,14},{8,16},{10,2},{12,4},{14,22},{16,24},{18,... | collective-permute-start | bytes 983048 | tf_op jit(solution)/shard_map/ppermute | solution.py:45
  4.3 9.7 %collective-permute-start.2 = (bf16[2,10,64,128]{3,2,1,0:T(8,128)(2,1)S(1)}, bf16[2,10,64,128]{3,2,1,0:T(8,128)(2,1)S(1)}, u32[]{:S(2)}, u32[]{:S(2)}) collective-permute-start(bf16[2,10,64,128]{3,2,1,0:T(8,128)(2,1)S(1)} %get-tuple-element.35), channel_id=1, source_target_pairs={{0,1},{1,0},{2,3},{3,2},{4,5},{5,4},{6,7},{7,6},{8,9},{9,8},{10,11... | collective-permute-start | bytes 983048 | tf_op jit(solution)/shard_map/ppermute | solution.py:239
  5.8 8.2 %collective-permute-start.9 = (bf16[2,10,64,128]{3,2,1,0:T(8,128)(2,1)S(1)}, bf16[2,10,64,128]{3,2,1,0:T(8,128)(2,1)S(1)}, u32[]{:S(2)}, u32[]{:S(2)}) collective-permute-start(bf16[2,10,64,128]{3,2,1,0:T(8,128)(2,1)S(1)} %collective-permute-done.1.refs_3_), channel_id=1, source_target_pairs={{0,8},{2,6},{4,0},{6,14},{8,16},{10,2},{12,4},{14,22},{16,24},{18,... | collective-permute-start | bytes 983048 | tf_op jit(solution)/shard_map/ppermute | solution.py:45
  9.3 7.2 %collective-permute-start.6 = (bf16[2,10,64,128]{3,2,1,0:T(8,128)(2,1)S(1)}, bf16[2,10,64,128]{3,2,1,0:T(8,128)(2,1)}, u32[]{:S(2)}, u32[]{:S(2)}) collective-permute-start(bf16[2,10,64,128]{3,2,1,0:T(8,128)(2,1)S(1)} %collective-permute-done.4.refs_6_), channel_id=1, source_target_pairs={{0,8},{2,6},{4,0},{6,14},{8,16},{10,2},{12,4},{14,22},{16,24},{18,... | collective-permute-start | bytes 983048 | tf_op jit(solution)/shard_map/ppermute | solution.py:45
  14.0 4.6 %collective-permute-start.3 = (bf16[2,10,64,128]{3,2,1,0:T(8,128)(2,1)S(1)}, bf16[2,10,64,128]{3,2,1,0:T(8,128)(2,1)S(1)}, u32[]{:S(2)}, u32[]{:S(2)}) collective-permute-start(bf16[2,10,64,128]{3,2,1,0:T(8,128)(2,1)S(1)} %collective-permute-done.2.refs_4_), channel_id=1, source_target_pairs={{0,2},{2,0},{4,6},{6,4},{8,10},{10,8},{12,14},{14,12},{16,18},{18,... | collective-permute-start | bytes 983048 | tf_op jit(solution)/shard_map/ppermute | solution.py:37
  14.0 7.2 %collective-permute-start.11 = (bf16[2,10,64,128]{3,2,1,0:T(8,128)(2,1)S(1)}, bf16[2,10,64,128]{3,2,1,0:T(8,128)(2,1)}, u32[]{:S(2)}, u32[]{:S(2)}) collective-permute-start(bf16[2,10,64,128]{3,2,1,0:T(8,128)(2,1)S(1)} %collective-permute-done.9.refs_10_), channel_id=1, source_target_pairs={{0,8},{2,6},{4,0},{6,14},{8,16},{10,2},{12,4},{14,22},{16,24},{18,... | collective-permute-start | bytes 983048 | tf_op jit(solution)/shard_map/ppermute | solution.py:45
  14.9 17.0 %collective-permute-start = (bf16[2,10,128,128]{3,2,1,0:T(8,128)(2,1)S(1)}, bf16[2,10,128,128]{3,2,1,0:T(8,128)(2,1)}, u32[]{:S(2)}, u32[]{:S(2)}) collective-permute-start(bf16[2,10,128,128]{3,2,1,0:T(8,128)(2,1)S(1)} %broadcast_multiply_fusion.refs_0_), channel_id=1, source_target_pairs={{0,1},{1,0},{2,3},{3,2},{4,5},{5,4},{6,7},{7,6},{8,9},{9,8},{10,11... | collective-permute-start | bytes 1966088 | tf_op jit(solution)/shard_map/ppermute | solution.py:239
  16.5 15.3 %collective-permute-start.7 = (bf16[2,10,64,128]{3,2,1,0:T(8,128)(2,1)S(1)}, bf16[2,10,64,128]{3,2,1,0:T(8,128)(2,1)S(1)}, u32[]{:S(2)}, u32[]{:S(2)}) collective-permute-start(bf16[2,10,64,128]{3,2,1,0:T(8,128)(2,1)S(1)} %collective-permute-done.2.refs_4_), channel_id=1, source_target_pairs={{0,8},{2,6},{4,0},{6,14},{8,16},{10,2},{12,4},{14,22},{16,24},{18,... | collective-permute-start | bytes 983048 | tf_op jit(solution)/shard_map/ppermute | solution.py:45
  21.2 12.3 %collective-permute-start.12 = (bf16[2,10,64,128]{3,2,1,0:T(8,128)(2,1)S(1)}, bf16[2,10,64,128]{3,2,1,0:T(8,128)(2,1)S(1)}, u32[]{:S(2)}, u32[]{:S(2)}) collective-permute-start(bf16[2,10,64,128]{3,2,1,0:T(8,128)(2,1)S(1)} %collective-permute-done.3.refs_5_), channel_id=1, source_target_pairs={{0,8},{2,6},{4,0},{6,14},{8,16},{10,2},{12,4},{14,22},{16,24},{18,... | collective-permute-start | bytes 983048 | tf_op jit(solution)/shard_map/ppermute | solution.py:45
  31.8 7.1 %collective-permute-start.14 = (bf16[2,10,64,128]{3,2,1,0:T(8,128)(2,1)S(1)}, bf16[2,10,64,128]{3,2,1,0:T(8,128)(2,1)S(1)}, u32[]{:S(2)}, u32[]{:S(2)}) collective-permute-start(bf16[2,10,64,128]{3,2,1,0:T(8,128)(2,1)S(1)} %collective-permute-done.7.refs_8_), channel_id=1, source_target_pairs={{0,8},{2,6},{4,0},{6,14},{8,16},{10,2},{12,4},{14,22},{16,24},{18,... | collective-permute-start | bytes 983048 | tf_op jit(solution)/shard_map/ppermute | solution.py:45
  33.0 16.5 %collective-permute-start.5 = (bf16[2,10,64,128]{3,2,1,0:T(8,128)(2,1)S(1)}, bf16[2,10,64,128]{3,2,1,0:T(8,128)(2,1)S(1)}, u32[]{:S(2)}, u32[]{:S(2)}) collective-permute-start(bf16[2,10,64,128]{3,2,1,0:T(8,128)(2,1)S(1)} %collective-permute-done.4.refs_6_), channel_id=1, source_target_pairs={{0,2},{2,0},{4,6},{6,4},{8,10},{10,8},{12,14},{14,12},{16,18},{18,... | collective-permute-start | bytes 983048 | tf_op jit(solution)/shard_map/ppermute | solution.py:37
  33.1 17.2 %collective-permute-start.10 = (bf16[2,10,64,128]{3,2,1,0:T(8,128)(2,1)S(1)}, bf16[2,10,64,128]{3,2,1,0:T(8,128)(2,1)S(1)}, u32[]{:S(2)}, u32[]{:S(2)}) collective-permute-start(bf16[2,10,64,128]{3,2,1,0:T(8,128)(2,1)S(1)} %collective-permute-done.9.refs_10_), channel_id=1, source_target_pairs={{0,2},{2,0},{4,6},{6,4},{8,10},{10,8},{12,14},{14,12},{16,18},{18,... | collective-permute-start | bytes 983048 | tf_op jit(solution)/shard_map/ppermute | solution.py:37
  33.5 8.9 %collective-permute-start.16 = (bf16[2,10,64,128]{3,2,1,0:T(8,128)(2,1)S(1)}, bf16[2,10,64,128]{3,2,1,0:T(8,128)(2,1)S(1)}, u32[]{:S(2)}, u32[]{:S(2)}) collective-permute-start(bf16[2,10,64,128]{3,2,1,0:T(8,128)(2,1)S(1)} %collective-permute-done.12.refs_12_), channel_id=1, source_target_pairs={{0,8},{2,6},{4,0},{6,14},{8,16},{10,2},{12,4},{14,22},{16,24},{18,... | collective-permute-start | bytes 983048 | tf_op jit(solution)/shard_map/ppermute | solution.py:45
  39.0 13.0 %collective-permute-start.15 = (bf16[4,10,64,128]{3,2,1,0:T(8,128)(2,1)S(1)}, bf16[4,10,64,128]{3,2,1,0:T(8,128)(2,1)S(1)}, u32[]{:S(2)}, u32[]{:S(2)}) collective-permute-start(bf16[4,10,64,128]{3,2,1,0:T(8,128)(2,1)S(1)} %constant_dynamic-update-slice_fusion.refs_14_), channel_id=1, source_target_pairs={{0,2},{2,0},{4,6},{6,4},{8,10},{10,8},{12,14},{14,12},{16,18},{18,... | collective-permute-start | bytes 1966088 | tf_op jit(solution)/shard_map/ppermute | solution.py:37
  42.5 9.5 %collective-permute-start.17 = (bf16[4,10,64,128]{3,2,1,0:T(8,128)(2,1)S(1)}, bf16[4,10,64,128]{3,2,1,0:T(8,128)(2,1)S(1)}, u32[]{:S(2)}, u32[]{:S(2)}) collective-permute-start(bf16[4,10,64,128]{3,2,1,0:T(8,128)(2,1)S(1)} %constant_dynamic-update-slice_fusion.2.refs_16_), channel_id=1, source_target_pairs={{0,2},{2,0},{4,6},{6,4},{8,10},{10,8},{12,14},{14,12},{16,18},{18,... | collective-permute-start | bytes 1966088 | tf_op jit(solution)/shard_map/ppermute | solution.py:37
  48.3 10.6 %collective-permute-start.18 = (bf16[4,10,64,128]{3,2,1,0:T(8,128)(2,1)S(1)}, bf16[4,10,64,128]{3,2,1,0:T(8,128)(2,1)S(1)}, u32[]{:S(2)}, u32[]{:S(2)}) collective-permute-start(bf16[4,10,64,128]{3,2,1,0:T(8,128)(2,1)S(1)} %constant_dynamic-update-slice_fusion.refs_14_), channel_id=1, source_target_pairs={{0,8},{2,6},{4,0},{6,14},{8,16},{10,2},{12,4},{14,22},{16,24},{18,... | collective-permute-start | bytes 1966088 | tf_op jit(solution)/shard_map/ppermute | solution.py:45
  49.5 2.0 %collective-permute-start.8 = (bf16[2,10,64,128]{3,2,1,0:T(8,128)(2,1)S(1)}, bf16[2,10,64,128]{3,2,1,0:T(8,128)(2,1)S(1)}, u32[]{:S(2)}, u32[]{:S(2)}) collective-permute-start(bf16[2,10,64,128]{3,2,1,0:T(8,128)(2,1)S(1)} %collective-permute-done.7.refs_8_), channel_id=1, source_target_pairs={{0,2},{2,0},{4,6},{6,4},{8,10},{10,8},{12,14},{14,12},{16,18},{18,... | collective-permute-start | bytes 983048 | tf_op jit(solution)/shard_map/ppermute | solution.py:37
  50.3 1.7 %collective-permute-start.13 = (bf16[2,10,64,128]{3,2,1,0:T(8,128)(2,1)S(1)}, bf16[2,10,64,128]{3,2,1,0:T(8,128)(2,1)S(1)}, u32[]{:S(2)}, u32[]{:S(2)}) collective-permute-start(bf16[2,10,64,128]{3,2,1,0:T(8,128)(2,1)S(1)} %collective-permute-done.12.refs_12_), channel_id=1, source_target_pairs={{0,2},{2,0},{4,6},{6,4},{8,10},{10,8},{12,14},{14,12},{16,18},{18,... | collective-permute-start | bytes 983048 | tf_op jit(solution)/shard_map/ppermute | solution.py:37
  51.5 14.5 %collective-permute-start.21 = (bf16[4,10,64,128]{3,2,1,0:T(8,128)(2,1)S(1)}, bf16[4,10,64,128]{3,2,1,0:T(8,128)(2,1)S(1)}, u32[]{:S(2)}, u32[]{:S(2)}) collective-permute-start(bf16[4,10,64,128]{3,2,1,0:T(8,128)(2,1)S(1)} %constant_dynamic-update-slice_fusion.2.refs_16_), channel_id=1, source_target_pairs={{0,8},{2,6},{4,0},{6,14},{8,16},{10,2},{12,4},{14,22},{16,24},{18,... | collective-permute-start | bytes 1966088 | tf_op jit(solution)/shard_map/ppermute | solution.py:45
  59.0 14.0 %collective-permute-start.23 = (bf16[4,10,64,128]{3,2,1,0:T(8,128)(2,1)S(1)}, bf16[4,10,64,128]{3,2,1,0:T(8,128)(2,1)S(1)}, u32[]{:S(2)}, u32[]{:S(2)}) collective-permute-start(bf16[4,10,64,128]{3,2,1,0:T(8,128)(2,1)S(1)} %collective-permute-done.18.refs_2_), channel_id=1, source_target_pairs={{0,8},{2,6},{4,0},{6,14},{8,16},{10,2},{12,4},{14,22},{16,24},{18,... | collective-permute-start | bytes 1966088 | tf_op jit(solution)/shard_map/ppermute | solution.py:45
  60.1 16.5 %collective-permute-start.19 = (bf16[40,64,128]{2,1,0:T(8,128)(2,1)S(1)}, bf16[40,64,128]{2,1,0:T(8,128)(2,1)S(1)}, u32[]{:S(2)}, u32[]{:S(2)}) collective-permute-start(bf16[40,64,128]{2,1,0:T(8,128)(2,1)S(1)} %get-tuple-element.28), channel_id=1, source_target_pairs={{0,1},{1,0},{2,3},{3,2},{4,5},{5,4},{6,7},{7,6},{8,9},{9,8},{10,11... | collective-permute-start | bytes 1966088 | tf_op jit(solution)/shard_map/ppermute | solution.py:239
  61.6 15.0 %collective-permute-start.20 = (bf16[4,10,64,128]{3,2,1,0:T(8,128)(2,1)S(1)}, bf16[4,10,64,128]{3,2,1,0:T(8,128)(2,1)S(1)}, u32[]{:S(2)}, u32[]{:S(2)}) collective-permute-start(bf16[4,10,64,128]{3,2,1,0:T(8,128)(2,1)S(1)} %collective-permute-done.18.refs_2_), channel_id=1, source_target_pairs={{0,2},{2,0},{4,6},{6,4},{8,10},{10,8},{12,14},{14,12},{16,18},{18,... | collective-permute-start | bytes 1966088 | tf_op jit(solution)/shard_map/ppermute | solution.py:37
  66.0 10.7 %collective-permute-start.22 = (bf16[4,10,64,128]{3,2,1,0:T(8,128)(2,1)S(1)}, bf16[4,10,64,128]{3,2,1,0:T(8,128)(2,1)S(1)}, u32[]{:S(2)}, u32[]{:S(2)}) collective-permute-start(bf16[4,10,64,128]{3,2,1,0:T(8,128)(2,1)S(1)} %collective-permute-done.21.refs_4_), channel_id=1, source_target_pairs={{0,2},{2,0},{4,6},{6,4},{8,10},{10,8},{12,14},{14,12},{16,18},{18,... | collective-permute-start | bytes 1966088 | tf_op jit(solution)/shard_map/ppermute | solution.py:37
  73.0 8.0 %collective-permute-start.24 = (bf16[4,10,64,128]{3,2,1,0:T(8,128)(2,1)S(1)}, bf16[4,10,64,128]{3,2,1,0:T(8,128)(2,1)S(1)}, u32[]{:S(2)}, u32[]{:S(2)}) collective-permute-start(bf16[4,10,64,128]{3,2,1,0:T(8,128)(2,1)S(1)} %collective-permute-done.23.refs_2_), channel_id=1, source_target_pairs={{0,2},{2,0},{4,6},{6,4},{8,10},{10,8},{12,14},{14,12},{16,18},{18,... | collective-permute-start | bytes 1966088 | tf_op jit(solution)/shard_map/ppermute | solution.py:37
  79.4 10.4 %collective-permute-start.25 = (bf16[20,64,128]{2,1,0:T(8,128)(2,1)S(1)}, bf16[20,64,128]{2,1,0:T(8,128)(2,1)S(1)}, u32[]{:S(2)}, u32[]{:S(2)}) collective-permute-start(bf16[20,64,128]{2,1,0:T(8,128)(2,1)S(1)} %get-tuple-element.33), channel_id=1, source_target_pairs={{0,1},{1,0},{2,3},{3,2},{4,5},{5,4},{6,7},{7,6},{8,9},{9,8},{10,11... | collective-permute-start | bytes 983048 | tf_op jit(solution)/shard_map/ppermute | solution.py:239
  82.9 8.7 %collective-permute-start.26 = (bf16[10,64,128]{2,1,0:T(8,128)(2,1)S(1)}, bf16[10,64,128]{2,1,0:T(8,128)(2,1)S(1)}, u32[]{:S(2)}, u32[]{:S(2)}) collective-permute-start(bf16[10,64,128]{2,1,0:T(8,128)(2,1)S(1)} %get-tuple-element.34), channel_id=1, source_target_pairs={{0,1},{1,0},{2,3},{3,2},{4,5},{5,4},{6,7},{7,6},{8,9},{9,8},{10,11... | collective-permute-start | bytes 491528 | tf_op jit(solution)/shard_map/ppermute | solution.py:239
